TPU v7x, 32 devices: a whole 2x2x4 slice. The times are simulated.
32 devices in a mesh: dp: 8 (over y, x, core), tp: 4 (over z).
Axes of the slice: x: 2, y: 2, z: 4, core: 2. Of those that a mesh axis runs over, the one named last changes fastest.
Arguments:
- tokens: bfloat16 [8, 1536, 1536], P('dp'), may hold values from -6 to 6
- attn_in: bfloat16 [4, 1536, 1536], P(None, 'dp', 'tp'), may hold values from -0.15625 to 0.15625
- head_gates: bfloat16 [3, 1536, 24], P(None, 'dp', 'tp'), may hold values from -0.15625 to 0.15625
- out_proj: bfloat16 [1536, 1536], P('tp', 'dp'), may hold values from -0.875 to 0.875
- norm_gains: bfloat16 [2, 1536], P(None, 'dp'), may hold values from 0.5 to 1.5
- qk_gains: bfloat16 [2, 64], replicated, may hold values from 0.5 to 1.5
- forget_bias: bfloat16 [24], replicated, may hold values from -1 to 8
- gate_up: bfloat16 [2, 1536, 4096], P(None, 'dp', 'tp'), may hold values from -0.15625 to 0.15625
- down_proj: bfloat16 [4096, 1536], P('tp', 'dp'), may hold values from -0.09375 to 0.09375
- carried_offset: float32 [8, 24], P('dp'), may hold values from -2 to 2
- reset_flag: int32 [8], P('dp'), may hold values from 0 to 1
- cotangent: bfloat16 [8, 1536, 1536], P('dp'), may hold values from -6 to 6
Outputs:
- layer_out: bfloat16 [8, 1536, 1536], P('dp', 'tp')
- grad_tokens: float32 [8, 1536, 1536], P('dp', 'tp')
- grad_attn_in: float32 [4, 1536, 1536], P(None, 'dp', 'tp')
- grad_head_gates: float32 [3, 1536, 24], P(None, 'dp', 'tp')
- grad_out_proj: float32 [1536, 1536], P('tp', 'dp')
- grad_gate_up: float32 [2, 1536, 4096], P(None, 'dp', 'tp')
- grad_down_proj: float32 [4096, 1536], P('tp', 'dp')
- grad_norm_gains: float32 [2, 1536], replicated
- grad_qk_gains: float32 [2, 64], replicated
- grad_forget_bias: float32 [24], replicated
All inputs are finite; a program needn't handle non-finite values.
Results may differ from a plain program's by a relative error of at most 0.014.
Values may be sent and summed in bfloat16 or wider, within the bound.
No kernel may reach another device: no remote copies, remote signals or barrier semaphores. Data moves between devices by JAX's collectives and lax.ppermute only.
A program may use at most 320 MiB of HBM per device.

v0:
```python
import jax
import jax.numpy as jnp
from jax import lax
from jax.sharding import PartitionSpec as P

QBLOCK = 512


EPSILON = 1e-06


def rms_apply(values, gain_row):
    return values * lax.rsqrt(jnp.mean(values * values, -1, keepdims=True) + EPSILON) * gain_row


def norm_back(values, gain_row, grad_out):
    factor = lax.rsqrt(jnp.mean(values * values, -1, keepdims=True) + EPSILON)
    normed = values * factor
    grad_normed = grad_out * gain_row
    grad_values = factor * (
        grad_normed - normed * jnp.mean(grad_normed * normed, -1, keepdims=True)
    )
    return (grad_values, grad_out * normed)


def token_shift(values, mixing):
    earlier = jnp.concatenate([jnp.zeros_like(values[:, :1]), values[:, :-1]], axis=1)
    return mixing[..., None] * earlier + (1.0 - mixing[..., None]) * values


def head_pieces(query_in, key_in, value_in, logits_in, gains_in, bias_in, offset_term):
    key_mix = jax.nn.sigmoid(logits_in[0])
    value_mix = jax.nn.sigmoid(logits_in[1])
    query_normed = rms_apply(query_in, gains_in[0])
    key_normed = rms_apply(token_shift(key_in, key_mix), gains_in[1])
    value_shifted = token_shift(value_in, value_mix)
    forget_logit = logits_in[2] + bias_in + offset_term
    cumulative = jnp.cumsum(jax.nn.log_sigmoid(forget_logit), axis=1)
    return (query_normed, key_normed, value_shifted, cumulative)


def block_scores(q_block, key_low, c_block, cum_heads, block_start, block_rows):
    head_scale = q_block.shape[3] ** (-0.5)
    scores = (
        jnp.einsum("bqhd,bkhd->bhqk", q_block, key_low, preferred_element_type=jnp.float32)
        * head_scale
    )
    scores = scores + c_block[..., None] - cum_heads[:, :, None, :]
    key_pos = jnp.arange(key_low.shape[1], dtype=jnp.int32)
    allowed = (block_start + jnp.arange(block_rows, dtype=jnp.int32))[:, None] >= key_pos[None, :]
    return jnp.where(allowed, scores, -1e30)


def attend_forward(query_low, key_low, value_low, cum_heads, block_rows):
    item_count, seq_len, heads_local, head_size = query_low.shape

    def one_block(block_start):
        q_block = lax.dynamic_slice_in_dim(query_low, block_start, block_rows, 1)
        c_block = lax.dynamic_slice_in_dim(cum_heads, block_start, block_rows, 2)
        scores = block_scores(q_block, key_low, c_block, cum_heads, block_start, block_rows)
        row_max = jnp.max(scores, -1, keepdims=True)
        weights = jnp.exp(scores - row_max)
        row_total = jnp.sum(weights, -1, keepdims=True)
        prob_low = (weights / row_total).astype(jnp.bfloat16)
        output = jnp.einsum(
            "bhqk,bkhd->bqhd", prob_low, value_low, preferred_element_type=jnp.float32
        )
        return (output, (row_max + jnp.log(row_total))[..., 0])

    starts = jnp.arange(seq_len // block_rows, dtype=jnp.int32) * block_rows
    outputs, log_totals = lax.map(one_block, starts)
    attended = jnp.moveaxis(outputs, 0, 1).reshape(item_count, seq_len, heads_local, head_size)
    return (attended, log_totals)


def attend_backward(query_low, key_low, value_low, cum_heads, log_totals, grad_att_low, block_rows):
    item_count, seq_len, heads_local, head_size = query_low.shape
    head_scale = head_size ** (-0.5)

    def one_block(carried, inputs):
        key_grad, value_grad, col_sums = carried
        block_start, block_lse = inputs
        q_block = lax.dynamic_slice_in_dim(query_low, block_start, block_rows, 1)
        g_block = lax.dynamic_slice_in_dim(grad_att_low, block_start, block_rows, 1)
        c_block = lax.dynamic_slice_in_dim(cum_heads, block_start, block_rows, 2)
        scores = block_scores(q_block, key_low, c_block, cum_heads, block_start, block_rows)
        prob_full = jnp.exp(scores - block_lse[..., None])
        prob_low = prob_full.astype(jnp.bfloat16)
        value_grad = value_grad + jnp.einsum(
            "bhqk,bqhd->bkhd", prob_low, g_block, preferred_element_type=jnp.float32
        )
        prob_grad = jnp.einsum(
            "bqhd,bkhd->bhqk", g_block, value_low, preferred_element_type=jnp.float32
        )
        score_grad = prob_full * (prob_grad - jnp.sum(prob_full * prob_grad, -1, keepdims=True))
        grad_low = score_grad.astype(jnp.bfloat16)
        query_grad = (
            jnp.einsum("bhqk,bkhd->bqhd", grad_low, key_low, preferred_element_type=jnp.float32)
            * head_scale
        )
        key_grad = (
            key_grad
            + jnp.einsum("bhqk,bqhd->bkhd", grad_low, q_block, preferred_element_type=jnp.float32)
            * head_scale
        )
        col_sums = col_sums + jnp.sum(score_grad, 2)
        return ((key_grad, value_grad, col_sums), (query_grad, jnp.sum(score_grad, -1)))

    starts = jnp.arange(seq_len // block_rows, dtype=jnp.int32) * block_rows
    zero_keys = jnp.zeros(query_low.shape, jnp.float32)
    zero_cols = jnp.zeros(cum_heads.shape, jnp.float32)
    carried, stacked = lax.scan(one_block, (zero_keys, zero_keys, zero_cols), (starts, log_totals))
    key_grad, value_grad, col_sums = carried
    query_blocks, row_blocks = stacked
    query_grad = jnp.moveaxis(query_blocks, 0, 1).reshape(query_low.shape)
    row_sums = jnp.moveaxis(row_blocks, 0, 2).reshape(cum_heads.shape)
    return (query_grad, key_grad, value_grad, row_sums - col_sums)


def shards(
    tokens,
    attn_in,
    head_gates,
    out_proj,
    norm_gains,
    qk_gains,
    forget_bias,
    gate_up,
    down_proj,
    carried_offset,
    reset_flag,
    cotangent,
):
    tp_count = lax.axis_size("tp")
    tp_rank = lax.axis_index("tp")
    item_count, seq_len, model_width = tokens.shape
    rows_own = seq_len // tp_count
    row_first = tp_rank * rows_own
    block_rows = min(QBLOCK, seq_len)

    def own_rows(values):
        return lax.dynamic_slice_in_dim(values, row_first, rows_own, 1)

    attn_full, gates_full, out_full, gains_full = (
        lax.all_gather(attn_in, "dp", axis=1, tiled=True),
        lax.all_gather(head_gates, "dp", axis=1, tiled=True),
        lax.all_gather(out_proj, "dp", axis=1, tiled=True),
        lax.all_gather(norm_gains, "dp", axis=1, tiled=True),
    )
    gate_up_full, down_full = (
        lax.all_gather(gate_up, "dp", axis=1, tiled=True),
        lax.all_gather(down_proj, "dp", axis=1, tiled=True),
    )
    head_size = qk_gains.shape[1]
    heads_local = gates_full.shape[2]
    local_width = heads_local * head_size
    head_shape = (item_count, seq_len, heads_local, head_size)
    inputs = tokens.astype(jnp.float32)
    gain_first = gains_full[0].astype(jnp.float32)
    gain_mid = gains_full[1].astype(jnp.float32)
    normed_low = rms_apply(inputs, gain_first).astype(jnp.bfloat16)
    projected = jnp.einsum(
        "bsd,mde->mbse", normed_low, attn_full, preferred_element_type=jnp.float32
    )
    gate_logits = jnp.einsum(
        "bsd,mdh->mbsh", normed_low, gates_full, preferred_element_type=jnp.float32
    )
    bias_local = lax.dynamic_slice_in_dim(
        forget_bias.astype(jnp.float32), tp_rank * heads_local, heads_local, 0
    )
    offset_local = lax.dynamic_slice_in_dim(carried_offset, tp_rank * heads_local, heads_local, 1)
    offset_term = (1 - reset_flag).astype(jnp.float32)[:, None, None] * offset_local[:, None, :]
    gains_qk = qk_gains.astype(jnp.float32)

    def local_heads(query_in, key_in, value_in, logits_in, gains_in, bias_in):
        return head_pieces(query_in, key_in, value_in, logits_in, gains_in, bias_in, offset_term)

    pieces, pieces_back = jax.vjp(
        local_heads,
        projected[0].reshape(head_shape),
        projected[1].reshape(head_shape),
        projected[2].reshape(head_shape),
        gate_logits,
        gains_qk,
        bias_local,
    )
    query_normed, key_normed, value_shifted, cumulative = pieces
    query_low = query_normed.astype(jnp.bfloat16)
    key_low = key_normed.astype(jnp.bfloat16)
    value_low = value_shifted.astype(jnp.bfloat16)
    cum_heads = jnp.transpose(cumulative, (0, 2, 1))
    attended, log_totals = attend_forward(query_low, key_low, value_low, cum_heads, block_rows)
    attended_flat = attended.reshape(item_count, seq_len, local_width)
    out_gate = jax.nn.sigmoid(projected[3])
    gated_low = (attended_flat * out_gate).astype(jnp.bfloat16)
    attn_part = jnp.einsum("bse,ed->bsd", gated_low, out_full, preferred_element_type=jnp.float32)
    mixed_full = inputs + lax.psum(attn_part, "tp")
    mid_low = rms_apply(mixed_full, gain_mid).astype(jnp.bfloat16)
    mixed_rows = own_rows(mixed_full)
    gate_pre = jnp.einsum(
        "bsd,mdf->mbsf", mid_low, gate_up_full, preferred_element_type=jnp.float32
    )

    def swiglu(gate_part, up_part):
        return jax.nn.silu(gate_part) * up_part

    hidden, hidden_back = jax.vjp(swiglu, gate_pre[0], gate_pre[1])
    hidden_low = hidden.astype(jnp.bfloat16)
    ffn_part = jnp.einsum("bsf,fd->bsd", hidden_low, down_full, preferred_element_type=jnp.float32)
    result = (
        mixed_rows
        + lax.psum_scatter(
            ffn_part.astype(jnp.bfloat16), "tp", scatter_dimension=1, tiled=True
        ).astype(jnp.float32)
    ).astype(jnp.bfloat16)
    gate_up_full, down_full = (
        lax.all_gather(gate_up, "dp", axis=1, tiled=True),
        lax.all_gather(down_proj, "dp", axis=1, tiled=True),
    )
    grad_out = cotangent.astype(jnp.float32)
    grad_down = jnp.einsum("bsf,bsd->fd", hidden_low, cotangent, preferred_element_type=jnp.float32)
    grad_hidden = jnp.einsum(
        "bsd,fd->bsf", cotangent, down_full, preferred_element_type=jnp.float32
    )
    grad_gate, grad_up = hidden_back(grad_hidden)
    pre_grad_low = jnp.stack([grad_gate, grad_up]).astype(jnp.bfloat16)
    grad_gate_up = jnp.einsum(
        "bsd,mbsf->mdf", mid_low, pre_grad_low, preferred_element_type=jnp.float32
    )
    mid_part = jnp.einsum(
        "mbsf,mdf->bsd", pre_grad_low, gate_up_full, preferred_element_type=jnp.float32
    )
    mid_grad = lax.psum(mid_part, "tp")
    back_mixed, gain_terms = norm_back(mixed_full, gain_mid, mid_grad)
    mixed_grad = grad_out + back_mixed
    resid_low = mixed_grad.astype(jnp.bfloat16)
    mixed_grad_rows = own_rows(mixed_grad)
    gain_mid_grad = jnp.sum(own_rows(gain_terms), (0, 1))
    attn_full, gates_full, out_full, gains_full = (
        lax.all_gather(attn_in, "dp", axis=1, tiled=True),
        lax.all_gather(head_gates, "dp", axis=1, tiled=True),
        lax.all_gather(out_proj, "dp", axis=1, tiled=True),
        lax.all_gather(norm_gains, "dp", axis=1, tiled=True),
    )
    gain_first = gains_full[0].astype(jnp.float32)
    grad_out_proj = jnp.einsum(
        "bse,bsd->ed", gated_low, resid_low, preferred_element_type=jnp.float32
    )
    grad_gated = jnp.einsum("bsd,ed->bse", resid_low, out_full, preferred_element_type=jnp.float32)
    grad_att_low = (grad_gated * out_gate).astype(jnp.bfloat16).reshape(head_shape)
    gate_pre_grad = grad_gated * attended_flat * out_gate * (1.0 - out_gate)
    query_grad, key_grad, value_grad, cum_grad_heads = attend_backward(
        query_low, key_low, value_low, cum_heads, log_totals, grad_att_low, block_rows
    )
    grad_query, grad_key, grad_value, grad_logits, grad_qk, grad_bias = pieces_back(
        (query_grad, key_grad, value_grad, jnp.transpose(cum_grad_heads, (0, 2, 1)))
    )
    flat_shape = (item_count, seq_len, local_width)
    proj_grad_low = jnp.stack(
        [
            grad_query.reshape(flat_shape),
            grad_key.reshape(flat_shape),
            grad_value.reshape(flat_shape),
            gate_pre_grad,
        ]
    ).astype(jnp.bfloat16)
    logit_grad_low = grad_logits.astype(jnp.bfloat16)
    grad_attn_in = jnp.einsum(
        "bsd,mbse->mde", normed_low, proj_grad_low, preferred_element_type=jnp.float32
    )
    grad_head_gates = jnp.einsum(
        "bsd,mbsh->mdh", normed_low, logit_grad_low, preferred_element_type=jnp.float32
    )
    input_part = jnp.einsum(
        "mbse,mde->bsd", proj_grad_low, attn_full, preferred_element_type=jnp.float32
    )
    input_part = input_part + jnp.einsum(
        "mbsh,mdh->bsd", logit_grad_low, gates_full, preferred_element_type=jnp.float32
    )
    input_grad_rows = lax.psum_scatter(input_part, "tp", scatter_dimension=1, tiled=True)
    back_input, first_terms = norm_back(own_rows(inputs), gain_first, input_grad_rows)
    grad_tokens = mixed_grad_rows + back_input
    gain_first_grad = jnp.sum(first_terms, (0, 1))
    shared_attn, shared_gates, shared_out, shared_gate_up, shared_down = (
        lax.psum_scatter(grad_attn_in, "dp", scatter_dimension=1, tiled=True),
        lax.psum_scatter(grad_head_gates, "dp", scatter_dimension=1, tiled=True),
        lax.psum_scatter(grad_out_proj, "dp", scatter_dimension=1, tiled=True),
        lax.psum_scatter(grad_gate_up, "dp", scatter_dimension=1, tiled=True),
        lax.psum_scatter(grad_down, "dp", scatter_dimension=1, tiled=True),
    )
    bias_full = lax.dynamic_update_slice_in_dim(
        jnp.zeros(forget_bias.shape, jnp.float32), grad_bias, tp_rank * heads_local, 0
    )
    norm_grad, qk_grad, bias_grad = lax.psum(
        (jnp.stack([gain_first_grad, gain_mid_grad]), grad_qk, bias_full), ("dp", "tp")
    )
    return (
        result,
        grad_tokens,
        shared_attn,
        shared_gates,
        shared_out,
        shared_gate_up,
        shared_down,
        norm_grad,
        qk_grad,
        bias_grad,
    )


def solution(mesh):
    return jax.shard_map(
        shards,
        mesh=mesh,
        in_specs=(
            P("dp", None, None),
            P(None, "dp", "tp"),
            P(None, "dp", "tp"),
            P("tp", "dp"),
            P(None, "dp"),
            P(),
            P(),
            P(None, "dp", "tp"),
            P("tp", "dp"),
            P("dp", None),
            P("dp"),
            P("dp", None, None),
        ),
        out_specs=(
            P("dp", "tp", None),
            P("dp", "tp", None),
            P(None, "dp", "tp"),
            P(None, "dp", "tp"),
            P("tp", "dp"),
            P(None, "dp", "tp"),
            P("tp", "dp"),
            P(),
            P(),
            P(),
        ),
        check_vma=False,
    )
```

profile of v0, /device:TPU:0, one launch (start us, length us, event | category | flops | bytes accessed | tf_op | source)
XLA Modules:
  0.0 1892.5 jit_solution(4130549712203092903)
XLA Ops:
  24.4 14.7 all_gather.26
  77.2 141.6 %while.31 = (s32[]{:T(128)}, f32[3,1,512,6,64]{2,0,4,3,1:T(4,128)}, f32[3,1,6,512]{3,2,1,0:T(8,128)S(1)}, s32[3]{0:T(128)S(1)}, bf16[1,1536,6,64]{1,3,2,0:T(8,12...) while((s32[]{:T(128)}, f32[3,1,512,6,64]{2,0,4,3,1:T(4,128)}, ...), condition=%wide.region_8.9_spmd, body=%wide.region_5.8_spmd.sunk | while | flops 1293678080 | bytes 66740408 | solution.py:71
  104.6 16.0 dynamic_update_slice.28
  147.8 16.0 dynamic_update_slice.28
  191.0 16.0 dynamic_update_slice.28
  232.3 323.7 %all-reduce.17.cloned.1.call-done = f32[1,1536,1536]{2,1,0:T(8,128)} async-done(((f32[1,1536,1536]{2,1,0:T(8,128)}), f32[1,1536,1536]{2,1,0:T(8,128)}) %all-reduce.17.cloned.1.call-update) | async-done | bytes 9437200 | tf_op jit(solution)/shard_map/psum | solution.py:197
  574.1 28.2 %all-gather.10.cloned.1.call-done = bf16[2,1536,1024]{2,1,0:T(8,128)(2,1)} async-done(((bf16[2,192,1024]{2,1,0:T(8,128)(2,1)}), bf16[2,1536,1024]{2,1,0:T(8,128)(2,1)}) %all-gather.10.cloned.1.call-update) | async-done | bytes 6291472 | tf_op jit(solution)/shard_map/all_gather | solution.py:151
  602.3 16.9 convolution_bitcast_fusion.3
  619.2 17.2 all-gather.12.cloned.1.call-done
  667.0 18.8 convolution_bitcast_fusion.2
  685.9 19.5 %copy.69 = f32[2,1536,1024]{2,0,1:T(2,128)} copy(f32[2,1536,1024]{1,2,0:T(8,128)} %convolution_bitcast_fusion.2) | data formatting | bytes 25165824 | tf_op jit(solution)/shard_map/bsd,mbsf->mdf/transpose | solution.py:227
  715.9 273.1 %all-reduce.19.cloned.1.call-done = f32[1,1536,1536]{2,1,0:T(8,128)} async-done(((f32[1,1536,1536]{2,1,0:T(8,128)}), f32[1,1536,1536]{2,1,0:T(8,128)}) %all-reduce.19.cloned.1.call-update) | async-done | bytes 9437200 | tf_op jit(solution)/shard_map/psum | solution.py:233
  1016.3 234.7 %while.32 = (s32[]{:T(128)}, f32[1,1536,6,64]{1,3,2,0:T(8,128)}, f32[1,1536,6,64]{1,3,2,0:T(8,128)S(1)}, f32[1,6,1536]{2,1,0:T(8,128)S(1)}, f32[3,1,512,6,64]{2,...) while((s32[]{:T(128)}, f32[1,1536,6,64]{1,3,2,0:T(8,128)}, ...), condition=%wide.region_19.20_spmd.clone, body=%wide.region_15.19_spmd.clone.sunk | while | flops 3085176320 | bytes 180818224 | solution.py:112
  1031.6 15.6 multiply_reduce_fusion.18
  1078.7 16.1 dynamic_update_slice.30
  1109.9 15.5 multiply_reduce_fusion.18
  1156.7 16.1 dynamic_update_slice.30
  1187.8 15.6 multiply_reduce_fusion.18
  1234.6 16.1 dynamic_update_slice.30
  1395.6 212.1 %all-reduce.21.cloned.1.call-done = (f32[4,1536,384]{2,0,1:T(4,128)}, f32[2,1536,1024]{2,0,1:T(2,128)}) async-done(((f32[4,1536,384]{2,0,1:T(4,128)}, f32[2,1536,1024]{2,0,1:T(2,128)}), (f32[4,1536,384]{2,0,1:T(4,128)}, f32[2,1536,1024]{2,0,1:T(2,128)})) %all-reduce.21.cloned.1.call-update) | async-done | bytes 22020112
  1613.8 157.6 %reduce-scatter.10.cloned.1.call-done = f32[1,384,1536]{2,1,0:T(8,128)} async-done(((f32[1,1536,1536]{2,1,0:T(8,128)}), f32[1,384,1536]{2,1,0:T(8,128)}) %reduce-scatter.10.cloned.1.call-update) | async-done | bytes 2359312 | tf_op jit(solution)/shard_map/reduce_scatter | solution.py:280
  1774.6 41.5 %all-reduce.11 = (f32[2,1536]{1,0:T(2,128)}, f32[2,64]{1,0:T(2,128)}, f32[24]{0:T(128)}) all-reduce(f32[2,1536]{1,0:T(2,128)S(1)} %pad_maximum_fusion.6, f32[2,64]{1,0:T(2,128)S(1)} %pad_add_fusion, f32[24]{0:T(128)S(1)} %negate_dynamic-update-slice_fusion), channel_id=1, replica_groups=mesh['dp'=8,'tp'=4] {'dp','tp'}, use_global_device_ids=true, to_apply=%region_37.38 | all-reduce | flops 3224 | bytes 25792 | tf_op jit(solution)/shard_map/psum | solution.py:294
  1820.6 18.4 reduce-scatter.14.cloned.1.call-done
  1839.0 46.3 %reduce-scatter.12.cloned.1.call-done = f32[384,192]{0,1:T(8,128)} async-done(((f32[384,1536]{0,1:T(8,128)}), f32[384,192]{0,1:T(8,128)}) %reduce-scatter.12.cloned.1.call-update) | async-done | bytes 294928 | tf_op jit(solution)/shard_map/reduce_scatter | solution.py:287
  (400 shorter events, 519.7 us)
Async XLA Ops:
  7.2 45.1 %all-gather.6.cloned.1.call-start = ((), (), s32[]{:S(2)}) async-start(), calls=%async_computation.5 | async-start | bytes 5308416 | tf_op jit(solution)/shard_map/all_gather | solution.py:145
  7.9 213.9 %all-gather.8.cloned.1.call-start = ((), (), s32[]{:S(2)}) async-start(), calls=%async_computation.6 | async-start | bytes 1327104 | tf_op jit(solution)/shard_map/all_gather | solution.py:147
  8.7 547.3 %all-reduce.17.cloned.1.call-start = ((), (), s32[]{:S(2)}) async-start(), calls=%async_computation.7 | async-start | bytes 18874368 | tf_op jit(solution)/shard_map/psum | solution.py:197
  20.0 20.0 %copy-start.71 = (f32[1,24]{1,0:T(1,128)S(1)}, f32[1,24]{1,0:T(1,128)}, u32[]{:S(2)}) copy-start(f32[1,24]{1,0:T(1,128)} %param.25) | copy-start | bytes 292
  23.5 28.8 %copy-start.58 = (f32[1536]{0:T(1024)}, f32[1536]{0:T(1024)S(1)}, u32[]{:S(2)}) copy-start(f32[1536]{0:T(1024)S(1)} %add_rsqrt_fusion.1) | copy-start | bytes 18436
  24.2 28.1 %copy-start.53 = (f32[1536]{0:T(1024)}, f32[1536]{0:T(1024)S(1)}, u32[]{:S(2)}) copy-start(f32[1536]{0:T(1024)S(1)} %get-tuple-element.256) | copy-start | bytes 18436
  43.9 20.3 %copy-start.27 = (f32[1536,3,6]{0,2,1:T(8,128)}, f32[1536,3,6]{0,2,1:T(8,128)S(1)}, u32[]{:S(2)}) copy-start(f32[1536,3,6]{0,2,1:T(8,128)S(1)} %fusion.128) | copy-start | bytes 331780
  46.0 22.6 %copy-start.38 = (f32[1536,6]{0,1:T(8,128)}, f32[1536,6]{0,1:T(8,128)S(1)}, u32[]{:S(2)}) copy-start(f32[1536,6]{0,1:T(8,128)S(1)} %get-tuple-element.327) | copy-start | bytes 110596
  46.0 25.8 %copy-start.40 = (f32[1536,6]{0,1:T(8,128)}, f32[1536,6]{0,1:T(8,128)S(1)}, u32[]{:S(2)}) copy-start(f32[1536,6]{0,1:T(8,128)S(1)} %get-tuple-element.326) | copy-start | bytes 110596
  46.1 22.5 %copy-start.33 = (f32[1536,6]{0,1:T(8,128)}, f32[1536,6]{0,1:T(8,128)S(1)}, u32[]{:S(2)}) copy-start(f32[1536,6]{0,1:T(8,128)S(1)} %get-tuple-element.329) | copy-start | bytes 110596
  46.1 25.8 %copy-start.35 = (f32[1536,6]{0,1:T(8,128)}, f32[1536,6]{0,1:T(8,128)S(1)}, u32[]{:S(2)}) copy-start(f32[1536,6]{0,1:T(8,128)S(1)} %get-tuple-element.328) | copy-start | bytes 110596
  46.1 24.1 %copy-start.63 = (f32[64]{0:T(128)}, f32[64]{0:T(128)S(1)}, u32[]{:S(2)}) copy-start(f32[64]{0:T(128)S(1)} %get-tuple-element.331) | copy-start | bytes 772
  46.1 27.5 %copy-start.61 = (f32[64]{0:T(128)}, f32[64]{0:T(128)S(1)}, u32[]{:S(2)}) copy-start(f32[64]{0:T(128)S(1)} %get-tuple-element.330) | copy-start | bytes 772
  231.1 371.2 %all-gather.10.cloned.1.call-start = ((), (), s32[]{:S(2)}) async-start(), calls=%async_computation.8 | async-start | bytes 7077888 | tf_op jit(solution)/shard_map/all_gather | solution.py:151
  231.6 404.7 %all-gather.12.cloned.1.call-start = ((), (), s32[]{:S(2)}) async-start(), calls=%async_computation.9 | async-start | bytes 3538944 | tf_op jit(solution)/shard_map/all_gather | solution.py:152
  232.2 756.8 %all-reduce.19.cloned.1.call-start = ((), (), s32[]{:S(2)}) async-start(), calls=%async_computation.11 | async-start | bytes 18874368 | tf_op jit(solution)/shard_map/psum | solution.py:233
  566.1 36.2 %copy-start.55 = (f32[1536]{0:T(1024)S(1)}, f32[1536]{0:T(1024)}, u32[]{:S(2)}) copy-start(f32[1536]{0:T(1024)} %get-tuple-element.255) | copy-start | bytes 18436
  664.2 726.1 %reduce-scatter.8.cloned.1.call-start = ((), (), s32[]{:S(2)}) async-start(), calls=%async_computation.10 | async-start | bytes 5898240 | tf_op jit(solution)/shard_map/reduce_scatter | solution.py:212
  715.8 677.9 %reduce-scatter.16.cloned.1.call-start = ((), (), s32[]{:S(2)}) async-start(), calls=%async_computation.15 | async-start | bytes 884736
  1294.7 313.0 %all-reduce.21.cloned.1.call-start = ((), (), s32[]{:S(2)}) async-start(), calls=%async_computation.16 | async-start | bytes 44040192
  1323.3 448.1 %reduce-scatter.10.cloned.1.call-start = ((), (), s32[]{:S(2)}) async-start(), calls=%async_computation.12 | async-start | bytes 11796480 | tf_op jit(solution)/shard_map/reduce_scatter | solution.py:280
  1341.3 497.8 %reduce-scatter.14.cloned.1.call-start = ((), (), s32[]{:S(2)}) async-start(), calls=%async_computation.14 | async-start | bytes 7077888 | tf_op jit(solution)/shard_map/reduce_scatter | solution.py:289
  1352.8 532.5 %reduce-scatter.12.cloned.1.call-start = ((), (), s32[]{:S(2)}) async-start(), calls=%async_computation.13 | async-start | bytes 2654208 | tf_op jit(solution)/shard_map/reduce_scatter | solution.py:287
  1771.5 44.7 %copy-start.16 = (f32[1,384,1536]{2,1,0:T(8,128)S(1)}, f32[1,384,1536]{2,1,0:T(8,128)}, u32[]{:S(2)}) copy-start(f32[1,384,1536]{2,1,0:T(8,128)} %reduce-scatter.10.cloned.1.call-done) | copy-start | bytes 7077892
  (78 other events, 407.2 us)
Sparse Core Ops, SparseCore 0:
  9.9 42.3 all-gather.5
  54.2 24.1 all-gather.7
  231.2 324.7 all-reduce.16
  557.7 44.5 all-gather.9
  604.0 32.3 all-gather.11
  664.3 324.6 all-reduce.18
  991.3 84.2 reduce-scatter.7
  1294.8 34.7 reduce-scatter.15
  1333.7 273.9 all-reduce.20
  1610.0 161.4 reduce-scatter.9
  1775.8 63.1 reduce-scatter.13
  1842.8 42.4 reduce-scatter.11
where the time goes:
time: 1910 us; the launch traced here: 1890 us
  waiting for transfers between devices  1080 us (57%)
  matrix products  327 us (17%)
  local copies, waits for them, and re-layouts  203 us (11%)
  other arithmetic  169 us (9%)
  blocking collectives  66.7 us (3%)
  loops' own time  24.6 us (1%)
    psum x1, waiting for transfers between devices, shards(): mixed_full = inputs + lax.psum(attn_part, 'tp')  324 us
    psum x1, waiting for transfers between devices, shards(): mid_grad = lax.psum(mid_part, 'tp')  273 us
    unnamed x14, waiting for transfers between devices  215 us
    reduce_scatter x1, waiting for transfers between devices, shards(): lax.psum_scatter(input_part, 'tp', scatter_dimension=1, tiled=True)  158 us
    dynamic_update_slice x15, local copies, waits for them, and re-layouts, attend_forward(): outputs, log_totals = lax.map(one_block, starts)  101 us
    dot_general x6, matrix products, block_scores(): jnp.einsum('bqhd,bkhd->bhqk', q_block, key_low, preferred_element_type=jn...  69.8 us
    reduce_scatter x1, waiting for transfers between devices, shards(): lax.psum_scatter(grad_out_proj, 'dp', scatter_dimension=1, tiled=True)  46.3 us
    psum x1, blocking collectives, shards(): lax.psum((jnp.stack([gain_first_grad, gain_mid_grad]), grad_qk, bias_full...  41.5 us
  transfers between devices with their start and end apart: 12, of which 9 were waited for; matrix products, arithmetic and copies ran while one was open for 34% of the time, Pallas kernels for 0%

commit v1 on v0

v1 whole, which is shorter than its diff:
```python
import functools

import jax
import jax.numpy as jnp
import numpy as np
from jax import lax
from jax.experimental import pallas as pl
from jax.experimental.pallas import tpu as pltpu
from jax.sharding import PartitionSpec as P

EPS = 1e-06
BF = jnp.bfloat16
F32 = jnp.float32
VMEM_LIMIT = 58 * 1024 * 1024
NT = (((1,), (1,)), ((), ()))
TN = (((0,), (0,)), ((), ()))


def dot(a, b, dims=(((1,), (0,)), ((), ()))):
    return lax.dot_general(a, b, dims, preferred_element_type=F32)


def params():
    return pltpu.CompilerParams(vmem_limit_bytes=VMEM_LIMIT)


def split2(v):
    hi = v.astype(BF)
    return hi, (v - hi.astype(F32)).astype(BF)


def split3(v):
    hi = v.astype(BF)
    rest = v - hi.astype(F32)
    mid = rest.astype(BF)
    return hi, mid, (rest - mid.astype(F32)).astype(BF)


def lanes(shape):
    return lax.broadcasted_iota(jnp.int32, shape, len(shape) - 1)


def rows_of(shape):
    return lax.broadcasted_iota(jnp.int32, shape, 0)


def const(array, dtype=BF):
    return jnp.asarray(array.astype(np.float32), dtype)


def full(shape):
    return pl.BlockSpec(shape, lambda *_: tuple(0 for _ in shape), pipeline_mode=pl.Buffered(1))


ANY = pl.BlockSpec(memory_space=pl.ANY)
SMEM = pl.BlockSpec(memory_space=pltpu.SMEM)


def pre_kernel(
    heads, x_ref, we_ref, wo_ref, ba_ref, g64_ref, tri_ref, mq_ref, mk_ref, rows_ref, gqk_ref,
    hn_ref, gain_ref, q8_ref, kn_ref, vl_ref, aq_ref, ak_ref, og_ref, q_ref, ks_ref, kd_ref, vd_ref, lg_ref,
    gain_s, carry_k, carry_v, carry_c,
):
    step = pl.program_id(0)
    half = we_ref.shape[0]
    width = q8_ref.shape[1]
    wide = 4 * width

    @pl.when(step == 0)
    def _():
        pick = (lanes((8, 128)) == 3 * heads + rows_of((8, 128))).astype(F32)
        pick = jnp.where(rows_of((8, 128)) < 2, pick, 0.0).astype(BF)
        gain_s[:, :half] = dot(pick, we_ref[:, wide:], NT)
        gain_s[:, half:] = dot(pick, wo_ref[:, wide:], NT)
        carry_k[...] = jnp.zeros_like(carry_k)
        carry_v[...] = jnp.zeros_like(carry_v)
        carry_c[...] = jnp.zeros_like(carry_c)
        gain_ref[...] = gain_s[...]

    x = x_ref[...].astype(F32)
    factor = lax.rsqrt(jnp.mean(x * x, -1, keepdims=True) + EPS)
    hn = (x * factor * gain_s[0:1, :]).astype(BF)
    hn_ref[...] = hn
    proj = dot(hn[:, :half], we_ref[...]) + dot(hn[:, half:], wo_ref[...])
    q = proj[:, :width]
    k = proj[:, width : 2 * width]
    v = proj[:, 2 * width : 3 * width]
    og_ref[...] = jax.nn.sigmoid(proj[:, 3 * width : wide])
    logits = proj[:, wide:]
    lg_ref[...] = logits
    mix = dot(jnp.concatenate(split2(jax.nn.sigmoid(logits)), 1), ba_ref[...])
    first = rows_of(k.shape) == 0
    kd = jnp.where(first, carry_k[0:1, :], pltpu.roll(k, 1, 0)) - k
    vd = jnp.where(first, carry_v[0:1, :], pltpu.roll(v, 1, 0)) - v
    last = k.shape[0] - 1
    carry_k[0:1, :] = k[last:, :]
    carry_v[0:1, :] = v[last:, :]
    ks = k + mix[:, :width] * kd
    vl_ref[...] = (v + mix[:, width:] * vd).astype(BF)
    q_ref[...] = q.astype(BF)
    ks_ref[...] = ks.astype(BF)
    kd_ref[...] = kd.astype(BF)
    vd_ref[...] = vd.astype(BF)
    rq = lax.rsqrt(dot((q * q).astype(BF), g64_ref[...]) + EPS)
    rk = lax.rsqrt(dot((ks * ks).astype(BF), g64_ref[...]) + EPS)
    q8_ref[...] = ((q * rq * gqk_ref[0:1, :]).astype(BF).astype(F32) * 0.125).astype(BF)
    kn_ref[...] = (ks * rk * gqk_ref[1:2, :]).astype(BF)
    z = logits + rows_ref[0:1, :]
    ls = jnp.minimum(z, 0.0) - jnp.log1p(jnp.exp(-jnp.abs(z)))
    sums = dot(tri_ref[...], jnp.concatenate(split3(ls), 1))
    cum = sums[:, :128] + sums[:, 128:256] + sums[:, 256:] + carry_c[0:1, :]
    carry_c[0:1, :] = cum[last:, :]
    parts = jnp.concatenate(split3(cum), 1)
    aq_ref[...] = (dot(parts, mq_ref[...]) + rows_ref[1:2, :]).astype(BF)
    ak_ref[...] = (dot(parts, mk_ref[...]) + rows_ref[2:3, :]).astype(BF)


def pre(x, we, wo, bias_row, gqk, heads):
    seq, model = x.shape
    wide = we.shape[1]
    width = (wide - 128) // 4
    block = min(256, seq)
    ba = np.zeros((256, 2 * width))
    for lane in range(2 * width):
        head = (lane % width) // 64 + (lane // width) * heads
        ba[head, lane] = ba[128 + head, lane] = 1.0
    g64 = np.kron(np.eye(width // 64), np.full((64, 64), 1 / 64))
    tri = np.tril(np.ones((block, block)))
    mq, mk = np.zeros((384, 128)), np.zeros((384, 128))
    ones_q, ones_k = np.zeros((1, 128)), np.zeros((1, 128))
    for head in range(heads):
        for piece in range(3):
            mq[128 * piece + 2 * heads + head, 6 * head + piece] = 1.0
            mk[128 * piece + 2 * heads + head, 6 * head + 3 + piece] = -1.0
            ones_q[0, 6 * head + 3 + piece] = 1.0
            ones_k[0, 6 * head + piece] = 1.0
    rows = jnp.concatenate([bias_row, const(ones_q, F32), const(ones_k, F32), jnp.zeros((5, 128), F32)], 0)

    def row(cols):
        return pl.BlockSpec((block, cols), lambda i: (i, 0))

    def shape(cols, dtype):
        return jax.ShapeDtypeStruct((seq, cols), dtype)

    return pl.pallas_call(
        functools.partial(pre_kernel, heads),
        grid=(seq // block,),
        in_specs=[row(model), full(we.shape), full(wo.shape), full(ba.shape), full(g64.shape), full(tri.shape),
                  full(mq.shape), full(mk.shape), full((8, 128)), full(gqk.shape)],
        out_specs=[row(model), full((8, model))] + [row(width)] * 3 + [row(128)] * 2 + [row(width)] * 5 + [row(128)],
        out_shape=[shape(model, BF), jax.ShapeDtypeStruct((8, model), F32)] + [shape(width, BF)] * 3
        + [shape(128, BF)] * 2 + [shape(width, F32)] + [shape(width, BF)] * 4 + [shape(128, F32)],
        scratch_shapes=[pltpu.VMEM((8, model), F32), pltpu.VMEM((8, width), F32), pltpu.VMEM((8, width), F32),
                        pltpu.VMEM((8, 128), F32)],
        compiler_params=params(),
        cost_estimate=pl.CostEstimate(flops=2 * seq * model * wide, bytes_accessed=30_000_000, transcendentals=0),
        name="pre",
    )(x, we, wo, const(ba), const(g64), const(tri), const(mq), const(mk), rows, gqk)


def fwd_kernel(chunk, block, q_ref, aq_ref, k_ref, ak_ref, v_ref, og_ref, *refs):
    u_ref, att_ref, li_ref = refs[-3:]
    pair = pl.program_id(0)
    q, aq = q_ref[...], aq_ref[...]
    lane = lanes(q.shape)
    ones = jnp.ones((block, 128), BF)
    out = []
    for side in range(2):
        head = 2 * pair + side
        mine = (lane >= 64 * side) & (lane < 64 * side + 64)
        aug = (lane >= 6 * head) & (lane < 6 * head + 6)
        zero = jnp.zeros_like(q)
        qa = jnp.concatenate([jnp.where(mine, q, zero), jnp.where(aug, aq, zero)], 1)
        acc = jnp.zeros((block, 256), F32)
        for j in range(chunk + 1):
            at = slice(j * block, (j + 1) * block)
            e = jnp.exp(dot(qa, jnp.concatenate([k_ref[at, :], ak_ref[at, :]], 1), NT))
            if j == chunk:
                e = jnp.where(rows_of(e.shape) >= lanes(e.shape), e, 0.0)
            acc = acc + dot(e.astype(BF), jnp.concatenate([v_ref[at, :], ones], 1))
        out.append(acc)
    low = lane < 64
    total = jnp.where(low, out[0][:, 128:], out[1][:, 128:])
    inverse = 1.0 / total
    att = jnp.where(low, out[0][:, :128], out[1][:, :128]) * inverse
    u_ref[...] = (att * og_ref[...]).astype(BF)
    att_ref[...] = att
    li_ref[...] = inverse


def attend(chunk, block, q8, aq, kn, ak, vl, og, kept):
    seq, width = q8.shape
    keys = (chunk + 1) * block
    grid = (width // 128,)
    mine = pl.BlockSpec((block, 128), lambda p: (chunk, p))
    other = pl.BlockSpec((keys, 128), lambda p: (0, p))
    return pl.pallas_call(
        functools.partial(fwd_kernel, chunk, block),
        grid=grid,
        in_specs=[mine, pl.BlockSpec((block, 128), lambda p: (chunk, 0)), other,
                  pl.BlockSpec((keys, 128), lambda p: (0, 0)), other, mine] + [ANY] * len(kept),
        out_specs=[pl.BlockSpec((block, 128), lambda p: (0, p)), mine, mine],
        out_shape=[jax.ShapeDtypeStruct((block, width), BF)] + [jax.ShapeDtypeStruct((seq, width), F32)] * 2,
        input_output_aliases={6 + i: 1 + i for i in range(len(kept))},
        compiler_params=params(),
        cost_estimate=pl.CostEstimate(flops=2 * 2 * block * keys * 256 * width // 64, bytes_accessed=5_000_000,
                                      transcendentals=block * keys * width // 64),
        name="attend",
    )(q8, aq, kn, ak, vl, og, *kept)


def ffn_kernel(
    count, chunk, block, step_rows, own, at_ref, x_ref, cot_ref, gain_ref, oe_ref, oo_ref, fe_ref, fo_ref, *refs
):
    us, outs = refs[:count], refs[-8:]
    h2_ref, hid_ref, dgu_ref, res_ref, uc_ref, part_ref, du_ref, gmid_ref = outs
    half = oe_ref.shape[0]
    hidden = hid_ref.shape[1]
    u = jnp.concatenate([r[...] for r in us], 1)
    uc_ref[...] = u
    x = x_ref[...].astype(F32)
    cot = cot_ref[...]
    y1 = x + jnp.concatenate([dot(u, oe_ref[...], NT), dot(u, oo_ref[...], NT)], 1)
    factor = lax.rsqrt(jnp.mean(y1 * y1, -1, keepdims=True) + EPS)
    n = y1 * factor
    gain = gain_ref[1:2, :]
    h2 = (n * gain).astype(BF)
    h2_ref[...] = h2
    gu = dot(h2[:, :half], fe_ref[:, : 2 * hidden]) + dot(h2[:, half:], fo_ref[:, : 2 * hidden])
    g, up = gu[:, :hidden], gu[:, hidden:]
    sg = jax.nn.sigmoid(g)
    act = g * sg
    hid = (act * up).astype(BF)
    hid_ref[...] = hid
    dhid = dot(cot[:, :half], fe_ref[:, 2 * hidden :]) + dot(cot[:, half:], fo_ref[:, 2 * hidden :])
    dg = dhid * up * sg * (1.0 + g * (1.0 - sg))
    dgu = jnp.concatenate([dg.astype(BF), (dhid * act).astype(BF)], 1)
    dgu_ref[...] = dgu
    part = jnp.concatenate([dot(hid, fe_ref[:, 2 * hidden :], NT), dot(hid, fo_ref[:, 2 * hidden :], NT)], 1)
    token = chunk * block + pl.program_id(0) * step_rows + rows_of((step_rows, 1))
    owned = (token >= at_ref[0] * own) & (token < (at_ref[0] + 1) * own)
    part_ref[...] = (part + jnp.where(owned, y1, 0.0)).astype(BF)
    dh2 = jnp.concatenate([dot(dgu, fe_ref[:, : 2 * hidden], NT), dot(dgu, fo_ref[:, : 2 * hidden], NT)], 1)
    gmid = jnp.sum(dh2 * n, 0, keepdims=True)

    @pl.when(pl.program_id(0) == 0)
    def _():
        gmid_ref[...] = jnp.zeros_like(gmid_ref)

    gmid_ref[0:1, :] += gmid
    wd = gain * dh2
    res = factor * (wd - n * jnp.mean(wd * n, -1, keepdims=True))
    res = jnp.where(at_ref[0] == 0, res + cot.astype(F32), res).astype(BF)
    res_ref[...] = res
    du_ref[...] = (dot(res[:, :half], oe_ref[...]) + dot(res[:, half:], oo_ref[...])).astype(BF)


def feed(chunk, block, own, place, x, cot, gains, oe, oo, fe, fo, us, kept):
    seq, model = x.shape
    hidden = fe.shape[1] // 3
    count = len(us)
    width = us[0].shape[1]
    step_rows = min(256, block)
    per = block // step_rows

    def mine(cols):
        return pl.BlockSpec((step_rows, cols), lambda i: (chunk * per + i, 0))

    def local(cols):
        return pl.BlockSpec((step_rows, cols), lambda i: (i, 0))

    kept_cols = [model, hidden, 2 * hidden, model, count * width, model]
    return pl.pallas_call(
        functools.partial(ffn_kernel, count, chunk, block, step_rows, own),
        grid=(per,),
        in_specs=[SMEM, mine(model), mine(model), full(gains.shape), full(oe.shape), full(oo.shape), full(fe.shape),
                  full(fo.shape)] + [local(width)] * count + [ANY] * len(kept),
        out_specs=[mine(c) for c in kept_cols] + [local(count * width), full((8, model))],
        out_shape=[jax.ShapeDtypeStruct((seq, c), BF) for c in kept_cols]
        + [jax.ShapeDtypeStruct((block, count * width), BF), jax.ShapeDtypeStruct((8, model), F32)],
        input_output_aliases={8 + count + i: i for i in range(len(kept))},
        compiler_params=params(),
        cost_estimate=pl.CostEstimate(flops=2 * block * model * (2 * count * width + 6 * hidden),
                                      bytes_accessed=30_000_000, transcendentals=0),
        name="feed",
    )(place, x, cot, gains, oe, oo, fe, fo, *us, *kept)


def bwd_kernel(
    heads, block, q_ref, aq_ref, k_ref, ak_ref, v_ref, og_ref, att_ref, li_ref, du_ref, ms_ref,
    dq_ref, dk_ref, dv_ref, dc_ref, da_s, ad_s,
):
    pair = pl.program_id(0)
    seq = q_ref.shape[0]
    count = seq // block
    lane = lanes((block, 128))
    zero = jnp.zeros((block, 128), BF)
    ones = jnp.ones((block, 128), BF)
    third = lane - 3 * (lane // 3)
    for i in range(count):
        at = slice(i * block, (i + 1) * block)
        da = (du_ref[at, :].astype(F32) * og_ref[at, :] * li_ref[at, :]).astype(BF)
        da_s[at, :] = da
        delta = dot(jnp.concatenate(split2(da.astype(F32) * att_ref[at, :]), 1), ms_ref[...])
        hi, mid, rest = split3(-delta)
        ad_s[at, :] = jnp.where(third == 0, hi, jnp.where(third == 1, mid, rest))
    dk_ref[...] = jnp.zeros_like(dk_ref)
    dv_ref[...] = jnp.zeros_like(dv_ref)

    @pl.when(pair == 0)
    def _():
        dc_ref[...] = jnp.zeros_like(dc_ref)

    vone = jnp.where(lane < 6, ones, zero)
    for i in range(count):
        at = slice(i * block, (i + 1) * block)
        q, aq, da, ad = q_ref[at, :], aq_ref[at, :], da_s[at, :], ad_s[at, :]
        dq = []
        for side in range(2):
            head = 2 * pair + side
            mine = (lane >= 64 * side) & (lane < 64 * side + 64)
            aug = (lane >= 6 * head) & (lane < 6 * head + 6)
            column = lane == 2 * heads + head
            qh = jnp.where(mine, q, zero)
            qa = jnp.concatenate([qh, jnp.where(aug, aq, zero)], 1)
            qo = jnp.concatenate([qh, ones], 1)
            dah = jnp.where(mine, da, zero)
            daa = jnp.concatenate([dah, jnp.where((lane >= 3 * side) & (lane < 3 * side + 3), ad, zero)], 1)
            acc = jnp.zeros((block, 256), F32)
            for j in range(i + 1):
                to = slice(j * block, (j + 1) * block)
                k = k_ref[to, :]
                e = jnp.exp(dot(jnp.concatenate([k, ak_ref[to, :]], 1), qa, NT))
                if j == i:
                    e = jnp.where(rows_of(e.shape) <= lanes(e.shape), e, 0.0)
                dv_ref[to, :] += dot(e.astype(BF), dah)
                ds = (e * dot(jnp.concatenate([v_ref[to, :], vone], 1), daa, NT)).astype(BF)
                dk = dot(ds, qo)
                dk_ref[to, :] += dk[:, :128]
                dc_ref[to, :] -= jnp.where(column, dk[:, 128:], 0.0)
                acc = acc + dot(ds, jnp.concatenate([k, ones], 1), TN)
            dq.append(acc[:, :128])
            dc_ref[at, :] += jnp.where(column, acc[:, 128:], 0.0)
        dq_ref[at, :] = jnp.where(lane < 64, dq[0], dq[1]) * 0.125


def attend_back(block, heads, q8, aq, kn, ak, vl, og, att, li, du):
    seq, width = q8.shape
    ms = np.zeros((256, 128))
    for lane in range(256):
        ms[lane, 3 * ((lane % 128) // 64) : 3 * ((lane % 128) // 64) + 3] = 1.0
    pair = pl.BlockSpec((seq, 128), lambda p: (0, p))
    one = pl.BlockSpec((seq, 128), lambda p: (0, 0))
    return pl.pallas_call(
        functools.partial(bwd_kernel, heads, block),
        grid=(width // 128,),
        in_specs=[pair, one, pair, one, pair, pair, pair, pair, pair, full((256, 128))],
        out_specs=[pair, pair, pair, one],
        out_shape=[jax.ShapeDtypeStruct((seq, width), F32)] * 3 + [jax.ShapeDtypeStruct((seq, 128), F32)],
        scratch_shapes=[pltpu.VMEM((seq, 128), BF), pltpu.VMEM((seq, 128), BF)],
        compiler_params=params(),
        cost_estimate=pl.CostEstimate(flops=5 * seq * seq * 256 * width // 64, bytes_accessed=25_000_000,
                                      transcendentals=seq * seq * width // 128),
        name="attend_back",
    )(q8, aq, kn, ak, vl, og, att, li, du, const(ms))


def post_kernel(
    heads, dq_ref, dk_ref, dv_ref, dc_ref, q_ref, ks_ref, kd_ref, vd_ref, lg_ref, du_ref, att_ref, og_ref, x_ref,
    res_ref, gain_ref, we_ref, wo_ref, ba_ref, g64_ref, tri_ref, ms_ref, rows_ref, gqk_ref,
    dp_ref, gt_ref, g0_ref, gq_ref, gb_ref, carry_k, carry_v, carry_c,
):
    step = pl.program_id(0)
    half = we_ref.shape[0]
    width = dq_ref.shape[1]
    rows = dq_ref.shape[0]

    @pl.when(step == 0)
    def _():
        carry_k[...] = jnp.zeros_like(carry_k)
        carry_v[...] = jnp.zeros_like(carry_v)
        carry_c[...] = jnp.zeros_like(carry_c)
        g0_ref[...] = jnp.zeros_like(g0_ref)
        gq_ref[...] = jnp.zeros_like(gq_ref)
        gb_ref[...] = jnp.zeros_like(gb_ref)

    def norm_back(raw, gain, grad):
        r = lax.rsqrt(dot((raw * raw).astype(BF), g64_ref[...]) + EPS)
        n = raw * r
        wd = grad * gain
        return r * (wd - n * dot((wd * n).astype(BF), g64_ref[...])), jnp.sum(grad * n, 0, keepdims=True)

    dq, gq = norm_back(q_ref[...].astype(F32), gqk_ref[0:1, :], dq_ref[...])
    dks, gk = norm_back(ks_ref[...].astype(F32), gqk_ref[1:2, :], dk_ref[...])
    gq_ref[0:1, :] += gq
    gq_ref[1:2, :] += gk
    dvs = dv_ref[...]
    logits = lg_ref[...]
    sg = jax.nn.sigmoid(logits)
    mix = dot(jnp.concatenate(split2(sg), 1), ba_ref[...])
    end = rows_of(dks.shape) == rows - 1

    def shift_back(grad, part, carry):
        w = part * grad
        later = jnp.where(end, carry[0:1, :], pltpu.roll(w, rows - 1, 0))
        carry[0:1, :] = w[0:1, :]
        return grad - w + later

    dk = shift_back(dks, mix[:, :width], carry_k)
    dv = shift_back(dvs, mix[:, width:], carry_v)
    terms = jnp.concatenate([dks * kd_ref[...].astype(F32), dvs * vd_ref[...].astype(F32)], 1)
    hi, rest = split2(terms)
    dmix = dot(hi, ms_ref[...]) + dot(rest, ms_ref[...])
    sums = dot(tri_ref[...], jnp.concatenate(split3(dc_ref[...]), 1))
    dls = sums[:, :128] + sums[:, 128:256] + sums[:, 256:] + carry_c[0:1, :]
    carry_c[0:1, :] = dls[0:1, :]
    lane = lanes(logits.shape)
    dz = dls * jax.nn.sigmoid(-(logits + rows_ref[0:1, :]))
    dgl = jnp.where(lane < 2 * heads, dmix * sg * (1.0 - sg), jnp.where(lane < 3 * heads, dz, 0.0))
    gb_ref[0:1, :] += jnp.sum(dgl, 0, keepdims=True)
    og = og_ref[...]
    do = du_ref[...].astype(F32) * att_ref[...] * og * (1.0 - og)
    dp = jnp.concatenate([dq.astype(BF), dk.astype(BF), dv.astype(BF), do.astype(BF), dgl.astype(BF)], 1)
    dp_ref[...] = dp
    dhn = jnp.concatenate([dot(dp, we_ref[...], NT), dot(dp, wo_ref[...], NT)], 1)
    x = x_ref[...].astype(F32)
    factor = lax.rsqrt(jnp.mean(x * x, -1, keepdims=True) + EPS)
    n = x * factor
    g0_ref[0:1, :] += jnp.sum(dhn * n, 0, keepdims=True)
    wd = dhn * gain_ref[0:1, :]
    back = factor * (wd - n * jnp.mean(wd * n, -1, keepdims=True))
    gt_ref[...] = (back + res_ref[...].astype(F32)).astype(BF)


def post(heads, dq, dk, dv, dc, q, ks, kd, vd, lg, du, att, og, x, res, gains, we, wo, bias_row, gqk):
    seq, width = dq.shape
    model = x.shape[1]
    wide = we.shape[1]
    block = min(256, seq)
    count = seq // block
    ba = np.zeros((256, 2 * width))
    ms = np.zeros((2 * width, 128))
    for lane in range(2 * width):
        head = (lane % width) // 64 + (lane // width) * heads
        ba[head, lane] = ba[128 + head, lane] = 1.0
        ms[lane, head] = 1.0
    g64 = np.kron(np.eye(width // 64), np.full((64, 64), 1 / 64))
    tri = np.triu(np.ones((block, block)))
    rows = jnp.concatenate([bias_row, jnp.zeros((7, 128), F32)], 0)

    def row(cols):
        return pl.BlockSpec((block, cols), lambda i: (count - 1 - i, 0))

    return pl.pallas_call(
        functools.partial(post_kernel, heads),
        grid=(count,),
        in_specs=[row(width)] * 3 + [row(128)] + [row(width)] * 4 + [row(128)] + [row(width)] * 3 + [row(model)] * 2
        + [full(gains.shape), full(we.shape), full(wo.shape), full(ba.shape), full(g64.shape), full(tri.shape),
           full(ms.shape), full((8, 128)), full(gqk.shape)],
        out_specs=[row(wide), row(model), full((8, model)), full((8, width)), full((8, 128))],
        out_shape=[jax.ShapeDtypeStruct((seq, wide), BF), jax.ShapeDtypeStruct((seq, model), BF),
                   jax.ShapeDtypeStruct((8, model), F32), jax.ShapeDtypeStruct((8, width), F32),
                   jax.ShapeDtypeStruct((8, 128), F32)],
        scratch_shapes=[pltpu.VMEM((8, width), F32), pltpu.VMEM((8, width), F32), pltpu.VMEM((8, 128), F32)],
        compiler_params=params(),
        cost_estimate=pl.CostEstimate(flops=2 * seq * model * wide, bytes_accessed=40_000_000, transcendentals=0),
        name="post",
    )(dq, dk, dv, dc, q, ks, kd, vd, lg, du, att, og, x, res, gains, we, wo, const(ba), const(g64), const(tri),
      const(ms), rows, gqk)


def swap(value, axis, bit):
    size = lax.axis_size(axis)
    return lax.ppermute(value, axis, [(i, i ^ bit) for i in range(size)])


def turn(value):
    size = lax.axis_size("tp")
    return lax.ppermute(value, "tp", [(i, (i + 1) % size) for i in range(size)])


def add(a, b):
    return (a.astype(F32) + b.astype(F32)).astype(BF)


def high_bits(size):
    bits, bit = [], 2
    while bit < size:
        bits.append(bit)
        bit *= 2
    return bits


def dp_gather(shard):
    size = lax.axis_size("dp")
    pieces = {0: shard}
    if size == 8:
        half = shard.shape[0] // 2
        pieces[2] = swap(shard, "dp", 2)
        pieces[4] = swap(shard, "dp", 4)
        pieces[6] = jnp.concatenate(
            [swap(pieces[2][:half], "dp", 4), swap(pieces[4][half:], "dp", 2)], 0
        )
    else:
        for bit in high_bits(size):
            pieces.update({r | bit: swap(p, "dp", bit) for r, p in list(pieces.items())})
    even = jnp.concatenate([pieces[r] for r in range(0, size, 2)], 0)
    return even, swap(even, "dp", 1)


def dp_scatter(even, odd):
    size = lax.axis_size("dp")
    total = add(even, swap(odd, "dp", 1))
    rows = total.shape[0] // (size // 2)
    pieces = {r: total[rows * (r // 2) : rows * (r // 2 + 1)] for r in range(0, size, 2)}
    if size == 8:
        half = rows // 2
        from_x = swap(pieces[6][:half], "dp", 2)
        from_y = swap(pieces[6][half:], "dp", 4)
        to_y = jnp.concatenate([add(pieces[4][:half], from_x), pieces[4][half:]], 0)
        to_x = jnp.concatenate([pieces[2][:half], add(pieces[2][half:], from_y)], 0)
        got_x, got_y = swap(to_x, "dp", 2), swap(to_y, "dp", 4)
        return pieces[0].astype(F32) + got_x.astype(F32) + got_y.astype(F32)
    for bit in reversed(high_bits(size)):
        got = {r: swap(pieces[r], "dp", bit) for r in pieces if r & bit}
        pieces = {r: add(p, got[r | bit]) for r, p in pieces.items() if not r & bit}
    return pieces[0].astype(F32)


def ring_gather(value):
    out = [value]
    for _ in range(lax.axis_size("tp") - 1):
        out.append(turn(out[-1]))
    return out


def ring_scatter_parts(parts):
    acc = parts[1]
    for part in parts[2:]:
        acc = add(turn(acc), part)
    return turn(acc)


def pad_to(value, size, axis):
    extra = size - value.shape[axis]
    if not extra:
        return value
    return jnp.pad(value, [(0, extra if a == axis else 0) for a in range(value.ndim)])


def shards(
    tokens, attn_in, head_gates, out_proj, norm_gains, qk_gains, forget_bias, gate_up, down_proj, carried_offset,
    reset_flag, cotangent,
):
    dp, tp = lax.axis_size("dp"), lax.axis_size("tp")
    me_d, me_t = lax.axis_index("dp"), lax.axis_index("tp")
    _, seq, model = tokens.shape
    own = seq // tp
    cut = attn_in.shape[1]
    width_real = attn_in.shape[2]
    heads_real = head_gates.shape[2]
    heads = heads_real + heads_real % 2
    width = 64 * heads
    hidden = gate_up.shape[2]
    block = 512 if seq % 512 == 0 else seq
    chunks = seq // block

    attn_rows = jnp.transpose(pad_to(attn_in, width, 2), (1, 0, 2)).reshape(cut, 4 * width)
    gate_rows = jnp.transpose(pad_to(head_gates, heads, 2), (1, 0, 2)).reshape(cut, 3 * heads)
    gate_rows = pad_to(jnp.concatenate([gate_rows, jnp.transpose(norm_gains)], 1), 128, 1)
    we, wo = dp_gather(jnp.concatenate([attn_rows, gate_rows], 1))
    out_rows = jnp.concatenate(ring_gather(pad_to(jnp.transpose(out_proj), width, 1)), 1)
    ffn_rows = jnp.concatenate([gate_up[0], gate_up[1], jnp.transpose(down_proj)], 1)
    we, wo, out_rows = lax.optimization_barrier((we, wo, out_rows))
    oe, oo = dp_gather(out_rows)
    oe, oo, ffn_rows = lax.optimization_barrier((oe, oo, ffn_rows))
    fe, fo = dp_gather(ffn_rows)

    order = [r for r in range(0, dp, 2)] + [r for r in range(1, dp, 2)]
    source = jnp.concatenate([(me_d ^ r) * cut + jnp.arange(cut, dtype=jnp.int32) for r in order])
    place = (jnp.arange(model, dtype=jnp.int32)[:, None] == source[None, :]).astype(BF)
    x = dot(tokens[0], place).astype(BF)
    cot = dot(cotangent[0], place).astype(BF)

    bias = lax.dynamic_slice_in_dim(forget_bias.astype(F32), me_t * heads_real, heads_real, 0)
    offset = lax.dynamic_slice_in_dim(carried_offset[0], me_t * heads_real, heads_real, 0)
    bias = bias + (1 - reset_flag[0]).astype(F32) * offset
    bias_row = jnp.pad(bias, (2 * heads, 128 - 2 * heads - heads_real))[None, :]
    gqk = pad_to(jnp.tile(qk_gains.astype(F32), (1, heads)), 8, 0)

    hn, gains, q8, kn, vl, aq, ak, og, q, ks, kd, vd, lg = pre(x, we, wo, bias_row, gqk, heads)
    at = me_t.astype(jnp.int32)[None]
    kept_att, kept_ffn, gmids, dus = (), (), [], []
    for chunk in range(chunks):
        u, *kept_att = attend(chunk, block, q8, aq, kn, ak, vl, og, kept_att)
        *kept_ffn, du, gmid = feed(chunk, block, own, at, x, cot, gains, oe, oo, fe, fo, ring_gather(u), kept_ffn)
        parts = [du[:, s * width : (s + 1) * width] for s in range(tp)]
        dus.append(add(ring_scatter_parts(parts), parts[0]))
        gmids.append(gmid[0:1])
    att, li = kept_att
    h2, hid, dgu, res, uc, part = kept_ffn
    du = jnp.concatenate(dus, 0)

    part, du = lax.optimization_barrier((part, du))

    def token_parts(values):
        return [
            lax.dynamic_slice_in_dim(values, lax.rem(me_t - s + tp, tp) * own, own, 0) for s in range(tp)
        ]

    parts = token_parts(part)
    result = dot(add(ring_scatter_parts(parts), parts[0]), place, NT).astype(BF)

    mid = model // 2

    def weight_grad(left, right):
        return dp_scatter(dot(left[:, :mid], right, TN).astype(BF), dot(left[:, mid:], right, TN).astype(BF))

    grad_down = weight_grad(cot, hid)
    grad_gu = weight_grad(h2, dgu)
    grad_out = weight_grad(res, uc)

    dq, dk, dv, dc = attend_back(block, heads, q8, aq, kn, ak, vl, og, att, li, du)
    dp_all, gt, g0, gq, gb = post(
        heads, dq, dk, dv, dc, q, ks, kd, vd, lg, du, att, og, x, res, gains, we, wo, bias_row, gqk
    )
    parts = token_parts(gt)
    grad_tokens = dot(parts[0], place, NT) + dot(ring_scatter_parts(parts), place, NT)
    grad_attn = weight_grad(hn, dp_all)

    out_low = grad_out.astype(BF)
    out_parts = [out_low[:, s * width : (s + 1) * width] for s in range(tp)]
    grad_out_own = out_parts[0].astype(F32) + ring_scatter_parts(out_parts).astype(F32)

    norm_rows = jnp.concatenate([g0[0:1], sum(gmids)], 0)
    norm_rows = sum(dot(part, place, NT) for part in split3(norm_rows))
    gq = gq[0:2].reshape(2, heads, 64).sum(1)
    gb = lax.dynamic_update_slice_in_dim(
        jnp.zeros(forget_bias.shape, F32), gb[0, 2 * heads : 2 * heads + heads_real], me_t * heads_real, 0
    )
    sizes = [2 * model, 2 * 64, forget_bias.shape[0]]
    flat = jnp.concatenate([norm_rows.reshape(-1), gq.reshape(-1), gb])
    flat = jnp.pad(flat, (0, -flat.shape[0] % 1024)).reshape(-1, 128)
    for axis, size in (("tp", tp), ("dp", dp)):
        bit = 1
        while bit < size:
            flat = flat + swap(flat, axis, bit)
            bit *= 2
    flat = flat.reshape(-1)
    norm_grad = flat[: sizes[0]].reshape(2, model)
    qk_grad = flat[sizes[0] : sizes[0] + sizes[1]].reshape(2, 64)
    bias_grad = flat[sizes[0] + sizes[1] : sum(sizes)]

    grad_attn_in = jnp.transpose(grad_attn[:, : 4 * width].reshape(cut, 4, width)[:, :, :width_real], (1, 0, 2))
    grad_gates = grad_attn[:, 4 * width : 4 * width + 3 * heads].reshape(cut, 3, heads)[:, :, :heads_real]
    return (
        result[None],
        grad_tokens[None],
        grad_attn_in,
        jnp.transpose(grad_gates, (1, 0, 2)),
        jnp.transpose(grad_out_own[:, :width_real]),
        jnp.stack([grad_gu[:, :hidden], grad_gu[:, hidden:]]),
        jnp.transpose(grad_down),
        norm_grad,
        qk_grad,
        bias_grad,
    )


def solution(mesh):
    return jax.shard_map(
        shards,
        mesh=mesh,
        in_specs=(
            P("dp", None, None), P(None, "dp", "tp"), P(None, "dp", "tp"), P("tp", "dp"), P(None, "dp"), P(), P(),
            P(None, "dp", "tp"), P("tp", "dp"), P("dp", None), P("dp"), P("dp", None, None),
        ),
        out_specs=(
            P("dp", "tp", None), P("dp", "tp", None), P(None, "dp", "tp"), P(None, "dp", "tp"), P("tp", "dp"),
            P(None, "dp", "tp"), P("tp", "dp"), P(), P(), P(),
        ),
        check_vma=False,
    )
```

time: 1910 us -> 718 us (0.38)
  waiting for transfers between devices: 1080 us -> 345 us
  matrix products: 327 us -> 89.2 us
  local copies, waits for them, and re-layouts: 203 us -> 24.3 us
  Pallas kernels: 0 us -> 173 us
  other arithmetic: 169 us -> 20.9 us
  blocking collectives: 66.7 us -> 0 us
  starting transfers between devices: 0.87 us -> 54 us
  loops' own time: 24.6 us -> 0 us
    psum x2 -> x0, waiting for transfers between devices: 597 us -> none  [the longest x1 324 us: shards(): mixed_full = inputs + lax.psum(attn_part, 'tp')]
    ppermute x0 -> x70, waiting for transfers between devices: none -> 345 us  [the longest x30 220 us: turn(): return lax.ppermute(value, 'tp', [(i, (i + 1) % size) for i in range(size)])]
    dot_general x36 -> x16, matrix products: 327 us -> 89.2 us  [dot(): return lax.dot_general(a, b, dims, preferred_element_type=F32)]
    reduce_scatter x4 -> x0, waiting for transfers between devices: 222 us -> none  [the longest x1 158 us: shards(): lax.psum_scatter(input_part, 'tp', scatter_dimension=1, tiled=True)]
    unnamed x14 -> x0, waiting for transfers between devices: 215 us -> none
    pallas_call x0 -> x9, Pallas kernels: none -> 173 us  [the longest x3 73.3 us: feed(): pl.pallas_call(functools.partial(ffn_kernel, count, chunk, block, step_ro...]
    dynamic_update_slice x15 -> x1, local copies, waits for them, and re-layouts: 101 us -> 0.84 us  [shards(): lax.dynamic_update_slice_in_dim(jnp.zeros(forget_bias.shape, F32), gb[0,...]
    reduce_sum x19 -> x1, other arithmetic: 99.3 us -> 0.02 us  [shards(): gq = gq[0:2].reshape(2, heads, 64).sum(1)]
  transfers between devices with their start and end apart: 12 -> 70, of which waited for: 9 -> 41; matrix products, arithmetic and copies ran while one was open for 34% -> 14% of each run, Pallas kernels for 0% -> 21%
where the time goes in v1:
time: 718 us; the launch traced here: 709 us
  waiting for transfers between devices  345 us (48%)
  Pallas kernels  173 us (24%)
  matrix products  89.2 us (12%)
  starting transfers between devices  54 us (8%)
  local copies, waits for them, and re-layouts  24.3 us (3%)
  other arithmetic  20.9 us (3%)
    ppermute x30, waiting for transfers between devices, turn(): return lax.ppermute(value, 'tp', [(i, (i + 1) % size) for i in range(size)])  220 us
    ppermute x40, waiting for transfers between devices, swap(): return lax.ppermute(value, axis, [(i, i ^ bit) for i in range(size)])  125 us
    dot_general x16, matrix products, dot(): return lax.dot_general(a, b, dims, preferred_element_type=F32)  89.2 us
    pallas_call x3, Pallas kernels, feed(): pl.pallas_call(functools.partial(ffn_kernel, count, chunk, block, step_ro...  73.3 us
    ppermute x40, starting transfers between devices, swap(): return lax.ppermute(value, axis, [(i, i ^ bit) for i in range(size)])  33.9 us
    pallas_call x1, Pallas kernels, attend_back(): pl.pallas_call(functools.partial(bwd_kernel, heads, block), grid=(width /...  32.6 us
    pallas_call x1, Pallas kernels, post(): pl.pallas_call(functools.partial(post_kernel, heads), grid=(count,), in_s...  25.3 us
    pallas_call x3, Pallas kernels, attend(): pl.pallas_call(functools.partial(fwd_kernel, chunk, block), grid=grid, in...  22.2 us
  transfers between devices with their start and end apart: 70, of which 41 were waited for; matrix products, arithmetic and copies ran while one was open for 14% of the time, Pallas kernels for 21%

profile of v1, /device:TPU:0, one launch (start us, length us, event | category | flops | bytes accessed | tf_op | source)
XLA Modules:
  0.0 709.2 jit_solution(3611775874730735088)
XLA Ops:
  7.9 12.9 %collective-permute-done = bf16[192,1664]{1,0:T(8,128)(2,1)S(1)} collective-permute-done((bf16[192,1664]{1,0:T(8,128)(2,1)S(1)}, bf16[192,1664]{1,0:T(8,128)(2,1)S(1)}, u32[]{:S(2)}, u32[]{:S(2)}) %collective-permute-start) | collective-permute-done | bytes 639008 | tf_op jit(solution)/shard_map/ppermute | solution.py:474
  55.5 10.9 %collective-permute-done.8 = bf16[192,1536]{1,0:T(8,128)(2,1)S(1)} collective-permute-done((bf16[192,1536]{1,0:T(8,128)(2,1)S(1)}, bf16[192,1536]{1,0:T(8,128)(2,1)S(1)}, u32[]{:S(2)}, u32[]{:S(2)}) %collective-permute-start.8) | collective-permute-done | bytes 589856 | tf_op jit(solution)/shard_map/ppermute | solution.py:474
  85.9 22.9 %collective-permute-done.13 = bf16[192,3072]{1,0:T(8,128)(2,1)S(1)} collective-permute-done((bf16[192,3072]{1,0:T(8,128)(2,1)S(1)}, bf16[192,3072]{1,0:T(8,128)(2,1)S(1)}, u32[]{:S(2)}, u32[]{:S(2)}) %collective-permute-start.13) | collective-permute-done | bytes 1179680 | tf_op jit(solution)/shard_map/ppermute | solution.py:474
  112.9 10.6 %collective-permute-done.15 = bf16[96,3072]{1,0:T(8,128)(2,1)S(1)} collective-permute-done((bf16[96,3072]{1,0:T(8,128)(2,1)S(1)}, bf16[96,3072]{1,0:T(8,128)(2,1)S(1)}, u32[]{:S(2)}, u32[]{:S(2)}) %collective-permute-start.15) | collective-permute-done | bytes 589856 | tf_op jit(solution)/shard_map/ppermute | solution.py:474
  125.9 11.6 %fusion.11.x_ref = bf16[1536,1536]{1,0:T(8,128)(2,1)} fusion(bf16[1,1536,1536]{2,1,0:T(8,128)(2,1)} %param.24, s32[1536]{0:T(1024)S(1)} %concatenate.63), kind=kOutput, calls=%fused_computation.12 | convolution fusion | flops 7252475904 | bytes 9443328 | tf_op jit(solution)/shard_map/dot_general | solution.py:20
  139.7 19.7 %pre.1 = (bf16[1536,1536]{1,0:T(8,128)(2,1)}, f32[8,1536]{1,0:T(8,128)}, bf16[1536,384]{1,0:T(8,128)(2,1)}, bf16[1536,384]{1,0:T(8,128)(2,1)}, bf16[1536,384]{1,...) custom-call(bf16[1536,1536]{1,0:T(8,128)(2,1)} %fusion.11.x_ref, ...), custom_call_target="tpu_custom_call" | custom-call | flops 7851737088 | bytes 30000000 | tf_op jit(solution)/shard_map/pre/pallas_call | solution.py:145
  172.7 9.3 %attend.5 = (bf16[512,384]{1,0:T(8,128)(2,1)}, f32[1536,384]{1,0:T(8,128)}, f32[1536,384]{1,0:T(8,128)}) custom-call(bf16[1536,384]{1,0:T(8,128)(2,1)} %get-tuple-element.80.q_ref, bf16[1536,128]{1,0:T(8,128)(2,1)} %get-tuple-element.81.aq_ref, bf16[1536,384]{1,0:T(8,128)(2,1)} %get-tuple-element.82.k_ref, ...), custom_call_target="tpu_custom_call", output_to_operand_aliasing={{1}: (6, {}), {2}: (7, {})} | custom-call | flops 4831838208 | bytes 5000000 | tf_op jit(solution)/shard_map/attend/pallas_call | solution.py:197
  187.0 9.0 %collective-permute-done.18.refs_1_ = bf16[512,384]{1,0:T(8,128)(2,1)S(1)} collective-permute-done((bf16[512,384]{1,0:T(8,128)(2,1)}, bf16[512,384]{1,0:T(8,128)(2,1)S(1)}, u32[]{:S(2)}, u32[]{:S(2)}) %collective-permute-start.18) | collective-permute-done | bytes 393248 | tf_op jit(solution)/shard_map/ppermute | solution.py:479
  205.2 9.6 %fusion.10.cot_ref = bf16[1536,1536]{1,0:T(8,128)(2,1)} fusion(bf16[1,1536,1536]{2,1,0:T(8,128)(2,1)S(1)} %bitcast.93, s32[1536]{0:T(1024)S(1)} %concatenate.63), kind=kOutput, calls=%fused_computation.11 | convolution fusion | flops 7252475904 | bytes 9443328 | tf_op jit(solution)/shard_map/dot_general | solution.py:20
  229.8 24.3 %feed.3 = (bf16[1536,1536]{1,0:T(8,128)(2,1)}, bf16[1536,1024]{1,0:T(8,128)(2,1)}, bf16[1536,2048]{1,0:T(8,128)(2,1)}, bf16[1536,1536]{1,0:T(8,128)(2,1)}, bf16[...) custom-call(s32[1]{0:T(128)} %bitcast.at_ref, ...), custom_call_target="tpu_custom_call" | custom-call | flops 14495514624 | bytes 30000000 | tf_op jit(solution)/shard_map/feed/pallas_call | solution.py:273
  254.8 24.7 %feed.4 = (bf16[1536,1536]{1,0:T(8,128)(2,1)}, bf16[1536,1024]{1,0:T(8,128)(2,1)}, bf16[1536,2048]{1,0:T(8,128)(2,1)}, bf16[1536,1536]{1,0:T(8,128)(2,1)}, bf16[...) custom-call(s32[1]{0:T(128)} %bitcast.at_ref, ...), custom_call_target="tpu_custom_call", output_to_operand_aliasing={{0}: (12, {}), {1}: (13, {}), {2}: (14, {}), {3}: (15, {}),... | custom-call | flops 14495514624 | bytes 30000000 | tf_op jit(solution)/shard_map/feed/pallas_call | solution.py:273
  280.3 24.4 %feed.5 = (bf16[1536,1536]{1,0:T(8,128)(2,1)}, bf16[1536,1024]{1,0:T(8,128)(2,1)}, bf16[1536,2048]{1,0:T(8,128)(2,1)}, bf16[1536,1536]{1,0:T(8,128)(2,1)}, bf16[...) custom-call(s32[1]{0:T(128)} %bitcast.at_ref, ...), custom_call_target="tpu_custom_call", output_to_operand_aliasing={{0}: (12, {}), {1}: (13, {}), {2}: (14, {}), {3}: (15, {}),... | custom-call | flops 14495514624 | bytes 30000000 | tf_op jit(solution)/shard_map/feed/pallas_call | solution.py:273
  304.7 9.3 %convolution_convert_fusion.3 = bf16[768,2048]{1,0:T(8,128)(2,1)} fusion(bf16[1536,2048]{1,0:T(8,128)(2,1)} %get-tuple-element.128, bf16[1536,1536]{1,0:T(8,128)(2,1)} %get-tuple-element.127), kind=kOutput, calls=%fused_computation.29 | convolution fusion | flops 4833411072 | bytes 11796480 | tf_op jit(solution)/shard_map/dot_general | solution.py:20
  345.3 8.2 %collective-permute-done.30 = bf16[512,384]{1,0:T(8,128)(2,1)S(1)} collective-permute-done((bf16[512,384]{1,0:T(8,128)(2,1)S(1)}, bf16[512,384]{1,0:T(8,128)(2,1)S(1)}, u32[]{:S(2)}, u32[]{:S(2)}) %collective-permute-start.30) | collective-permute-done | bytes 393248 | tf_op jit(solution)/shard_map/ppermute | solution.py:479
  395.8 8.3 %collective-permute-done.32 = bf16[512,384]{1,0:T(8,128)(2,1)S(1)} collective-permute-done((bf16[512,384]{1,0:T(8,128)(2,1)S(1)}, bf16[512,384]{1,0:T(8,128)(2,1)S(1)}, u32[]{:S(2)}, u32[]{:S(2)}) %collective-permute-start.32) | collective-permute-done | bytes 393248 | tf_op jit(solution)/shard_map/ppermute | solution.py:479
  412.0 32.6 %attend_back.1 = (f32[1536,384]{1,0:T(8,128)}, f32[1536,384]{1,0:T(8,128)}, f32[1536,384]{1,0:T(8,128)}, f32[1536,128]{1,0:T(8,128)}) custom-call(bf16[1536,384]{1,0:T(8,128)(2,1)} %get-tuple-element.80.q_ref, bf16[1536,128]{1,0:T(8,128)(2,1)} %get-tuple-element.81.aq_ref, bf16[1536,384]{1,0:T(8,128)(2,1)} %get-tuple-element.82.k_ref, ...), custom_call_target="tpu_custom_call" | custom-call | flops 18119393280 | bytes 25000000 | tf_op jit(solution)/shard_map/attend_back/pallas_call | solution.py:354
  444.6 25.3 %post.1 = (bf16[1536,1664]{1,0:T(8,128)(2,1)}, bf16[1536,1536]{1,0:T(8,128)(2,1)}, f32[8,1536]{1,0:T(8,128)}, f32[8,384]{1,0:T(8,128)}, f32[8,128]{1,0:T(8,128)}) custom-call(f32[1536,384]{1,0:T(8,128)} %get-tuple-element.113.dq_ref, f32[1536,384]{1,0:T(8,128)} %get-tuple-element.114.dk_ref, f32[1536,384]{1,0:T(8,128)} %get-tuple-element.115.dv_ref, ...), custom_call_target="tpu_custom_call" | custom-call | flops 7851737088 | bytes 40000000 | tf_op jit(solution)/shard_map/post/pallas_call | solution.py:454
  484.0 8.5 %convolution_convert_fusion.4 = bf16[768,1664]{1,0:T(8,128)(2,1)} fusion(bf16[1536,1664]{1,0:T(8,128)(2,1)} %get-tuple-element.125, bf16[1536,1536]{1,0:T(8,128)(2,1)S(1)} %bitcast.99), kind=kOutput, calls=%fused_computation.30 | convolution fusion | flops 3927146496 | bytes 10027008 | tf_op jit(solution)/shard_map/dot_general | solution.py:20
  526.5 21.2 %collective-permute-done.39 = bf16[384,1536]{1,0:T(8,128)(2,1)S(1)} collective-permute-done((bf16[384,1536]{1,0:T(8,128)(2,1)}, bf16[384,1536]{1,0:T(8,128)(2,1)S(1)}, u32[]{:S(2)}, u32[]{:S(2)}) %collective-permute-start.39) | collective-permute-done | bytes 1179680 | tf_op jit(solution)/shard_map/ppermute | solution.py:479
  574.3 27.0 %collective-permute-done.52 = bf16[192,384]{1,0:T(8,128)(2,1)S(1)} collective-permute-done((bf16[192,384]{1,0:T(8,128)(2,1)S(1)}, bf16[192,384]{1,0:T(8,128)(2,1)S(1)}, u32[]{:S(2)}, u32[]{:S(2)}) %collective-permute-start.52) | collective-permute-done | bytes 147488 | tf_op jit(solution)/shard_map/ppermute | solution.py:479
  604.2 29.9 %collective-permute-done.53 = bf16[192,384]{1,0:T(8,128)(2,1)S(1)} collective-permute-done((bf16[192,384]{1,0:T(8,128)(2,1)S(1)}, bf16[192,384]{1,0:T(8,128)(2,1)S(1)}, u32[]{:S(2)}, u32[]{:S(2)}) %collective-permute-start.53) | collective-permute-done | bytes 147488 | tf_op jit(solution)/shard_map/ppermute | solution.py:479
  646.5 12.9 %collective-permute-done.43 = bf16[96,1664]{1,0:T(8,128)(2,1)S(1)} collective-permute-done((bf16[96,1664]{1,0:T(8,128)(2,1)S(1)}, bf16[96,1664]{1,0:T(8,128)(2,1)S(1)}, u32[]{:S(2)}, u32[]{:S(2)}) %collective-permute-start.43) | collective-permute-done | bytes 319520 | tf_op jit(solution)/shard_map/ppermute | solution.py:474
  664.4 9.8 %collective-permute-done.44 = bf16[192,1664]{1,0:T(8,128)(2,1)S(1)} collective-permute-done((bf16[192,1664]{1,0:T(8,128)(2,1)S(1)}, bf16[192,1664]{1,0:T(8,128)(2,1)S(1)}, u32[]{:S(2)}, u32[]{:S(2)}) %collective-permute-start.44) | collective-permute-done | bytes 639008 | tf_op jit(solution)/shard_map/ppermute | solution.py:474
  677.7 21.3 %collective-permute-done.38 = bf16[384,1536]{1,0:T(8,128)(2,1)} collective-permute-done((bf16[384,1536]{1,0:T(8,128)(2,1)S(1)}, bf16[384,1536]{1,0:T(8,128)(2,1)}, u32[]{:S(2)}, u32[]{:S(2)}) %collective-permute-start.38) | collective-permute-done | bytes 1179680 | tf_op jit(solution)/shard_map/ppermute | solution.py:479
  (355 shorter events, 302.3 us)
Async XLA Ops:
  80.8 28.0 %collective-permute-start.13 = (bf16[192,3072]{1,0:T(8,128)(2,1)S(1)}, bf16[192,3072]{1,0:T(8,128)(2,1)S(1)}, u32[]{:S(2)}, u32[]{:S(2)}) collective-permute-start(bf16[192,3072]{1,0:T(8,128)(2,1)S(1)} %pad_maximum_fusion.1), channel_id=1, source_target_pairs={{0,8},{4,12},{8,0},{12,4},{16,24},{20,28},{24,16},{28,20},{1,9},{5... | collective-permute-start | bytes 3538952 | tf_op jit(solution)/shard_map/ppermute | solution.py:474
  82.2 28.0 %collective-permute-start.14 = (bf16[192,3072]{1,0:T(8,128)(2,1)S(1)}, bf16[192,3072]{1,0:T(8,128)(2,1)S(1)}, u32[]{:S(2)}, u32[]{:S(2)}) collective-permute-start(bf16[192,3072]{1,0:T(8,128)(2,1)S(1)} %pad_maximum_fusion.1), channel_id=1, source_target_pairs={{0,16},{4,20},{8,24},{12,28},{16,0},{20,4},{24,8},{28,12},{1,17},{... | collective-permute-start | bytes 3538952 | tf_op jit(solution)/shard_map/ppermute | solution.py:474
  125.8 104.0 %collective-permute-start.17 = (bf16[768,3072]{1,0:T(8,128)(2,1)}, bf16[768,3072]{1,0:T(8,128)(2,1)}, u32[]{:S(2)}, u32[]{:S(2)}) collective-permute-start(bf16[768,3072]{1,0:T(8,128)(2,1)} %constant_dynamic-update-slice_fusion.10.fe_ref), channel_id=1, source_target_pairs={{0,4},{4,0},{8,12},{12,8},{16,20},{20,16},{24,28},{28,24},{1,5},{5... | collective-permute-start | bytes 14155784 | tf_op jit(solution)/shard_map/ppermute | solution.py:474
  186.9 27.8 %collective-permute-start.22 = (bf16[512,384]{1,0:T(8,128)(2,1)S(1)}, bf16[512,384]{1,0:T(8,128)(2,1)}, u32[]{:S(2)}, u32[]{:S(2)}) collective-permute-start(bf16[512,384]{1,0:T(8,128)(2,1)S(1)} %collective-permute-done.21.refs_1_), channel_id=1, source_target_pairs={{0,1},{1,2},{2,3},{3,0},{4,5},{5,6},{6,7},{7,4},{8,9},{9,10},{10,1... | collective-permute-start | bytes 1179656 | tf_op jit(solution)/shard_map/ppermute | solution.py:479
  204.5 25.3 %collective-permute-start.26 = (bf16[512,384]{1,0:T(8,128)(2,1)}, bf16[512,384]{1,0:T(8,128)(2,1)}, u32[]{:S(2)}, u32[]{:S(2)}) collective-permute-start(bf16[512,384]{1,0:T(8,128)(2,1)} %collective-permute-done.25.refs_2_), channel_id=1, source_target_pairs={{0,1},{1,2},{2,3},{3,0},{4,5},{5,6},{6,7},{7,4},{8,9},{9,10},{10,1... | collective-permute-start | bytes 1179656 | tf_op jit(solution)/shard_map/ppermute | solution.py:479
  214.7 39.3 %collective-permute-start.23 = (bf16[512,384]{1,0:T(8,128)(2,1)}, bf16[512,384]{1,0:T(8,128)(2,1)S(1)}, u32[]{:S(2)}, u32[]{:S(2)}) collective-permute-start(bf16[512,384]{1,0:T(8,128)(2,1)} %collective-permute-done.22.refs_2_), channel_id=1, source_target_pairs={{0,1},{1,2},{2,3},{3,0},{4,5},{5,6},{6,7},{7,4},{8,9},{9,10},{10,1... | collective-permute-start | bytes 1179656 | tf_op jit(solution)/shard_map/ppermute | solution.py:479
  221.2 58.3 %collective-permute-start.20 = (bf16[512,384]{1,0:T(8,128)(2,1)S(1)}, bf16[512,384]{1,0:T(8,128)(2,1)S(1)}, u32[]{:S(2)}, u32[]{:S(2)}) collective-permute-start(bf16[512,384]{1,0:T(8,128)(2,1)S(1)} %collective-permute-done.19.refs_2_), channel_id=1, source_target_pairs={{0,1},{1,2},{2,3},{3,0},{4,5},{5,6},{6,7},{7,4},{8,9},{9,10},{10,1... | collective-permute-start | bytes 1179656 | tf_op jit(solution)/shard_map/ppermute | solution.py:479
  334.6 27.4 %collective-permute-start.33 = (bf16[512,384]{1,0:T(8,128)(2,1)S(1)}, bf16[512,384]{1,0:T(8,128)(2,1)S(1)}, u32[]{:S(2)}, u32[]{:S(2)}) collective-permute-start(bf16[512,384]{1,0:T(8,128)(2,1)S(1)} %slice.273), channel_id=1, source_target_pairs={{0,1},{1,2},{2,3},{3,0},{4,5},{5,6},{6,7},{7,4},{8,9},{9,10},{10,1... | collective-permute-start | bytes 1179656 | tf_op jit(solution)/shard_map/ppermute | solution.py:479
  337.3 155.2 %collective-permute-start.60 = (bf16[768,1024]{1,0:T(8,128)(2,1)S(1)}, bf16[768,1024]{1,0:T(8,128)(2,1)S(1)}, u32[]{:S(2)}, u32[]{:S(2)}) collective-permute-start(bf16[768,1024]{1,0:T(8,128)(2,1)S(1)} %fusion.41), channel_id=1, source_target_pairs={{0,4},{4,0},{8,12},{12,8},{16,20},{20,16},{24,28},{28,24},{1,5},{5... | collective-permute-start | bytes 4718600 | tf_op jit(solution)/shard_map/ppermute | solution.py:474
  482.9 75.2 %collective-permute-start.55 = (bf16[768,2048]{1,0:T(8,128)(2,1)}, bf16[768,2048]{1,0:T(8,128)(2,1)}, u32[]{:S(2)}, u32[]{:S(2)}) collective-permute-start(bf16[768,2048]{1,0:T(8,128)(2,1)} %convolution_convert_fusion.2), channel_id=1, source_target_pairs={{0,4},{4,0},{8,12},{12,8},{16,20},{20,16},{24,28},{28,24},{1,5},{5... | collective-permute-start | bytes 9437192 | tf_op jit(solution)/shard_map/ppermute | solution.py:474
  483.0 39.2 %collective-permute-start.47 = (bf16[768,1536]{1,0:T(8,128)(2,1)}, bf16[768,1536]{1,0:T(8,128)(2,1)}, u32[]{:S(2)}, u32[]{:S(2)}) collective-permute-start(bf16[768,1536]{1,0:T(8,128)(2,1)} %convolution_convert_fusion), channel_id=1, source_target_pairs={{0,4},{4,0},{8,12},{12,8},{16,20},{20,16},{24,28},{28,24},{1,5},{5... | collective-permute-start | bytes 7077896 | tf_op jit(solution)/shard_map/ppermute | solution.py:474
  512.4 123.4 %collective-permute-start.42 = (bf16[768,1664]{1,0:T(8,128)(2,1)}, bf16[768,1664]{1,0:T(8,128)(2,1)}, u32[]{:S(2)}, u32[]{:S(2)}) collective-permute-start(bf16[768,1664]{1,0:T(8,128)(2,1)} %convolution_convert_fusion.4), channel_id=1, source_target_pairs={{0,4},{4,0},{8,12},{12,8},{16,20},{20,16},{24,28},{28,24},{1,5},{5... | collective-permute-start | bytes 7667720 | tf_op jit(solution)/shard_map/ppermute | solution.py:474
  516.7 31.1 %collective-permute-start.39 = (bf16[384,1536]{1,0:T(8,128)(2,1)}, bf16[384,1536]{1,0:T(8,128)(2,1)S(1)}, u32[]{:S(2)}, u32[]{:S(2)}) collective-permute-start(bf16[384,1536]{1,0:T(8,128)(2,1)} %constant_dynamic-slice_fusion), channel_id=1, source_target_pairs={{0,1},{1,2},{2,3},{3,0},{4,5},{5,6},{6,7},{7,4},{8,9},{9,10},{10,1... | collective-permute-start | bytes 3538952 | tf_op jit(solution)/shard_map/ppermute | solution.py:479
  518.3 55.5 %collective-permute-start.36 = (bf16[384,1536]{1,0:T(8,128)(2,1)S(1)}, bf16[384,1536]{1,0:T(8,128)(2,1)S(1)}, u32[]{:S(2)}, u32[]{:S(2)}) collective-permute-start(bf16[384,1536]{1,0:T(8,128)(2,1)S(1)} %constant_dynamic-slice_fusion.1), channel_id=1, source_target_pairs={{0,1},{1,2},{2,3},{3,0},{4,5},{5,6},{6,7},{7,4},{8,9},{9,10},{10,1... | collective-permute-start | bytes 3538952 | tf_op jit(solution)/shard_map/ppermute | solution.py:479
  549.5 85.7 %collective-permute-start.40 = (bf16[384,1536]{1,0:T(8,128)(2,1)S(1)}, bf16[384,1536]{1,0:T(8,128)(2,1)S(1)}, u32[]{:S(2)}, u32[]{:S(2)}) collective-permute-start(bf16[384,1536]{1,0:T(8,128)(2,1)S(1)} %add_convert_fusion.5), channel_id=1, source_target_pairs={{0,1},{1,2},{2,3},{3,0},{4,5},{5,6},{6,7},{7,4},{8,9},{9,10},{10,1... | collective-permute-start | bytes 3538952 | tf_op jit(solution)/shard_map/ppermute | solution.py:479
  570.8 30.6 %collective-permute-start.56 = (bf16[96,2048]{1,0:T(8,128)(2,1)S(1)}, bf16[96,2048]{1,0:T(8,128)(2,1)S(1)}, u32[]{:S(2)}, u32[]{:S(2)}) collective-permute-start(bf16[96,2048]{1,0:T(8,128)(2,1)S(1)} %get-tuple-element.139), channel_id=1, source_target_pairs={{0,16},{4,20},{8,24},{12,28},{16,0},{20,4},{24,8},{28,12},{1,17},{... | collective-permute-start | bytes 1179656 | tf_op jit(solution)/shard_map/ppermute | solution.py:474
  572.7 29.6 %collective-permute-start.58 = (bf16[96,2048]{1,0:T(8,128)(2,1)S(1)}, bf16[96,2048]{1,0:T(8,128)(2,1)S(1)}, u32[]{:S(2)}, u32[]{:S(2)}) collective-permute-start(bf16[96,2048]{1,0:T(8,128)(2,1)S(1)} %get-tuple-element.138), channel_id=1, source_target_pairs={{0,8},{4,12},{8,0},{12,4},{16,24},{20,28},{24,16},{28,20},{1,9},{5... | collective-permute-start | bytes 1179656 | tf_op jit(solution)/shard_map/ppermute | solution.py:474
  573.9 27.4 %collective-permute-start.52 = (bf16[192,384]{1,0:T(8,128)(2,1)S(1)}, bf16[192,384]{1,0:T(8,128)(2,1)S(1)}, u32[]{:S(2)}, u32[]{:S(2)}) collective-permute-start(bf16[192,384]{1,0:T(8,128)(2,1)S(1)} %slice.353), channel_id=1, source_target_pairs={{0,1},{1,2},{2,3},{3,0},{4,5},{5,6},{6,7},{7,4},{8,9},{9,10},{10,1... | collective-permute-start | bytes 442376 | tf_op jit(solution)/shard_map/ppermute | solution.py:479
  601.3 42.7 %collective-permute-start.37 = (bf16[384,1536]{1,0:T(8,128)(2,1)S(1)}, bf16[384,1536]{1,0:T(8,128)(2,1)S(1)}, u32[]{:S(2)}, u32[]{:S(2)}) collective-permute-start(bf16[384,1536]{1,0:T(8,128)(2,1)S(1)} %add_convert_fusion.8), channel_id=1, source_target_pairs={{0,1},{1,2},{2,3},{3,0},{4,5},{5,6},{6,7},{7,4},{8,9},{9,10},{10,1... | collective-permute-start | bytes 3538952 | tf_op jit(solution)/shard_map/ppermute | solution.py:479
  601.4 32.7 %collective-permute-start.53 = (bf16[192,384]{1,0:T(8,128)(2,1)S(1)}, bf16[192,384]{1,0:T(8,128)(2,1)S(1)}, u32[]{:S(2)}, u32[]{:S(2)}) collective-permute-start(bf16[192,384]{1,0:T(8,128)(2,1)S(1)} %add_convert_fusion.29), channel_id=1, source_target_pairs={{0,1},{1,2},{2,3},{3,0},{4,5},{5,6},{6,7},{7,4},{8,9},{9,10},{10,1... | collective-permute-start | bytes 442376 | tf_op jit(solution)/shard_map/ppermute | solution.py:479
  602.6 58.6 %collective-permute-start.57 = (bf16[192,2048]{1,0:T(8,128)(2,1)S(1)}, bf16[192,2048]{1,0:T(8,128)(2,1)S(1)}, u32[]{:S(2)}, u32[]{:S(2)}) collective-permute-start(bf16[192,2048]{1,0:T(8,128)(2,1)S(1)} %pad_maximum_fusion.3), channel_id=1, source_target_pairs={{0,8},{4,12},{8,0},{12,4},{16,24},{20,28},{24,16},{28,20},{1,9},{5... | collective-permute-start | bytes 2359304 | tf_op jit(solution)/shard_map/ppermute | solution.py:474
  634.1 28.6 %collective-permute-start.59 = (bf16[192,2048]{1,0:T(8,128)(2,1)S(1)}, bf16[192,2048]{1,0:T(8,128)(2,1)S(1)}, u32[]{:S(2)}, u32[]{:S(2)}) collective-permute-start(bf16[192,2048]{1,0:T(8,128)(2,1)S(1)} %pad_maximum_fusion.4), channel_id=1, source_target_pairs={{0,16},{4,20},{8,24},{12,28},{16,0},{20,4},{24,8},{28,12},{1,17},{... | collective-permute-start | bytes 2359304 | tf_op jit(solution)/shard_map/ppermute | solution.py:474
  645.7 58.3 %collective-permute-start.41 = (bf16[384,1536]{1,0:T(8,128)(2,1)S(1)}, bf16[384,1536]{1,0:T(8,128)(2,1)}, u32[]{:S(2)}, u32[]{:S(2)}) collective-permute-start(bf16[384,1536]{1,0:T(8,128)(2,1)S(1)} %add_convert_fusion.4), channel_id=1, source_target_pairs={{0,1},{1,2},{2,3},{3,0},{4,5},{5,6},{6,7},{7,4},{8,9},{9,10},{10,1... | collective-permute-start | bytes 3538952 | tf_op jit(solution)/shard_map/ppermute | solution.py:479
  659.4 39.6 %collective-permute-start.38 = (bf16[384,1536]{1,0:T(8,128)(2,1)S(1)}, bf16[384,1536]{1,0:T(8,128)(2,1)}, u32[]{:S(2)}, u32[]{:S(2)}) collective-permute-start(bf16[384,1536]{1,0:T(8,128)(2,1)S(1)} %add_convert_fusion.7), channel_id=1, source_target_pairs={{0,1},{1,2},{2,3},{3,0},{4,5},{5,6},{6,7},{7,4},{8,9},{9,10},{10,1... | collective-permute-start | bytes 3538952 | tf_op jit(solution)/shard_map/ppermute | solution.py:479
  (91 other events, 1789.4 us)

commit v2 on v1

v2 whole, which is shorter than its diff:
```python
import functools

import jax
import jax.numpy as jnp
import numpy as np
from jax import lax
from jax.experimental import pallas as pl
from jax.experimental.pallas import tpu as pltpu
from jax.sharding import PartitionSpec as P

EPS = 1e-06
BF = jnp.bfloat16
F32 = jnp.float32
VMEM_LIMIT = 58 * 1024 * 1024
NT = (((1,), (1,)), ((), ()))
TN = (((0,), (0,)), ((), ()))


COST = pl.CostEstimate(flops=1, bytes_accessed=1, transcendentals=0)


def dot(a, b, dims=(((1,), (0,)), ((), ()))):
    return lax.dot_general(a, b, dims, preferred_element_type=F32)


def params():
    return pltpu.CompilerParams(vmem_limit_bytes=VMEM_LIMIT)


def split2(v):
    hi = v.astype(BF)
    return hi, (v - hi.astype(F32)).astype(BF)


def split3(v):
    hi = v.astype(BF)
    rest = v - hi.astype(F32)
    mid = rest.astype(BF)
    return hi, mid, (rest - mid.astype(F32)).astype(BF)


def lanes(shape):
    return lax.broadcasted_iota(jnp.int32, shape, len(shape) - 1)


def rows_of(shape):
    return lax.broadcasted_iota(jnp.int32, shape, 0)


def const(array, dtype=BF):
    return jnp.asarray(array.astype(np.float32), dtype)


def full(shape):
    return pl.BlockSpec(shape, lambda *_: tuple(0 for _ in shape), pipeline_mode=pl.Buffered(1))


ANY = pl.BlockSpec(memory_space=pl.ANY)
SMEM = pl.BlockSpec(memory_space=pltpu.SMEM)


def pre_kernel(
    heads, spots, me_ref, x_ref, ba_ref, g64_ref, tri_ref, mq_ref, mk_ref, rows_ref, gqk_ref, *refs,
):
    pieces, refs = refs[: len(spots)], refs[len(spots) :]
    (hn_ref, w_ref, gain_ref, q8_ref, kn_ref, vl_ref, aq_ref, ak_ref, og_ref, q_ref, ks_ref, kd_ref, vd_ref, lg_ref,
     gain_s, carry_k, carry_v, carry_c, sems) = refs
    step = pl.program_id(0)
    width = q8_ref.shape[1]
    wide = 4 * width

    @pl.when(step == 0)
    def _():
        copies = []
        for i, (far, start, count, cut) in enumerate(spots):
            row = pl.multiple_of((me_ref[0] ^ far) * cut + start, 16)
            copies.append(pltpu.make_async_copy(pieces[i], w_ref.at[pl.ds(row, count), :], sems.at[i]))
        for copy in copies:
            copy.start()
        for copy in copies:
            copy.wait()
        pick = (lanes((8, 128)) == 3 * heads + rows_of((8, 128))).astype(F32)
        pick = jnp.where(rows_of((8, 128)) < 2, pick, 0.0).astype(BF)
        gain_s[...] = dot(pick, w_ref[:, wide:], NT)
        carry_k[...] = jnp.zeros_like(carry_k)
        carry_v[...] = jnp.zeros_like(carry_v)
        carry_c[...] = jnp.zeros_like(carry_c)
        gain_ref[...] = gain_s[...]

    x = x_ref[...].astype(F32)
    factor = lax.rsqrt(jnp.mean(x * x, -1, keepdims=True) + EPS)
    hn = (x * factor * gain_s[0:1, :]).astype(BF)
    hn_ref[...] = hn
    proj = dot(hn, w_ref[...])
    q = proj[:, :width]
    k = proj[:, width : 2 * width]
    v = proj[:, 2 * width : 3 * width]
    og_ref[...] = jax.nn.sigmoid(proj[:, 3 * width : wide])
    logits = proj[:, wide:]
    lg_ref[...] = logits
    mix = dot(jnp.concatenate(split2(jax.nn.sigmoid(logits)), 1), ba_ref[...])
    first = rows_of(k.shape) == 0
    kd = jnp.where(first, carry_k[0:1, :], pltpu.roll(k, 1, 0)) - k
    vd = jnp.where(first, carry_v[0:1, :], pltpu.roll(v, 1, 0)) - v
    last = k.shape[0] - 1
    carry_k[0:1, :] = k[last:, :]
    carry_v[0:1, :] = v[last:, :]
    ks = k + mix[:, :width] * kd
    vl_ref[...] = (v + mix[:, width:] * vd).astype(BF)
    q_ref[...] = q.astype(BF)
    ks_ref[...] = ks.astype(BF)
    kd_ref[...] = kd.astype(BF)
    vd_ref[...] = vd.astype(BF)
    rq = lax.rsqrt(dot((q * q).astype(BF), g64_ref[...]) + EPS)
    rk = lax.rsqrt(dot((ks * ks).astype(BF), g64_ref[...]) + EPS)
    q8_ref[...] = ((q * rq * gqk_ref[0:1, :]).astype(BF).astype(F32) * 0.125).astype(BF)
    kn_ref[...] = (ks * rk * gqk_ref[1:2, :]).astype(BF)
    z = logits + rows_ref[0:1, :]
    ls = jnp.minimum(z, 0.0) - jnp.log1p(jnp.exp(-jnp.abs(z)))
    sums = dot(tri_ref[...], jnp.concatenate(split3(ls), 1))
    cum = sums[:, :128] + sums[:, 128:256] + sums[:, 256:] + carry_c[0:1, :]
    carry_c[0:1, :] = cum[last:, :]
    parts = jnp.concatenate(split3(cum), 1)
    aq_ref[...] = (dot(parts, mq_ref[...]) + rows_ref[1:2, :]).astype(BF)
    ak_ref[...] = (dot(parts, mk_ref[...]) + rows_ref[2:3, :]).astype(BF)


def pre(x, place, pieces, bias_row, gqk, heads):
    seq, model = x.shape
    cut = pieces[0, 0].shape[0]
    spots = [(far, start, p.shape[0], cut) for (far, start), p in sorted(pieces.items())]
    wide = pieces[0, 0].shape[1]
    width = (wide - 128) // 4
    block = min(256, seq)
    ba = np.zeros((256, 2 * width))
    for lane in range(2 * width):
        head = (lane % width) // 64 + (lane // width) * heads
        ba[head, lane] = ba[128 + head, lane] = 1.0
    g64 = np.kron(np.eye(width // 64), np.full((64, 64), 1 / 64))
    tri = np.tril(np.ones((block, block)))
    mq, mk = np.zeros((384, 128)), np.zeros((384, 128))
    ones_q, ones_k = np.zeros((1, 128)), np.zeros((1, 128))
    for head in range(heads):
        for piece in range(3):
            mq[128 * piece + 2 * heads + head, 6 * head + piece] = 1.0
            mk[128 * piece + 2 * heads + head, 6 * head + 3 + piece] = -1.0
            ones_q[0, 6 * head + 3 + piece] = 1.0
            ones_k[0, 6 * head + piece] = 1.0
    rows = jnp.concatenate([bias_row, const(ones_q, F32), const(ones_k, F32), jnp.zeros((5, 128), F32)], 0)

    def row(cols):
        return pl.BlockSpec((block, cols), lambda i: (i, 0))

    def shape(cols, dtype):
        return jax.ShapeDtypeStruct((seq, cols), dtype)

    return pl.pallas_call(
        functools.partial(pre_kernel, heads, spots),
        grid=(seq // block,),
        in_specs=[SMEM, row(model), full(ba.shape), full(g64.shape), full(tri.shape), full(mq.shape), full(mk.shape),
                  full((8, 128)), full(gqk.shape)] + [ANY] * len(spots),
        out_specs=[row(model), full((model, wide)), full((8, model))] + [row(width)] * 3 + [row(128)] * 2 + [row(width)] * 5 + [row(128)],
        out_shape=[shape(model, BF), jax.ShapeDtypeStruct((model, wide), BF), jax.ShapeDtypeStruct((8, model), F32)]
        + [shape(width, BF)] * 3
        + [shape(128, BF)] * 2 + [shape(width, F32)] + [shape(width, BF)] * 4 + [shape(128, F32)],
        scratch_shapes=[pltpu.VMEM((8, model), F32), pltpu.VMEM((8, width), F32), pltpu.VMEM((8, width), F32),
                        pltpu.VMEM((8, 128), F32), pltpu.SemaphoreType.DMA((len(spots),))],
        compiler_params=params(),
        cost_estimate=COST,
        name="pre",
    )(place, x, const(ba), const(g64), const(tri), const(mq), const(mk), rows, gqk,
      *[p for _, p in sorted(pieces.items())])


def fwd_kernel(chunk, block, q_ref, aq_ref, k_ref, ak_ref, v_ref, og_ref, *refs):
    u_ref, att_ref, li_ref = refs[-3:]
    pair = pl.program_id(0)
    q, aq = q_ref[...], aq_ref[...]
    lane = lanes(q.shape)
    ones = jnp.ones((block, 128), BF)
    out = []
    for side in range(2):
        head = 2 * pair + side
        mine = (lane >= 64 * side) & (lane < 64 * side + 64)
        aug = (lane >= 6 * head) & (lane < 6 * head + 6)
        zero = jnp.zeros_like(q)
        qa = jnp.concatenate([jnp.where(mine, q, zero), jnp.where(aug, aq, zero)], 1)
        acc = jnp.zeros((block, 256), F32)
        for j in range(chunk + 1):
            at = slice(j * block, (j + 1) * block)
            e = jnp.exp(dot(qa, jnp.concatenate([k_ref[at, :], ak_ref[at, :]], 1), NT))
            if j == chunk:
                e = jnp.where(rows_of(e.shape) >= lanes(e.shape), e, 0.0)
            acc = acc + dot(e.astype(BF), jnp.concatenate([v_ref[at, :], ones], 1))
        out.append(acc)
    low = lane < 64
    total = jnp.where(low, out[0][:, 128:], out[1][:, 128:])
    inverse = 1.0 / total
    att = jnp.where(low, out[0][:, :128], out[1][:, :128]) * inverse
    u_ref[...] = (att * og_ref[...]).astype(BF)
    att_ref[...] = att
    li_ref[...] = inverse


def attend(chunk, block, q8, aq, kn, ak, vl, og, kept):
    seq, width = q8.shape
    keys = (chunk + 1) * block
    grid = (width // 128,)
    mine = pl.BlockSpec((block, 128), lambda p: (chunk, p))
    other = pl.BlockSpec((keys, 128), lambda p: (0, p))
    return pl.pallas_call(
        functools.partial(fwd_kernel, chunk, block),
        grid=grid,
        in_specs=[mine, pl.BlockSpec((block, 128), lambda p: (chunk, 0)), other,
                  pl.BlockSpec((keys, 128), lambda p: (0, 0)), other, mine] + [ANY] * len(kept),
        out_specs=[pl.BlockSpec((block, 128), lambda p: (0, p)), mine, mine],
        out_shape=[jax.ShapeDtypeStruct((block, width), BF)] + [jax.ShapeDtypeStruct((seq, width), F32)] * 2,
        input_output_aliases={6 + i: 1 + i for i in range(len(kept))},
        compiler_params=params(),
        cost_estimate=COST,
        name="attend",
    )(q8, aq, kn, ak, vl, og, *kept)


def ffn_kernel(
    count, chunk, block, step_rows, own, at_ref, x_ref, cot_ref, gain_ref, o_ref, f_ref, *refs
):
    us, outs = refs[:count], refs[-7 - count :]
    h2_ref, hid_ref, dgu_ref, res_ref, uc_ref, part_ref = outs[:6]
    dus, gmid_ref = outs[6:-1], outs[-1]
    hidden = hid_ref.shape[1]
    u = jnp.concatenate([r[...] for r in us], 1)
    uc_ref[...] = u
    x = x_ref[...].astype(F32)
    cot = cot_ref[...]
    y1 = x + dot(u, o_ref[...], NT)
    factor = lax.rsqrt(jnp.mean(y1 * y1, -1, keepdims=True) + EPS)
    n = y1 * factor
    gain = gain_ref[1:2, :]
    h2 = (n * gain).astype(BF)
    h2_ref[...] = h2
    gu = dot(h2, f_ref[:, : 2 * hidden])
    g, up = gu[:, :hidden], gu[:, hidden:]
    sg = jax.nn.sigmoid(g)
    act = g * sg
    hid = (act * up).astype(BF)
    hid_ref[...] = hid
    dhid = dot(cot, f_ref[:, 2 * hidden :])
    dg = dhid * up * sg * (1.0 + g * (1.0 - sg))
    dgu = jnp.concatenate([dg.astype(BF), (dhid * act).astype(BF)], 1)
    dgu_ref[...] = dgu
    part = dot(hid, f_ref[:, 2 * hidden :], NT)
    token = chunk * block + pl.program_id(0) * step_rows + rows_of((step_rows, 1))
    owned = (token >= at_ref[0] * own) & (token < (at_ref[0] + 1) * own)
    part_ref[...] = (part + jnp.where(owned, y1, 0.0)).astype(BF)
    dh2 = dot(dgu, f_ref[:, : 2 * hidden], NT)
    gmid = jnp.sum(dh2 * n, 0, keepdims=True)

    @pl.when(pl.program_id(0) == 0)
    def _():
        gmid_ref[...] = jnp.zeros_like(gmid_ref)

    gmid_ref[0:1, :] += gmid
    wd = gain * dh2
    res = factor * (wd - n * jnp.mean(wd * n, -1, keepdims=True))
    res = jnp.where(at_ref[0] == 0, res + cot.astype(F32), res).astype(BF)
    res_ref[...] = res
    du = dot(res, o_ref[...]).astype(BF)
    width = du.shape[1] // count
    for s in range(count):
        dus[s][...] = du[:, s * width : (s + 1) * width]


def feed(chunk, block, own, place, x, cot, gains, o, f, us, kept):
    seq, model = x.shape
    hidden = f.shape[1] // 3
    count = len(us)
    width = us[0].shape[1]
    step_rows = min(256, block)
    per = block // step_rows

    def mine(cols):
        return pl.BlockSpec((step_rows, cols), lambda i: (chunk * per + i, 0))

    def local(cols):
        return pl.BlockSpec((step_rows, cols), lambda i: (i, 0))

    kept_cols = [model, hidden, 2 * hidden, model, count * width, model]
    return pl.pallas_call(
        functools.partial(ffn_kernel, count, chunk, block, step_rows, own),
        grid=(per,),
        in_specs=[SMEM, mine(model), mine(model), full(gains.shape), full(o.shape), full(f.shape)]
        + [local(width)] * count + [ANY] * len(kept),
        out_specs=[mine(c) for c in kept_cols] + [local(width)] * count + [full((8, model))],
        out_shape=[jax.ShapeDtypeStruct((seq, c), BF) for c in kept_cols]
        + [jax.ShapeDtypeStruct((block, width), BF)] * count + [jax.ShapeDtypeStruct((8, model), F32)],
        input_output_aliases={6 + count + i: i for i in range(len(kept))},
        compiler_params=params(),
        cost_estimate=COST,
        name="feed",
    )(place, x, cot, gains, o, f, *us, *kept)


def bwd_kernel(
    pair, heads, block, q_ref, aq_ref, k_ref, ak_ref, v_ref, og_ref, att_ref, li_ref, du_ref, ms_ref,
    dq_ref, dk_ref, dv_ref, dc_ref, da_s, ad_s,
):
    seq = q_ref.shape[0]
    count = seq // block
    lane = lanes((block, 128))
    zero = jnp.zeros((block, 128), BF)
    ones = jnp.ones((block, 128), BF)
    third = lane - 3 * (lane // 3)
    for i in range(count):
        at = slice(i * block, (i + 1) * block)
        da = (du_ref[at, :].astype(F32) * og_ref[at, :] * li_ref[at, :]).astype(BF)
        da_s[at, :] = da
        delta = dot(jnp.concatenate(split2(da.astype(F32) * att_ref[at, :]), 1), ms_ref[...])
        hi, mid, rest = split3(-delta)
        ad_s[at, :] = jnp.where(third == 0, hi, jnp.where(third == 1, mid, rest))
    dk_ref[...] = jnp.zeros_like(dk_ref)
    dv_ref[...] = jnp.zeros_like(dv_ref)
    dc_ref[...] = jnp.zeros_like(dc_ref)

    vone = jnp.where(lane < 6, ones, zero)
    for i in range(count):
        at = slice(i * block, (i + 1) * block)
        q, aq, da, ad = q_ref[at, :], aq_ref[at, :], da_s[at, :], ad_s[at, :]
        dq = []
        for side in range(2):
            head = 2 * pair + side
            mine = (lane >= 64 * side) & (lane < 64 * side + 64)
            aug = (lane >= 6 * head) & (lane < 6 * head + 6)
            column = lane == 2 * heads + head
            qh = jnp.where(mine, q, zero)
            qa = jnp.concatenate([qh, jnp.where(aug, aq, zero)], 1)
            qo = jnp.concatenate([qh, ones], 1)
            dah = jnp.where(mine, da, zero)
            daa = jnp.concatenate([dah, jnp.where((lane >= 3 * side) & (lane < 3 * side + 3), ad, zero)], 1)
            acc = jnp.zeros((block, 256), F32)
            for j in range(i + 1):
                to = slice(j * block, (j + 1) * block)
                k = k_ref[to, :]
                e = jnp.exp(dot(jnp.concatenate([k, ak_ref[to, :]], 1), qa, NT))
                if j == i:
                    e = jnp.where(rows_of(e.shape) <= lanes(e.shape), e, 0.0)
                dv_ref[to, :] += dot(e.astype(BF), dah)
                ds = (e * dot(jnp.concatenate([v_ref[to, :], vone], 1), daa, NT)).astype(BF)
                dk = dot(ds, qo)
                dk_ref[to, :] += dk[:, :128]
                dc_ref[to, :] -= jnp.where(column, dk[:, 128:], 0.0)
                acc = acc + dot(ds, jnp.concatenate([k, ones], 1), TN)
            dq.append(acc[:, :128])
            dc_ref[at, :] += jnp.where(column, acc[:, 128:], 0.0)
        dq_ref[at, :] = jnp.where(lane < 64, dq[0], dq[1]) * 0.125


def attend_back(pair, block, heads, q8, aq, kn, ak, vl, og, att, li, du):
    seq, width = q8.shape
    ms = np.zeros((256, 128))
    for lane in range(256):
        ms[lane, 3 * ((lane % 128) // 64) : 3 * ((lane % 128) // 64) + 3] = 1.0
    mine = pl.BlockSpec((seq, 128), lambda p: (0, pair))
    one = pl.BlockSpec((seq, 128), lambda p: (0, 0))
    return pl.pallas_call(
        functools.partial(bwd_kernel, pair, heads, block),
        grid=(1,),
        in_specs=[mine, one, mine, one, mine, mine, mine, mine, mine, full((256, 128))],
        out_specs=[one] * 4,
        out_shape=[jax.ShapeDtypeStruct((seq, 128), F32)] * 4,
        scratch_shapes=[pltpu.VMEM((seq, 128), BF), pltpu.VMEM((seq, 128), BF)],
        compiler_params=params(),
        cost_estimate=COST,
        name="attend_back",
    )(q8, aq, kn, ak, vl, og, att, li, du, const(ms))


def post_kernel(
    heads, pairs, q_ref, ks_ref, kd_ref, vd_ref, lg_ref, du_ref, att_ref, og_ref, x_ref,
    res_ref, gain_ref, w_ref, ba_ref, g64_ref, tri_ref, ms_ref, rows_ref, gqk_ref, *refs,
):
    grads, refs = refs[: 4 * pairs], refs[4 * pairs :]
    dp_ref, gt_ref, g0_ref, gq_ref, gb_ref, carry_k, carry_v, carry_c = refs
    dq_raw, dk_raw, dvs = [
        jnp.concatenate([r[...] for r in grads[i * pairs : (i + 1) * pairs]], 1) for i in range(3)
    ]
    dc = sum(r[...] for r in grads[3 * pairs :])
    step = pl.program_id(0)
    rows, width = q_ref.shape

    @pl.when(step == 0)
    def _():
        carry_k[...] = jnp.zeros_like(carry_k)
        carry_v[...] = jnp.zeros_like(carry_v)
        carry_c[...] = jnp.zeros_like(carry_c)
        g0_ref[...] = jnp.zeros_like(g0_ref)
        gq_ref[...] = jnp.zeros_like(gq_ref)
        gb_ref[...] = jnp.zeros_like(gb_ref)

    def norm_back(raw, gain, grad):
        r = lax.rsqrt(dot((raw * raw).astype(BF), g64_ref[...]) + EPS)
        n = raw * r
        wd = grad * gain
        return r * (wd - n * dot((wd * n).astype(BF), g64_ref[...])), jnp.sum(grad * n, 0, keepdims=True)

    dq, gq = norm_back(q_ref[...].astype(F32), gqk_ref[0:1, :], dq_raw)
    dks, gk = norm_back(ks_ref[...].astype(F32), gqk_ref[1:2, :], dk_raw)
    gq_ref[0:1, :] += gq
    gq_ref[1:2, :] += gk
    logits = lg_ref[...]
    sg = jax.nn.sigmoid(logits)
    mix = dot(jnp.concatenate(split2(sg), 1), ba_ref[...])
    end = rows_of(dks.shape) == rows - 1

    def shift_back(grad, part, carry):
        w = part * grad
        later = jnp.where(end, carry[0:1, :], pltpu.roll(w, rows - 1, 0))
        carry[0:1, :] = w[0:1, :]
        return grad - w + later

    dk = shift_back(dks, mix[:, :width], carry_k)
    dv = shift_back(dvs, mix[:, width:], carry_v)
    terms = jnp.concatenate([dks * kd_ref[...].astype(F32), dvs * vd_ref[...].astype(F32)], 1)
    hi, rest = split2(terms)
    dmix = dot(hi, ms_ref[...]) + dot(rest, ms_ref[...])
    sums = dot(tri_ref[...], jnp.concatenate(split3(dc), 1))
    dls = sums[:, :128] + sums[:, 128:256] + sums[:, 256:] + carry_c[0:1, :]
    carry_c[0:1, :] = dls[0:1, :]
    lane = lanes(logits.shape)
    dz = dls * jax.nn.sigmoid(-(logits + rows_ref[0:1, :]))
    dgl = jnp.where(lane < 2 * heads, dmix * sg * (1.0 - sg), jnp.where(lane < 3 * heads, dz, 0.0))
    gb_ref[0:1, :] += jnp.sum(dgl, 0, keepdims=True)
    og = og_ref[...]
    do = du_ref[...].astype(F32) * att_ref[...] * og * (1.0 - og)
    dp = jnp.concatenate([dq.astype(BF), dk.astype(BF), dv.astype(BF), do.astype(BF), dgl.astype(BF)], 1)
    dp_ref[...] = dp
    dhn = dot(dp, w_ref[...], NT)
    x = x_ref[...].astype(F32)
    factor = lax.rsqrt(jnp.mean(x * x, -1, keepdims=True) + EPS)
    n = x * factor
    g0_ref[0:1, :] += jnp.sum(dhn * n, 0, keepdims=True)
    wd = dhn * gain_ref[0:1, :]
    back = factor * (wd - n * jnp.mean(wd * n, -1, keepdims=True))
    gt_ref[...] = (back + res_ref[...].astype(F32)).astype(BF)


def post(heads, dq, dk, dv, dc, q, ks, kd, vd, lg, du, att, og, x, res, gains, w, bias_row, gqk):
    seq, width = q.shape
    pairs = len(dq)
    model = x.shape[1]
    wide = w.shape[1]
    block = min(256, seq)
    count = seq // block
    ba = np.zeros((256, 2 * width))
    ms = np.zeros((2 * width, 128))
    for lane in range(2 * width):
        head = (lane % width) // 64 + (lane // width) * heads
        ba[head, lane] = ba[128 + head, lane] = 1.0
        ms[lane, head] = 1.0
    g64 = np.kron(np.eye(width // 64), np.full((64, 64), 1 / 64))
    tri = np.triu(np.ones((block, block)))
    rows = jnp.concatenate([bias_row, jnp.zeros((7, 128), F32)], 0)

    def row(cols):
        return pl.BlockSpec((block, cols), lambda i: (count - 1 - i, 0))

    return pl.pallas_call(
        functools.partial(post_kernel, heads, pairs),
        grid=(count,),
        in_specs=[row(width)] * 4 + [row(128)] + [row(width)] * 3 + [row(model)] * 2
        + [full(gains.shape), full(w.shape), full(ba.shape), full(g64.shape), full(tri.shape),
           full(ms.shape), full((8, 128)), full(gqk.shape)] + [row(128)] * (4 * pairs),
        out_specs=[row(wide), row(model), full((8, model)), full((8, width)), full((8, 128))],
        out_shape=[jax.ShapeDtypeStruct((seq, wide), BF), jax.ShapeDtypeStruct((seq, model), BF),
                   jax.ShapeDtypeStruct((8, model), F32), jax.ShapeDtypeStruct((8, width), F32),
                   jax.ShapeDtypeStruct((8, 128), F32)],
        scratch_shapes=[pltpu.VMEM((8, width), F32), pltpu.VMEM((8, width), F32), pltpu.VMEM((8, 128), F32)],
        compiler_params=params(),
        cost_estimate=COST,
        name="post",
    )(q, ks, kd, vd, lg, du, att, og, x, res, gains, w, const(ba), const(g64), const(tri),
      const(ms), rows, gqk, *dq, *dk, *dv, *dc)


def swap(value, axis, bit):
    size = lax.axis_size(axis)
    return lax.ppermute(value, axis, [(i, i ^ bit) for i in range(size)])


def turn(value):
    size = lax.axis_size("tp")
    return lax.ppermute(value, "tp", [(i, (i + 1) % size) for i in range(size)])


def add(a, b):
    return (a.astype(F32) + b.astype(F32)).astype(BF)


def high_bits(size):
    bits, bit = [], 2
    while bit < size:
        bits.append(bit)
        bit *= 2
    return bits


def gather_1(shard):
    pieces = {(0, 0): shard, (2, 0): swap(shard, "dp", 2)}
    if lax.axis_size("dp") == 8:
        pieces[4, 0] = swap(shard, "dp", 4)
    pieces[1, 0] = swap(shard, "dp", 1)
    return pieces


def gather_2(pieces):
    size = lax.axis_size("dp")
    pieces = dict(pieces)
    if size == 8:
        half = pieces[0, 0].shape[0] // 2
        pieces[6, 0] = swap(pieces[2, 0][:half], "dp", 4)
        pieces[6, half] = swap(pieces[4, 0][half:], "dp", 2)
        pieces[3, 0] = swap(pieces[2, 0], "dp", 1)
        pieces[5, 0] = swap(pieces[4, 0], "dp", 1)
        return pieces
    for bit in high_bits(size)[1:]:
        pieces.update({(r | bit, 0): swap(p, "dp", bit) for (r, _), p in list(pieces.items()) if not r & 1})
    return pieces


def gather_3(pieces):
    pieces = dict(pieces)
    pieces.update({(r | 1, s): swap(p, "dp", 1) for (r, s), p in list(pieces.items()) if (r | 1, s) not in pieces})
    return pieces


def assemble(pieces, me):
    cut, cols = pieces[0, 0].shape
    whole = jnp.zeros((cut * lax.axis_size("dp"), cols), BF)
    for (far, start), piece in sorted(pieces.items()):
        whole = lax.dynamic_update_slice_in_dim(whole, piece, (me ^ far) * cut + start, 0)
    return whole


def scatter(whole):
    return lax.psum_scatter(whole, "dp", scatter_dimension=0, tiled=True)


def total_of(terms):
    return sum(term.astype(F32) for term in terms)


tie = lax.optimization_barrier


def pad_to(value, size, axis):
    extra = size - value.shape[axis]
    if not extra:
        return value
    return jnp.pad(value, [(0, extra if a == axis else 0) for a in range(value.ndim)])


def shards(
    tokens, attn_in, head_gates, out_proj, norm_gains, qk_gains, forget_bias, gate_up, down_proj, carried_offset,
    reset_flag, cotangent,
):
    dp, tp = lax.axis_size("dp"), lax.axis_size("tp")
    me_d, me_t = lax.axis_index("dp"), lax.axis_index("tp")
    _, seq, model = tokens.shape
    own = seq // tp
    cut = attn_in.shape[1]
    width_real = attn_in.shape[2]
    heads_real = head_gates.shape[2]
    heads = heads_real + heads_real % 2
    width = 64 * heads
    hidden = gate_up.shape[2]
    block = 512 if seq % 512 == 0 else seq
    chunks = seq // block

    attn_rows = jnp.transpose(pad_to(attn_in, width, 2), (1, 0, 2)).reshape(cut, 4 * width)
    gate_rows = jnp.transpose(pad_to(head_gates, heads, 2), (1, 0, 2)).reshape(cut, 3 * heads)
    gate_rows = pad_to(jnp.concatenate([gate_rows, jnp.transpose(norm_gains)], 1), 128, 1)
    attn_rows = jnp.concatenate([attn_rows, gate_rows], 1)
    out_own = pad_to(jnp.transpose(out_proj), width, 1)
    ffn_rows = jnp.concatenate([gate_up[0], gate_up[1], jnp.transpose(down_proj)], 1)

    bias = lax.dynamic_slice_in_dim(forget_bias.astype(F32), me_t * heads_real, heads_real, 0)
    offset = lax.dynamic_slice_in_dim(carried_offset[0], me_t * heads_real, heads_real, 0)
    bias = bias + (1 - reset_flag[0]).astype(F32) * offset
    bias_row = jnp.pad(bias, (2 * heads, 128 - 2 * heads - heads_real))[None, :]
    gqk = pad_to(jnp.tile(qk_gains.astype(F32), (1, heads)), 8, 0)
    at = me_t.astype(jnp.int32)[None]

    here = me_d.astype(jnp.int32)[None]
    x, cot = tokens[0], cotangent[0]

    def token_part(values, s):
        return lax.dynamic_slice_in_dim(values, lax.rem(me_t - s + tp, tp) * own, own, 0)

    def product(left, right):
        return dot(left, right, TN).astype(BF)

    attn_p = gather_1(attn_rows)
    out_rows = [out_own, turn(out_own)]
    while len(out_rows) < tp - 1:
        out_rows.append(turn(out_rows[-1]))
    attn_p, out_rows, ffn_rows = tie((attn_p, out_rows, ffn_rows))
    attn_p = gather_2(attn_p)
    out_rows.append(turn(out_rows[-1]))
    attn_p, out_rows, ffn_rows = tie((attn_p, out_rows, ffn_rows))
    out_whole = jnp.concatenate(out_rows, 1)
    attn_p, out_whole, ffn_rows = tie((attn_p, out_whole, ffn_rows))
    ffn_all = lax.all_gather(ffn_rows, "dp", axis=0, tiled=True)
    out_p = gather_1(out_whole)
    attn_p = gather_3(attn_p)
    hn, w, gains, q8, kn, vl, aq, ak, og, q, ks, kd, vd, lg = pre(x, here, attn_p, bias_row, gqk, heads)
    q8, out_p = tie((q8, out_p))
    out_p = gather_2(out_p)
    u, *kept_att = attend(0, block, q8, aq, kn, ak, vl, og, ())
    u, kept_att, q8 = tie((u, kept_att, q8))
    us = [[u]]

    first = tp - 1
    kept_ffn, gmids = (), []
    parts, got = [None] * chunks, [None] * chunks

    made = first + chunks
    sums = []
    out_all = None
    for t in range(first + chunks - 1 + first + 1):
        send = {}
        for c in range(chunks):
            step = t - first - c
            if 1 <= step <= first:
                send[c] = parts[c][1] if step == 1 else add(got[c], parts[c][step])
        y_send = token_part(kept_ffn[5], 1) if t == made + first - 1 else None
        send, q8, kept_ffn, x, y_send = tie((send, q8, kept_ffn, x, y_send))
        new_u = {c: turn(us[c][-1]) for c in range(len(us)) if 1 <= t - c + 1 <= first}
        new_du = {c: turn(value) for c, value in send.items()}
        fresh = None
        if t + 1 < chunks:
            fresh, *kept_att = attend(t + 1, block, q8, aq, kn, ak, vl, og, kept_att)
        if t == 1:
            out_p = gather_3(out_p)
        if t == 2:
            out_all = assemble(out_p, me_d)
        chunk = t - first
        if 0 <= chunk < chunks:
            outs = feed(chunk, block, own, at, x, cot, gains, out_all, ffn_all, us[chunk], kept_ffn)
            kept_ffn, parts[chunk] = outs[:6], outs[6:-1]
            gmids.append(outs[-1][0:1])
        h2, hid, dgu, res, uc, part = kept_ffn if kept_ffn else [None] * 6
        if t == made + first - 1:
            y_acc = turn(y_send)
        fill = None
        for i, pair in enumerate(((res, uc), (h2, dgu), (cot, hid))):
            if t == made + i:
                fill = product(*pair)
        new_u, new_du, fresh, kept_att, kept_ffn, parts, fill, out_p, out_all, q8 = tie(
            (new_u, new_du, fresh, kept_att, kept_ffn, parts, fill, out_p, out_all, q8)
        )
        if fill is not None:
            sums.append(scatter(fill))
        for c, value in new_u.items():
            us[c].append(value)
        if fresh is not None:
            us.append([fresh])
        got = [new_du.get(c, got[c]) for c in range(chunks)]
    att, li = kept_att
    h2, hid, dgu, res, uc, part = kept_ffn

    du = jnp.concatenate([add(got[c], parts[c][0]) for c in range(chunks)], 0)
    du, gmid = tie((du, sum(gmids)))
    pairs, back_parts = width // 128, []
    cuts = [0, 1, pairs] if pairs > 1 else [0, pairs]
    y_step = 2
    for begin, end in zip(cuts, cuts[1:]):
        for pair in range(begin, end):
            back_parts.append(attend_back(pair, block, heads, q8, aq, kn, ak, vl, og, att, li, du))
        y_acc, back_parts = tie((y_acc, back_parts))
        if y_step < tp:
            send, y_step = add(y_acc, token_part(part, y_step)), y_step + 1
            send, du = tie((send, du))
            y_acc = turn(send)
    dq, dk, dv, dc = zip(*back_parts)
    dp_all, gt, g0, gq, gb = post(
        heads, dq, dk, dv, dc, q, ks, kd, vd, lg, du, att, og, x, res, gains, w, bias_row, gqk
    )
    y_acc, dp_all, gt, g0 = tie((y_acc, dp_all, gt, g0))

    gq = gq[0:2].reshape(2, heads, 64).sum(1)
    gb = lax.dynamic_update_slice_in_dim(
        jnp.zeros(forget_bias.shape, F32), gb[0, 2 * heads : 2 * heads + heads_real], me_t * heads_real, 0
    )
    small = jnp.concatenate([gq.reshape(-1), gb])
    small = jnp.pad(small, (0, model - small.shape[0]))[None]
    flat = jnp.concatenate([g0[0:1], gmid, small, jnp.zeros((5, model), F32)], 0)
    ring = [sums[0][:, i * width : (i + 1) * width] for i in range(tp)]
    low, high = slice(0, model // 2), slice(model // 2, model)
    send, out_send = [token_part(gt[:, cols], 1) for cols in (low, high)], ring[1]
    send, out_send, flat, dp_all = tie((send, out_send, flat, dp_all))
    while y_step < tp:
        y_acc, y_step = turn(add(y_acc, token_part(part, y_step))), y_step + 1
    back = [turn(value) for value in send]
    fill = product(hn, dp_all)
    back, fill = tie((back, fill))
    sums.append(scatter(fill))
    for s in range(2, tp):
        back = [turn(add(value, token_part(gt[:, cols], s))) for value, cols in zip(back, (low, high))]
    out_acc = turn(out_send)
    for s in range(2, tp):
        out_acc = turn(add(out_acc, ring[s]))
    for axis, size in (("tp", tp), ("dp", dp)):
        for bit in range(size.bit_length() - 1):
            flat = flat + swap(flat, axis, 1 << bit)
    result = total_of((y_acc, token_part(part, 0))).astype(BF)
    grad_tokens = total_of((token_part(gt, 0), jnp.concatenate(back, 1)))
    grad_gu, grad_down, grad_attn = [value.astype(F32) for value in sums[1:]]
    grad_out_own = total_of((ring[0], out_acc))
    norm_grad = flat[0:2]
    qk_grad = flat[2, : 2 * 64].reshape(2, 64)
    bias_grad = flat[2, 2 * 64 : 2 * 64 + forget_bias.shape[0]]

    grad_attn_in = jnp.transpose(grad_attn[:, : 4 * width].reshape(cut, 4, width)[:, :, :width_real], (1, 0, 2))
    grad_gates = grad_attn[:, 4 * width : 4 * width + 3 * heads].reshape(cut, 3, heads)[:, :, :heads_real]
    return (
        result[None],
        grad_tokens[None],
        grad_attn_in,
        jnp.transpose(grad_gates, (1, 0, 2)),
        jnp.transpose(grad_out_own[:, :width_real]),
        jnp.stack([grad_gu[:, :hidden], grad_gu[:, hidden:]]),
        jnp.transpose(grad_down),
        norm_grad,
        qk_grad,
        bias_grad,
    )


def solution(mesh):
    return jax.shard_map(
        shards,
        mesh=mesh,
        in_specs=(
            P("dp", None, None), P(None, "dp", "tp"), P(None, "dp", "tp"), P("tp", "dp"), P(None, "dp"), P(), P(),
            P(None, "dp", "tp"), P("tp", "dp"), P("dp", None), P("dp"), P("dp", None, None),
        ),
        out_specs=(
            P("dp", "tp", None), P("dp", "tp", None), P(None, "dp", "tp"), P(None, "dp", "tp"), P("tp", "dp"),
            P(None, "dp", "tp"), P("tp", "dp"), P(), P(), P(),
        ),
        check_vma=False,
    )
```

time: 718 us -> 526 us (0.73)
  waiting for transfers between devices: 345 us -> 122 us
  matrix products: 89.2 us -> 50.9 us
  local copies, waits for them, and re-layouts: 24.3 us -> 47.1 us
  other arithmetic: 20.9 us -> 36.7 us
  between operations: 2.88 us -> 15.6 us
  Pallas kernels: 173 us -> 185 us
    ppermute x30 -> x33, waiting for transfers between devices: 220 us -> 101 us  [turn(): return lax.ppermute(value, 'tp', [(i, (i + 1) % size) for i in range(size)])]
    ppermute x40 -> x23, waiting for transfers between devices: 125 us -> 19.8 us  [swap(): return lax.ppermute(value, axis, [(i, i ^ bit) for i in range(size)])]
    dot_general x16 -> x4, matrix products: 89.2 us -> 50.9 us  [dot(): return lax.dot_general(a, b, dims, preferred_element_type=F32)]
    ppermute x30 -> x33, starting transfers between devices: 20.2 us -> 43.4 us  [turn(): return lax.ppermute(value, 'tp', [(i, (i + 1) % size) for i in range(size)])]
    ppermute x40 -> x23, starting transfers between devices: 33.9 us -> 15.7 us  [swap(): return lax.ppermute(value, axis, [(i, i ^ bit) for i in range(size)])]
    dynamic_update_slice x0 -> x10, local copies, waits for them, and re-layouts: none -> 13 us  [assemble(): lax.dynamic_update_slice_in_dim(whole, piece, (me ^ far) * cut + start, 0)]
    pallas_call x3 -> x5, Pallas kernels: 77.6 us -> 88.2 us  [the longest x3 38.6 us: attend_back(): pl.pallas_call(functools.partial(bwd_kernel, pair, heads, block), grid=(1...]
    convert_element_type x22 -> x16, other arithmetic: 9.91 us -> 16.5 us  [add(): return (a.astype(F32) + b.astype(F32)).astype(BF)]
  transfers between devices with their start and end apart: 70 -> 61, of which waited for: 41 -> 26; matrix products, arithmetic and copies ran while one was open for 14% -> 24% of each run, Pallas kernels for 21% -> 36%
where the time goes in v2:
time: 526 us; the launch traced here: 516 us
  Pallas kernels  185 us (35%)
  waiting for transfers between devices  122 us (23%)
  starting transfers between devices  59.5 us (11%)
  matrix products  50.9 us (10%)
  local copies, waits for them, and re-layouts  47.1 us (9%)
  other arithmetic  36.7 us (7%)
  between operations  15.6 us (3%)
    ppermute x33, waiting for transfers between devices, turn(): return lax.ppermute(value, 'tp', [(i, (i + 1) % size) for i in range(size)])  101 us
    pallas_call x3, Pallas kernels, feed(): pl.pallas_call(functools.partial(ffn_kernel, count, chunk, block, step_ro...  74.5 us
    dot_general x4, matrix products, dot(): return lax.dot_general(a, b, dims, preferred_element_type=F32)  50.9 us
    ppermute x33, starting transfers between devices, turn(): return lax.ppermute(value, 'tp', [(i, (i + 1) % size) for i in range(size)])  43.4 us
    pallas_call x3, Pallas kernels, attend_back(): pl.pallas_call(functools.partial(bwd_kernel, pair, heads, block), grid=(1...  38.6 us
    pallas_call x1, Pallas kernels, post(): pl.pallas_call(functools.partial(post_kernel, heads, pairs), grid=(count,...  26.4 us
    pallas_call x1, Pallas kernels, pre(): pl.pallas_call(functools.partial(pre_kernel, heads, spots), grid=(seq //...  23.2 us
    pallas_call x3, Pallas kernels, attend(): pl.pallas_call(functools.partial(fwd_kernel, chunk, block), grid=grid, in...  21.9 us
  transfers between devices with their start and end apart: 61, of which 26 were waited for; matrix products, arithmetic and copies ran while one was open for 24% of the time, Pallas kernels for 36%

profile of v2, /device:TPU:0, one launch (start us, length us, event | category | flops | bytes accessed | tf_op | source)
XLA Modules:
  0.0 516.0 jit_solution(2579842160655986330)
XLA Ops:
  16.3 6.0 %collective-permute-done.3 = bf16[192,384]{1,0:T(8,128)(2,1)} collective-permute-done((bf16[192,384]{1,0:T(8,128)(2,1)S(1)}, bf16[192,384]{1,0:T(8,128)(2,1)}, u32[]{:S(2)}, u32[]{:S(2)}) %collective-permute-start.3) | collective-permute-done | bytes 147488 | tf_op jit(solution)/shard_map/ppermute | solution.py:492
  23.4 6.0 %collective-permute-done.4 = bf16[192,384]{1,0:T(8,128)(2,1)S(1)} collective-permute-done((bf16[192,384]{1,0:T(8,128)(2,1)}, bf16[192,384]{1,0:T(8,128)(2,1)S(1)}, u32[]{:S(2)}, u32[]{:S(2)}) %collective-permute-start.4) | collective-permute-done | bytes 147488 | tf_op jit(solution)/shard_map/ppermute | solution.py:492
  33.9 5.5 %collective-permute-done.9 = bf16[192,384]{1,0:T(8,128)(2,1)S(1)} collective-permute-done((bf16[192,384]{1,0:T(8,128)(2,1)S(1)}, bf16[192,384]{1,0:T(8,128)(2,1)S(1)}, u32[]{:S(2)}, u32[]{:S(2)}) %collective-permute-start.9) | collective-permute-done | bytes 147488 | tf_op jit(solution)/shard_map/ppermute | solution.py:492
  48.6 23.2 %pre.1 = (bf16[1536,1536]{1,0:T(8,128)(2,1)}, bf16[1536,1664]{1,0:T(8,128)(2,1)}, f32[8,1536]{1,0:T(8,128)}, bf16[1536,384]{1,0:T(8,128)(2,1)}, bf16[1536,384]{1...) custom-call(s32[1]{0:T(128)} %bitcast.me_ref, ...), custom_call_target="tpu_custom_call" | custom-call | flops 1 | bytes 1 | tf_op jit(solution)/shard_map/pre/pallas_call | solution.py:157
  82.5 7.4 %attend.4 = (bf16[512,384]{1,0:T(8,128)(2,1)}, f32[1536,384]{1,0:T(8,128)}, f32[1536,384]{1,0:T(8,128)}) custom-call(bf16[1536,384]{1,0:T(8,128)(2,1)} %get-tuple-element.602.q_ref, bf16[1536,128]{1,0:T(8,128)(2,1)} %get-tuple-element.377.aq_ref, bf16[1536,384]{1,0:T(8,128)(2,1)} %get-tuple-element.378.k_ref, ...), custom_call_target="tpu_custom_call", output_to_operand_aliasing={{1}: (6, {}), {2}: (7, {})} | custom-call | flops 1 | bytes 1 | tf_op jit(solution)/shard_map/attend/pallas_call | solution.py:211
  89.9 5.5 %collective-permute-done.18 = bf16[96,1536]{1,0:T(8,128)(2,1)} collective-permute-done((bf16[96,1536]{1,0:T(8,128)(2,1)S(1)}, bf16[96,1536]{1,0:T(8,128)(2,1)}, u32[]{:S(2)}, u32[]{:S(2)}) %collective-permute-start.18) | collective-permute-done | bytes 294944 | tf_op jit(solution)/shard_map/ppermute | solution.py:487
  100.5 9.2 %attend.5 = (bf16[512,384]{1,0:T(8,128)(2,1)}, f32[1536,384]{1,0:T(8,128)}, f32[1536,384]{1,0:T(8,128)}) custom-call(bf16[1536,384]{1,0:T(8,128)(2,1)} %get-tuple-element.602.q_ref, bf16[1536,128]{1,0:T(8,128)(2,1)} %get-tuple-element.377.aq_ref, bf16[1536,384]{1,0:T(8,128)(2,1)} %get-tuple-element.378.k_ref, ...), custom_call_target="tpu_custom_call", output_to_operand_aliasing={{1}: (6, {}), {2}: (7, {})} | custom-call | flops 1 | bytes 1 | tf_op jit(solution)/shard_map/attend/pallas_call | solution.py:211
  111.1 6.0 %collective-permute-done.21.refs_1_ = bf16[512,384]{1,0:T(8,128)(2,1)S(1)} collective-permute-done((bf16[512,384]{1,0:T(8,128)(2,1)}, bf16[512,384]{1,0:T(8,128)(2,1)S(1)}, u32[]{:S(2)}, u32[]{:S(2)}) %collective-permute-start.21) | collective-permute-done | bytes 393248 | tf_op jit(solution)/shard_map/ppermute | solution.py:492
  145.2 24.8 %feed.3 = (bf16[1536,1536]{1,0:T(8,128)(2,1)}, bf16[1536,1024]{1,0:T(8,128)(2,1)}, bf16[1536,2048]{1,0:T(8,128)(2,1)}, bf16[1536,1536]{1,0:T(8,128)(2,1)}, bf16[...) custom-call(s32[1]{0:T(128)} %bitcast.12.at_ref, ...), custom_call_target="tpu_custom_call" | custom-call | flops 1 | bytes 1 | tf_op jit(solution)/shard_map/feed/pallas_call | solution.py:289
  175.0 24.8 %feed.4 = (bf16[1536,1536]{1,0:T(8,128)(2,1)}, bf16[1536,1024]{1,0:T(8,128)(2,1)}, bf16[1536,2048]{1,0:T(8,128)(2,1)}, bf16[1536,1536]{1,0:T(8,128)(2,1)}, bf16[...) custom-call(s32[1]{0:T(128)} %bitcast.12.at_ref, ...), custom_call_target="tpu_custom_call", output_to_operand_aliasing={{0}: (10, {}), {1}: (11, {}), {2}: (12, {}), {3}: (13, {}),... | custom-call | flops 1 | bytes 1 | tf_op jit(solution)/shard_map/feed/pallas_call | solution.py:289
  200.1 9.0 %collective-permute-start.32 = (bf16[512,384]{1,0:T(8,128)(2,1)}, bf16[512,384]{1,0:T(8,128)(2,1)S(1)}, u32[]{:S(2)}, u32[]{:S(2)}) collective-permute-start(bf16[512,384]{1,0:T(8,128)(2,1)} %get-tuple-element.501), channel_id=1, source_target_pairs={{0,1},{1,2},{2,3},{3,0},{4,5},{5,6},{6,7},{7,4},{8,9},{9,10},{10,1... | collective-permute-start | bytes 1179656 | tf_op jit(solution)/shard_map/ppermute | solution.py:492
  209.1 24.9 %feed.5 = (bf16[1536,1536]{1,0:T(8,128)(2,1)}, bf16[1536,1024]{1,0:T(8,128)(2,1)}, bf16[1536,2048]{1,0:T(8,128)(2,1)}, bf16[1536,1536]{1,0:T(8,128)(2,1)}, bf16[...) custom-call(s32[1]{0:T(128)} %bitcast.12.at_ref, ...), custom_call_target="tpu_custom_call", output_to_operand_aliasing={{0}: (10, {}), {1}: (11, {}), {2}: (12, {}), {3}: (13, {}),... | custom-call | flops 1 | bytes 1 | tf_op jit(solution)/shard_map/feed/pallas_call | solution.py:289
  238.9 12.3 %convolution_convert_fusion.2 = bf16[1536,1536]{1,0:T(8,128)(2,1)} fusion(bf16[1536,1536]{1,0:T(8,128)(2,1)} %get-tuple-element.644.res_ref, bf16[1536,1536]{1,0:T(8,128)(2,1)} %get-tuple-element.550), kind=kOutput, calls=%fused_computation.2 | convolution fusion | flops 7250116608 | bytes 14155776 | tf_op jit(solution)/shard_map/dot_general | solution.py:23
  264.5 15.9 %convolution_convert_fusion.1 = bf16[1536,2048]{1,0:T(8,128)(2,1)} fusion(bf16[1536,1536]{1,0:T(8,128)(2,1)} %get-tuple-element.574, bf16[1536,2048]{1,0:T(8,128)(2,1)} %get-tuple-element.576), kind=kOutput, calls=%fused_computation.1 | convolution fusion | flops 9666822144 | bytes 17301504 | tf_op jit(solution)/shard_map/dot_general | solution.py:23
  284.8 8.9 %fusion = bf16[1536,1024]{0,1:T(8,128)(2,1)} fusion(bf16[1536,1024]{1,0:T(8,128)(2,1)S(1)} %copy-done, bf16[1,1536,1536]{2,1,0:T(8,128)(2,1)} %param.37), kind=kOutput, calls=%fused_computation.4 | convolution fusion | flops 4833411072 | bytes 11010048 | tf_op jit(solution)/shard_map/dot_general | solution.py:23
  306.4 12.7 %attend_back.3 = (f32[1536,128]{1,0:T(8,128)}, f32[1536,128]{1,0:T(8,128)}, f32[1536,128]{1,0:T(8,128)}, f32[1536,128]{1,0:T(8,128)}) custom-call(bf16[1536,384]{1,0:T(8,128)(2,1)} %get-tuple-element.602.q_ref, bf16[1536,128]{1,0:T(8,128)(2,1)} %get-tuple-element.377.aq_ref, bf16[1536,384]{1,0:T(8,128)(2,1)} %get-tuple-element.378.k_ref, ...), custom_call_target="tpu_custom_call" | custom-call | flops 1 | bytes 1 | tf_op jit(solution)/shard_map/attend_back/pallas_call | solution.py:365
  319.2 6.1 %collective-permute-done.38 = bf16[384,1536]{1,0:T(8,128)(2,1)S(1)} collective-permute-done((bf16[384,1536]{1,0:T(8,128)(2,1)S(1)}, bf16[384,1536]{1,0:T(8,128)(2,1)S(1)}, u32[]{:S(2)}, u32[]{:S(2)}) %collective-permute-start.38) | collective-permute-done | bytes 1179680 | tf_op jit(solution)/shard_map/ppermute | solution.py:492
  328.3 12.9 %attend_back.5 = (f32[1536,128]{1,0:T(8,128)}, f32[1536,128]{1,0:T(8,128)}, f32[1536,128]{1,0:T(8,128)}, f32[1536,128]{1,0:T(8,128)}) custom-call(bf16[1536,384]{1,0:T(8,128)(2,1)} %get-tuple-element.602.q_ref, bf16[1536,128]{1,0:T(8,128)(2,1)} %get-tuple-element.377.aq_ref, bf16[1536,384]{1,0:T(8,128)(2,1)} %get-tuple-element.378.k_ref, ...), custom_call_target="tpu_custom_call" | custom-call | flops 1 | bytes 1 | tf_op jit(solution)/shard_map/attend_back/pallas_call | solution.py:365
  341.2 13.0 %attend_back.4 = (f32[1536,128]{1,0:T(8,128)}, f32[1536,128]{1,0:T(8,128)}, f32[1536,128]{1,0:T(8,128)}, f32[1536,128]{1,0:T(8,128)}) custom-call(bf16[1536,384]{1,0:T(8,128)(2,1)} %get-tuple-element.602.q_ref, bf16[1536,128]{1,0:T(8,128)(2,1)} %get-tuple-element.377.aq_ref, bf16[1536,384]{1,0:T(8,128)(2,1)} %get-tuple-element.378.k_ref, ...), custom_call_target="tpu_custom_call" | custom-call | flops 1 | bytes 1 | tf_op jit(solution)/shard_map/attend_back/pallas_call | solution.py:365
  356.0 26.4 %post.1 = (bf16[1536,1664]{1,0:T(8,128)(2,1)}, bf16[1536,1536]{1,0:T(8,128)(2,1)}, f32[8,1536]{1,0:T(8,128)}, f32[8,384]{1,0:T(8,128)}, f32[8,128]{1,0:T(8,128)}) custom-call(bf16[1536,384]{1,0:T(8,128)(2,1)} %get-tuple-element.637.q_ref, bf16[1536,384]{1,0:T(8,128)(2,1)} %get-tuple-element.638.ks_ref, bf16[1536,384]{1,0:T(8,128)(2,1)} %get-tuple-element.639.kd_ref, ...), custom_call_target="tpu_custom_call" | custom-call | flops 1 | bytes 1 | tf_op jit(solution)/shard_map/post/pallas_call | solution.py:467
  396.3 13.8 %convolution_convert_fusion = bf16[1536,1664]{1,0:T(8,128)(2,1)} fusion(bf16[1536,1536]{1,0:T(8,128)(2,1)} %get-tuple-element.671, bf16[1536,1664]{1,0:T(8,128)(2,1)} %get-tuple-element.672), kind=kOutput, calls=%fused_computation | convolution fusion | flops 7854292992 | bytes 14942208 | tf_op jit(solution)/shard_map/dot_general | solution.py:23
  446.3 9.7 %collective-permute-done.44 = bf16[384,768]{1,0:T(8,128)(2,1)} collective-permute-done((bf16[384,768]{1,0:T(8,128)(2,1)}, bf16[384,768]{1,0:T(8,128)(2,1)}, u32[]{:S(2)}, u32[]{:S(2)}) %collective-permute-start.44) | collective-permute-done | bytes 589856 | tf_op jit(solution)/shard_map/ppermute | solution.py:492
  457.4 11.1 %collective-permute-done.46 = bf16[384,768]{1,0:T(8,128)(2,1)S(1)} collective-permute-done((bf16[384,768]{1,0:T(8,128)(2,1)}, bf16[384,768]{1,0:T(8,128)(2,1)S(1)}, u32[]{:S(2)}, u32[]{:S(2)}) %collective-permute-start.46) | collective-permute-done | bytes 589856 | tf_op jit(solution)/shard_map/ppermute | solution.py:492
  474.0 24.7 %collective-permute-done.50 = bf16[192,384]{1,0:T(8,128)(2,1)S(1)} collective-permute-done((bf16[192,384]{1,0:T(8,128)(2,1)S(1)}, bf16[192,384]{1,0:T(8,128)(2,1)S(1)}, u32[]{:S(2)}, u32[]{:S(2)}) %collective-permute-start.50) | collective-permute-done | bytes 147488 | tf_op jit(solution)/shard_map/ppermute | solution.py:492
  (279 shorter events, 180.8 us)
Async XLA Ops:
  7.2 138.0 %all-gather.2.cloned.1.call-start = ((), (), s32[]{:S(2)}) async-start(), calls=%async_computation.4 | async-start | bytes 10616832 | tf_op jit(solution)/shard_map/all_gather | solution.py:612
  42.8 348.0 %reduce-scatter.7.cloned.1.call-start = ((), (), s32[]{:S(2)}) async-start(), calls=%async_computation.5 | async-start | bytes 5308416 | tf_op jit(solution)/shard_map/reduce_scatter | solution.py:545
  42.9 28.9 %collective-permute-start.12 = (bf16[192,1536]{1,0:T(8,128)(2,1)S(1)}, bf16[192,1536]{1,0:T(8,128)(2,1)}, u32[]{:S(2)}, u32[]{:S(2)}) collective-permute-start(bf16[192,1536]{1,0:T(8,128)(2,1)S(1)} %pad_maximum_fusion.3), channel_id=1, source_target_pairs={{0,4},{4,0},{8,12},{12,8},{16,20},{20,16},{24,28},{28,24},{1,5},{5... | collective-permute-start | bytes 1769480 | tf_op jit(solution)/shard_map/ppermute | solution.py:487
  43.0 28.9 %collective-permute-start.13 = (bf16[192,1536]{1,0:T(8,128)(2,1)S(1)}, bf16[192,1536]{1,0:T(8,128)(2,1)S(1)}, u32[]{:S(2)}, u32[]{:S(2)}) collective-permute-start(bf16[192,1536]{1,0:T(8,128)(2,1)S(1)} %pad_maximum_fusion.3), channel_id=1, source_target_pairs={{0,8},{4,12},{8,0},{12,4},{16,24},{20,28},{24,16},{28,20},{1,9},{5... | collective-permute-start | bytes 1769480 | tf_op jit(solution)/shard_map/ppermute | solution.py:487
  43.6 28.3 %collective-permute-start.14 = (bf16[192,1536]{1,0:T(8,128)(2,1)S(1)}, bf16[192,1536]{1,0:T(8,128)(2,1)S(1)}, u32[]{:S(2)}, u32[]{:S(2)}) collective-permute-start(bf16[192,1536]{1,0:T(8,128)(2,1)S(1)} %pad_maximum_fusion.3), channel_id=1, source_target_pairs={{0,16},{4,20},{8,24},{12,28},{16,0},{20,4},{24,8},{28,12},{1,17},{... | collective-permute-start | bytes 1769480 | tf_op jit(solution)/shard_map/ppermute | solution.py:487
  71.9 25.0 %collective-permute-start.16 = (bf16[192,1536]{1,0:T(8,128)(2,1)S(1)}, bf16[192,1536]{1,0:T(8,128)(2,1)S(1)}, u32[]{:S(2)}, u32[]{:S(2)}) collective-permute-start(bf16[192,1536]{1,0:T(8,128)(2,1)S(1)} %collective-permute-done.13), channel_id=1, source_target_pairs={{0,4},{4,0},{8,12},{12,8},{16,20},{20,16},{24,28},{28,24},{1,5},{5... | collective-permute-start | bytes 1769480 | tf_op jit(solution)/shard_map/ppermute | solution.py:487
  72.1 24.8 %collective-permute-start.17 = (bf16[192,1536]{1,0:T(8,128)(2,1)S(1)}, bf16[192,1536]{1,0:T(8,128)(2,1)S(1)}, u32[]{:S(2)}, u32[]{:S(2)}) collective-permute-start(bf16[192,1536]{1,0:T(8,128)(2,1)S(1)} %collective-permute-done.14), channel_id=1, source_target_pairs={{0,4},{4,0},{8,12},{12,8},{16,20},{20,16},{24,28},{28,24},{1,5},{5... | collective-permute-start | bytes 1769480 | tf_op jit(solution)/shard_map/ppermute | solution.py:487
  118.5 26.4 %collective-permute-start.26 = (bf16[512,384]{1,0:T(8,128)(2,1)}, bf16[512,384]{1,0:T(8,128)(2,1)}, u32[]{:S(2)}, u32[]{:S(2)}) collective-permute-start(bf16[512,384]{1,0:T(8,128)(2,1)} %get-tuple-element.417.refs_0_), channel_id=1, source_target_pairs={{0,1},{1,2},{2,3},{3,0},{4,5},{5,6},{6,7},{7,4},{8,9},{9,10},{10,1... | collective-permute-start | bytes 1179656 | tf_op jit(solution)/shard_map/ppermute | solution.py:492
  144.9 25.1 %collective-permute-start.27 = (bf16[512,384]{1,0:T(8,128)(2,1)}, bf16[512,384]{1,0:T(8,128)(2,1)S(1)}, u32[]{:S(2)}, u32[]{:S(2)}) collective-permute-start(bf16[512,384]{1,0:T(8,128)(2,1)} %collective-permute-done.25.refs_2_), channel_id=1, source_target_pairs={{0,1},{1,2},{2,3},{3,0},{4,5},{5,6},{6,7},{7,4},{8,9},{9,10},{10,1... | collective-permute-start | bytes 1179656 | tf_op jit(solution)/shard_map/ppermute | solution.py:492
  144.9 25.1 %collective-permute-start.28 = (bf16[512,384]{1,0:T(8,128)(2,1)}, bf16[512,384]{1,0:T(8,128)(2,1)S(1)}, u32[]{:S(2)}, u32[]{:S(2)}) collective-permute-start(bf16[512,384]{1,0:T(8,128)(2,1)} %collective-permute-done.26.refs_1_), channel_id=1, source_target_pairs={{0,1},{1,2},{2,3},{3,0},{4,5},{5,6},{6,7},{7,4},{8,9},{9,10},{10,1... | collective-permute-start | bytes 1179656 | tf_op jit(solution)/shard_map/ppermute | solution.py:492
  170.0 29.8 %collective-permute-start.30 = (bf16[512,384]{1,0:T(8,128)(2,1)}, bf16[512,384]{1,0:T(8,128)(2,1)S(1)}, u32[]{:S(2)}, u32[]{:S(2)}) collective-permute-start(bf16[512,384]{1,0:T(8,128)(2,1)} %get-tuple-element.464), channel_id=1, source_target_pairs={{0,1},{1,2},{2,3},{3,0},{4,5},{5,6},{6,7},{7,4},{8,9},{9,10},{10,1... | collective-permute-start | bytes 1179656 | tf_op jit(solution)/shard_map/ppermute | solution.py:492
  170.7 29.1 %collective-permute-start.29 = (bf16[512,384]{1,0:T(8,128)(2,1)S(1)}, bf16[512,384]{1,0:T(8,128)(2,1)S(1)}, u32[]{:S(2)}, u32[]{:S(2)}) collective-permute-start(bf16[512,384]{1,0:T(8,128)(2,1)S(1)} %collective-permute-done.28.refs_2_), channel_id=1, source_target_pairs={{0,1},{1,2},{2,3},{3,0},{4,5},{5,6},{6,7},{7,4},{8,9},{9,10},{10,1... | collective-permute-start | bytes 1179656 | tf_op jit(solution)/shard_map/ppermute | solution.py:492
  200.0 34.0 %collective-permute-start.31 = (bf16[512,384]{1,0:T(8,128)(2,1)S(1)}, bf16[512,384]{1,0:T(8,128)(2,1)S(1)}, u32[]{:S(2)}, u32[]{:S(2)}) collective-permute-start(bf16[512,384]{1,0:T(8,128)(2,1)S(1)} %add_convert_fusion.15), channel_id=1, source_target_pairs={{0,1},{1,2},{2,3},{3,0},{4,5},{5,6},{6,7},{7,4},{8,9},{9,10},{10,1... | collective-permute-start | bytes 1179656 | tf_op jit(solution)/shard_map/ppermute | solution.py:492
  200.1 33.9 %collective-permute-start.32 = (bf16[512,384]{1,0:T(8,128)(2,1)}, bf16[512,384]{1,0:T(8,128)(2,1)S(1)}, u32[]{:S(2)}, u32[]{:S(2)}) collective-permute-start(bf16[512,384]{1,0:T(8,128)(2,1)} %get-tuple-element.501), channel_id=1, source_target_pairs={{0,1},{1,2},{2,3},{3,0},{4,5},{5,6},{6,7},{7,4},{8,9},{9,10},{10,1... | collective-permute-start | bytes 1179656 | tf_op jit(solution)/shard_map/ppermute | solution.py:492
  259.8 167.4 %reduce-scatter.13.cloned.1.call-start = ((), (), s32[]{:S(2)}) async-start(), calls=%async_computation.8 | async-start | bytes 3538944
  299.3 203.2 %reduce-scatter.11.cloned.1.call-start = ((), (), s32[]{:S(2)}) async-start(), calls=%async_computation.7 | async-start | bytes 7077888 | tf_op jit(solution)/shard_map/reduce_scatter | solution.py:545
  299.9 205.4 %reduce-scatter.9.cloned.1.call-start = ((), (), s32[]{:S(2)}) async-start(), calls=%async_computation.6 | async-start | bytes 5750784 | tf_op jit(solution)/shard_map/reduce_scatter | solution.py:545
  326.9 27.3 %collective-permute-start.40 = (bf16[384,1536]{1,0:T(8,128)(2,1)S(1)}, bf16[384,1536]{1,0:T(8,128)(2,1)S(1)}, u32[]{:S(2)}, u32[]{:S(2)}) collective-permute-start(bf16[384,1536]{1,0:T(8,128)(2,1)S(1)} %add_convert_fusion.2), channel_id=1, source_target_pairs={{0,1},{1,2},{2,3},{3,0},{4,5},{5,6},{6,7},{7,4},{8,9},{9,10},{10,1... | collective-permute-start | bytes 3538952 | tf_op jit(solution)/shard_map/ppermute | solution.py:492
  355.8 28.3 %collective-permute-start.41 = (bf16[384,1536]{1,0:T(8,128)(2,1)S(1)}, bf16[384,1536]{1,0:T(8,128)(2,1)S(1)}, u32[]{:S(2)}, u32[]{:S(2)}) collective-permute-start(bf16[384,1536]{1,0:T(8,128)(2,1)S(1)} %add_convert_fusion.1), channel_id=1, source_target_pairs={{0,1},{1,2},{2,3},{3,0},{4,5},{5,6},{6,7},{7,4},{8,9},{9,10},{10,1... | collective-permute-start | bytes 3538952 | tf_op jit(solution)/shard_map/ppermute | solution.py:492
  439.9 28.6 %collective-permute-start.46 = (bf16[384,768]{1,0:T(8,128)(2,1)}, bf16[384,768]{1,0:T(8,128)(2,1)S(1)}, u32[]{:S(2)}, u32[]{:S(2)}) collective-permute-start(bf16[384,768]{1,0:T(8,128)(2,1)} %add_convert_fusion.4), channel_id=1, source_target_pairs={{0,1},{1,2},{2,3},{3,0},{4,5},{5,6},{6,7},{7,4},{8,9},{9,10},{10,1... | collective-permute-start | bytes 1769480 | tf_op jit(solution)/shard_map/ppermute | solution.py:492
  442.9 28.9 %collective-permute-start.49 = (bf16[192,384]{1,0:T(8,128)(2,1)}, bf16[192,384]{1,0:T(8,128)(2,1)}, u32[]{:S(2)}, u32[]{:S(2)}) collective-permute-start(bf16[192,384]{1,0:T(8,128)(2,1)} %add_convert_fusion.17), channel_id=1, source_target_pairs={{0,1},{1,2},{2,3},{3,0},{4,5},{5,6},{6,7},{7,4},{8,9},{9,10},{10,1... | collective-permute-start | bytes 442376 | tf_op jit(solution)/shard_map/ppermute | solution.py:492
  457.4 42.1 %collective-permute-start.45 = (bf16[384,768]{1,0:T(8,128)(2,1)S(1)}, bf16[384,768]{1,0:T(8,128)(2,1)S(1)}, u32[]{:S(2)}, u32[]{:S(2)}) collective-permute-start(bf16[384,768]{1,0:T(8,128)(2,1)S(1)} %add_convert_fusion.5), channel_id=1, source_target_pairs={{0,1},{1,2},{2,3},{3,0},{4,5},{5,6},{6,7},{7,4},{8,9},{9,10},{10,1... | collective-permute-start | bytes 1769480 | tf_op jit(solution)/shard_map/ppermute | solution.py:492
  468.7 30.8 %collective-permute-start.47 = (bf16[384,768]{1,0:T(8,128)(2,1)S(1)}, bf16[384,768]{1,0:T(8,128)(2,1)S(1)}, u32[]{:S(2)}, u32[]{:S(2)}) collective-permute-start(bf16[384,768]{1,0:T(8,128)(2,1)S(1)} %add_convert_fusion.3), channel_id=1, source_target_pairs={{0,1},{1,2},{2,3},{3,0},{4,5},{5,6},{6,7},{7,4},{8,9},{9,10},{10,1... | collective-permute-start | bytes 1769480 | tf_op jit(solution)/shard_map/ppermute | solution.py:492
  472.7 26.0 %collective-permute-start.50 = (bf16[192,384]{1,0:T(8,128)(2,1)S(1)}, bf16[192,384]{1,0:T(8,128)(2,1)S(1)}, u32[]{:S(2)}, u32[]{:S(2)}) collective-permute-start(bf16[192,384]{1,0:T(8,128)(2,1)S(1)} %add_convert_fusion.16), channel_id=1, source_target_pairs={{0,1},{1,2},{2,3},{3,0},{4,5},{5,6},{6,7},{7,4},{8,9},{9,10},{10,1... | collective-permute-start | bytes 442376 | tf_op jit(solution)/shard_map/ppermute | solution.py:492
  (73 other events, 910.2 us)
Sparse Core Ops, SparseCore 0:
  42.9 70.2 all-gather.1
  259.9 52.7 reduce-scatter.6
  316.5 46.2 reduce-scatter.12
  366.0 61.7 reduce-scatter.10
  431.6 55.7 reduce-scatter.8

commit v3 on v2

--- a/solution.py
+++ b/solution.py
@@ -5,6 +5,7 @@
 import numpy as np
 from jax import lax
 from jax.experimental import pallas as pl
+from jax.experimental.layout import Layout, with_layout_constraint
 from jax.experimental.pallas import tpu as pltpu
 from jax.sharding import PartitionSpec as P
 
@@ -178,6 +179,7 @@
     q, aq = q_ref[...], aq_ref[...]
     lane = lanes(q.shape)
     ones = jnp.ones((block, 128), BF)
+    fine = block // 2
     out = []
     for side in range(2):
         head = 2 * pair + side
@@ -186,13 +188,18 @@
         zero = jnp.zeros_like(q)
         qa = jnp.concatenate([jnp.where(mine, q, zero), jnp.where(aug, aq, zero)], 1)
         acc = jnp.zeros((block, 256), F32)
-        for j in range(chunk + 1):
+        for j in range(chunk):
             at = slice(j * block, (j + 1) * block)
             e = jnp.exp(dot(qa, jnp.concatenate([k_ref[at, :], ak_ref[at, :]], 1), NT))
-            if j == chunk:
-                e = jnp.where(rows_of(e.shape) >= lanes(e.shape), e, 0.0)
             acc = acc + dot(e.astype(BF), jnp.concatenate([v_ref[at, :], ones], 1))
-        out.append(acc)
+        tops = []
+        for begin in range(0, block, fine):
+            at = slice(chunk * block, chunk * block + begin + fine)
+            rows = slice(begin, begin + fine)
+            e = jnp.exp(dot(qa[rows], jnp.concatenate([k_ref[at, :], ak_ref[at, :]], 1), NT))
+            e = jnp.where(rows_of(e.shape) + begin >= lanes(e.shape), e, 0.0)
+            tops.append(acc[rows] + dot(e.astype(BF), jnp.concatenate([v_ref[at, :], ones[: begin + fine]], 1)))
+        out.append(jnp.concatenate(tops, 0))
     low = lane < 64
     total = jnp.where(low, out[0][:, 128:], out[1][:, 128:])
     inverse = 1.0 / total
@@ -223,52 +230,93 @@
 
 
 def ffn_kernel(
-    count, chunk, block, step_rows, own, at_ref, x_ref, cot_ref, gain_ref, o_ref, f_ref, *refs
+    count, chunk, block, step_rows, own, at_ref, x_ref, cot_ref, gain_ref, o_any, f_any, *refs
 ):
-    us, outs = refs[:count], refs[-7 - count :]
+    us, outs = refs[:count], refs[-10 - count : -3]
+    o_ref, f_ref, sems = refs[-3:]
+    copies = [pltpu.make_async_copy(a, b, sems.at[i]) for i, (a, b) in enumerate(((o_any, o_ref), (f_any, f_ref)))]
+
+    copies[0].start()
+    copies[1].start()
     h2_ref, hid_ref, dgu_ref, res_ref, uc_ref, part_ref = outs[:6]
     dus, gmid_ref = outs[6:-1], outs[-1]
     hidden = hid_ref.shape[1]
-    u = jnp.concatenate([r[...] for r in us], 1)
-    uc_ref[...] = u
-    x = x_ref[...].astype(F32)
-    cot = cot_ref[...]
-    y1 = x + dot(u, o_ref[...], NT)
-    factor = lax.rsqrt(jnp.mean(y1 * y1, -1, keepdims=True) + EPS)
-    n = y1 * factor
     gain = gain_ref[1:2, :]
-    h2 = (n * gain).astype(BF)
-    h2_ref[...] = h2
-    gu = dot(h2, f_ref[:, : 2 * hidden])
-    g, up = gu[:, :hidden], gu[:, hidden:]
-    sg = jax.nn.sigmoid(g)
-    act = g * sg
-    hid = (act * up).astype(BF)
-    hid_ref[...] = hid
-    dhid = dot(cot, f_ref[:, 2 * hidden :])
-    dg = dhid * up * sg * (1.0 + g * (1.0 - sg))
-    dgu = jnp.concatenate([dg.astype(BF), (dhid * act).astype(BF)], 1)
-    dgu_ref[...] = dgu
-    part = dot(hid, f_ref[:, 2 * hidden :], NT)
-    token = chunk * block + pl.program_id(0) * step_rows + rows_of((step_rows, 1))
-    owned = (token >= at_ref[0] * own) & (token < (at_ref[0] + 1) * own)
-    part_ref[...] = (part + jnp.where(owned, y1, 0.0)).astype(BF)
-    dh2 = dot(dgu, f_ref[:, : 2 * hidden], NT)
-    gmid = jnp.sum(dh2 * n, 0, keepdims=True)
-
-    @pl.when(pl.program_id(0) == 0)
-    def _():
-        gmid_ref[...] = jnp.zeros_like(gmid_ref)
-
-    gmid_ref[0:1, :] += gmid
-    wd = gain * dh2
-    res = factor * (wd - n * jnp.mean(wd * n, -1, keepdims=True))
-    res = jnp.where(at_ref[0] == 0, res + cot.astype(F32), res).astype(BF)
-    res_ref[...] = res
-    du = dot(res, o_ref[...]).astype(BF)
-    width = du.shape[1] // count
-    for s in range(count):
-        dus[s][...] = du[:, s * width : (s + 1) * width]
+    rows = x_ref.shape[0]
+    size = rows // 2
+    width = o_ref.shape[1] // count
+    subs = [slice(i * size, (i + 1) * size) for i in range(2)]
+    y1, n, factor, h2, gu, dhid, hid, dgu, dh2, res = [[None, None] for _ in range(10)]
+
+    def first(i):
+        u = jnp.concatenate([r[subs[i], :] for r in us], 1)
+        uc_ref[subs[i], :] = u
+        y1[i] = x_ref[subs[i], :].astype(F32) + dot(u, o_ref[...], NT)
+
+    def normed(i):
+        factor[i] = lax.rsqrt(jnp.mean(y1[i] * y1[i], -1, keepdims=True) + EPS)
+        n[i] = y1[i] * factor[i]
+        h2[i] = (n[i] * gain).astype(BF)
+        h2_ref[subs[i], :] = h2[i]
+
+    def gates(i):
+        gu[i] = dot(h2[i], f_ref[:, : 2 * hidden])
+
+    def hidden_back(i):
+        dhid[i] = dot(cot_ref[subs[i], :], f_ref[:, 2 * hidden :])
+
+    def activated(i):
+        g, up = gu[i][:, :hidden], gu[i][:, hidden:]
+        sg = jax.nn.sigmoid(g)
+        act = g * sg
+        hid[i] = (act * up).astype(BF)
+        hid_ref[subs[i], :] = hid[i]
+        dg = dhid[i] * up * sg * (1.0 + g * (1.0 - sg))
+        dgu[i] = jnp.concatenate([dg.astype(BF), (dhid[i] * act).astype(BF)], 1)
+        dgu_ref[subs[i], :] = dgu[i]
+
+    def normed_back(i):
+        dh2[i] = dot(dgu[i], f_ref[:, : 2 * hidden], NT)
+
+    def part(i):
+        token = chunk * block + pl.program_id(0) * step_rows + i * size + rows_of((size, 1))
+        owned = (token >= at_ref[0] * own) & (token < (at_ref[0] + 1) * own)
+        total = dot(hid[i], f_ref[:, 2 * hidden :], NT) + jnp.where(owned, y1[i], 0.0)
+        part_ref[subs[i], :] = total.astype(BF)
+
+    def residual(i):
+        gmid_ref[i : i + 1, :] = jnp.sum(dh2[i] * n[i], 0, keepdims=True)
+        wd = gain * dh2[i]
+        back = factor[i] * (wd - n[i] * jnp.mean(wd * n[i], -1, keepdims=True))
+        res[i] = jnp.where(at_ref[0] == 0, back + cot_ref[subs[i], :].astype(F32), back).astype(BF)
+        res_ref[subs[i], :] = res[i]
+
+    def last(i):
+        du = dot(res[i], o_ref[...]).astype(BF)
+        for s in range(count):
+            dus[s][subs[i], :] = du[:, s * width : (s + 1) * width]
+
+    gmid_ref[...] = jnp.zeros_like(gmid_ref)
+    copies[0].wait()
+    first(0)
+    first(1)
+    copies[1].wait()
+    normed(0)
+    hidden_back(0)
+    gates(0)
+    normed(1)
+    hidden_back(1)
+    gates(1)
+    activated(0)
+    normed_back(0)
+    activated(1)
+    normed_back(1)
+    residual(0)
+    part(0)
+    last(0)
+    residual(1)
+    part(1)
+    last(1)
 
 
 def feed(chunk, block, own, place, x, cot, gains, o, f, us, kept):
@@ -276,8 +324,8 @@
     hidden = f.shape[1] // 3
     count = len(us)
     width = us[0].shape[1]
-    step_rows = min(256, block)
-    per = block // step_rows
+    step_rows = block
+    per = 1
 
     def mine(cols):
         return pl.BlockSpec((step_rows, cols), lambda i: (chunk * per + i, 0))
@@ -289,11 +337,12 @@
     return pl.pallas_call(
         functools.partial(ffn_kernel, count, chunk, block, step_rows, own),
         grid=(per,),
-        in_specs=[SMEM, mine(model), mine(model), full(gains.shape), full(o.shape), full(f.shape)]
+        in_specs=[SMEM, mine(model), mine(model), full(gains.shape), ANY, ANY]
         + [local(width)] * count + [ANY] * len(kept),
         out_specs=[mine(c) for c in kept_cols] + [local(width)] * count + [full((8, model))],
         out_shape=[jax.ShapeDtypeStruct((seq, c), BF) for c in kept_cols]
         + [jax.ShapeDtypeStruct((block, width), BF)] * count + [jax.ShapeDtypeStruct((8, model), F32)],
+        scratch_shapes=[pltpu.VMEM(o.shape, BF), pltpu.VMEM(f.shape, BF), pltpu.SemaphoreType.DMA((2,))],
         input_output_aliases={6 + count + i: i for i in range(len(kept))},
         compiler_params=params(),
         cost_estimate=COST,
@@ -302,9 +351,10 @@
 
 
 def bwd_kernel(
-    pair, heads, block, q_ref, aq_ref, k_ref, ak_ref, v_ref, og_ref, att_ref, li_ref, du_ref, ms_ref,
+    begin, heads, block, q_ref, aq_ref, k_ref, ak_ref, v_ref, og_ref, att_ref, li_ref, du_ref, ms_ref,
     dq_ref, dk_ref, dv_ref, dc_ref, da_s, ad_s,
 ):
+    pair = begin + pl.program_id(0)
     seq = q_ref.shape[0]
     count = seq // block
     lane = lanes((block, 128))
@@ -320,7 +370,11 @@
         ad_s[at, :] = jnp.where(third == 0, hi, jnp.where(third == 1, mid, rest))
     dk_ref[...] = jnp.zeros_like(dk_ref)
     dv_ref[...] = jnp.zeros_like(dv_ref)
-    dc_ref[...] = jnp.zeros_like(dc_ref)
+
+    @pl.when(pl.program_id(0) == 0)
+    def _():
+        dc_ref[...] = jnp.zeros_like(dc_ref)
+
 
     vone = jnp.where(lane < 6, ones, zero)
     for i in range(count):
@@ -338,36 +392,47 @@
             dah = jnp.where(mine, da, zero)
             daa = jnp.concatenate([dah, jnp.where((lane >= 3 * side) & (lane < 3 * side + 3), ad, zero)], 1)
             acc = jnp.zeros((block, 256), F32)
-            for j in range(i + 1):
-                to = slice(j * block, (j + 1) * block)
+
+            def pair_of(to, first):
+                size = to.stop - to.start
                 k = k_ref[to, :]
-                e = jnp.exp(dot(jnp.concatenate([k, ak_ref[to, :]], 1), qa, NT))
-                if j == i:
-                    e = jnp.where(rows_of(e.shape) <= lanes(e.shape), e, 0.0)
-                dv_ref[to, :] += dot(e.astype(BF), dah)
-                ds = (e * dot(jnp.concatenate([v_ref[to, :], vone], 1), daa, NT)).astype(BF)
-                dk = dot(ds, qo)
+                e = jnp.exp(dot(jnp.concatenate([k, ak_ref[to, :]], 1), qa[first:], NT))
+                if to.stop > i * block:
+                    shift = to.start - i * block - first
+                    e = jnp.where(rows_of(e.shape) + shift <= lanes(e.shape), e, 0.0)
+                dv_ref[to, :] += dot(e.astype(BF), dah[first:])
+                ds = (e * dot(jnp.concatenate([v_ref[to, :], vone[:size]], 1), daa[first:], NT)).astype(BF)
+                dk = dot(ds, qo[first:])
                 dk_ref[to, :] += dk[:, :128]
-                dc_ref[to, :] -= jnp.where(column, dk[:, 128:], 0.0)
-                acc = acc + dot(ds, jnp.concatenate([k, ones], 1), TN)
+                dc_ref[to, :] -= jnp.where(column[:size], dk[:, 128:], 0.0)
+                return dot(ds, jnp.concatenate([k, ones[:size]], 1), TN)
+
+            for j in range(i):
+                acc = acc + pair_of(slice(j * block, (j + 1) * block), 0)
+            half = block // 2
+            acc = acc + pair_of(slice(i * block, i * block + half), 0)
+            acc = jnp.concatenate(
+                [acc[:half], acc[half:] + pair_of(slice(i * block + half, (i + 1) * block), half)], 0
+            )
             dq.append(acc[:, :128])
             dc_ref[at, :] += jnp.where(column, acc[:, 128:], 0.0)
         dq_ref[at, :] = jnp.where(lane < 64, dq[0], dq[1]) * 0.125
 
 
-def attend_back(pair, block, heads, q8, aq, kn, ak, vl, og, att, li, du):
+def attend_back(begin, end, block, heads, q8, aq, kn, ak, vl, og, att, li, du):
     seq, width = q8.shape
     ms = np.zeros((256, 128))
     for lane in range(256):
         ms[lane, 3 * ((lane % 128) // 64) : 3 * ((lane % 128) // 64) + 3] = 1.0
-    mine = pl.BlockSpec((seq, 128), lambda p: (0, pair))
+    mine = pl.BlockSpec((seq, 128), lambda p: (0, begin + p))
+    own = pl.BlockSpec((seq, 128), lambda p: (0, p))
     one = pl.BlockSpec((seq, 128), lambda p: (0, 0))
     return pl.pallas_call(
-        functools.partial(bwd_kernel, pair, heads, block),
-        grid=(1,),
+        functools.partial(bwd_kernel, begin, heads, block),
+        grid=(end - begin,),
         in_specs=[mine, one, mine, one, mine, mine, mine, mine, mine, full((256, 128))],
-        out_specs=[one] * 4,
-        out_shape=[jax.ShapeDtypeStruct((seq, 128), F32)] * 4,
+        out_specs=[own, own, own, one],
+        out_shape=[jax.ShapeDtypeStruct((seq, 128 * (end - begin)), F32)] * 3 + [jax.ShapeDtypeStruct((seq, 128), F32)],
         scratch_shapes=[pltpu.VMEM((seq, 128), BF), pltpu.VMEM((seq, 128), BF)],
         compiler_params=params(),
         cost_estimate=COST,
@@ -376,15 +441,15 @@
 
 
 def post_kernel(
-    heads, pairs, q_ref, ks_ref, kd_ref, vd_ref, lg_ref, du_ref, att_ref, og_ref, x_ref,
+    heads, groups, q_ref, ks_ref, kd_ref, vd_ref, lg_ref, du_ref, att_ref, og_ref, x_ref,
     res_ref, gain_ref, w_ref, ba_ref, g64_ref, tri_ref, ms_ref, rows_ref, gqk_ref, *refs,
 ):
-    grads, refs = refs[: 4 * pairs], refs[4 * pairs :]
+    grads, refs = refs[: 4 * groups], refs[4 * groups :]
     dp_ref, gt_ref, g0_ref, gq_ref, gb_ref, carry_k, carry_v, carry_c = refs
     dq_raw, dk_raw, dvs = [
-        jnp.concatenate([r[...] for r in grads[i * pairs : (i + 1) * pairs]], 1) for i in range(3)
+        jnp.concatenate([r[...] for r in grads[i * groups : (i + 1) * groups]], 1) for i in range(3)
     ]
-    dc = sum(r[...] for r in grads[3 * pairs :])
+    dc = sum(r[...] for r in grads[3 * groups :])
     step = pl.program_id(0)
     rows, width = q_ref.shape
 
@@ -446,7 +511,7 @@
 
 def post(heads, dq, dk, dv, dc, q, ks, kd, vd, lg, du, att, og, x, res, gains, w, bias_row, gqk):
     seq, width = q.shape
-    pairs = len(dq)
+    groups = len(dq)
     model = x.shape[1]
     wide = w.shape[1]
     block = min(256, seq)
@@ -465,11 +530,11 @@
         return pl.BlockSpec((block, cols), lambda i: (count - 1 - i, 0))
 
     return pl.pallas_call(
-        functools.partial(post_kernel, heads, pairs),
+        functools.partial(post_kernel, heads, groups),
         grid=(count,),
         in_specs=[row(width)] * 4 + [row(128)] + [row(width)] * 3 + [row(model)] * 2
         + [full(gains.shape), full(w.shape), full(ba.shape), full(g64.shape), full(tri.shape),
-           full(ms.shape), full((8, 128)), full(gqk.shape)] + [row(128)] * (4 * pairs),
+           full(ms.shape), full((8, 128)), full(gqk.shape)] + [row(g.shape[1]) for g in dq + dk + dv + dc],
         out_specs=[row(wide), row(model), full((8, model)), full((8, width)), full((8, 128))],
         out_shape=[jax.ShapeDtypeStruct((seq, wide), BF), jax.ShapeDtypeStruct((seq, model), BF),
                    jax.ShapeDtypeStruct((8, model), F32), jax.ShapeDtypeStruct((8, width), F32),
@@ -539,6 +604,53 @@
     for (far, start), piece in sorted(pieces.items()):
         whole = lax.dynamic_update_slice_in_dim(whole, piece, (me ^ far) * cut + start, 0)
     return whole
+
+
+def cut_out(whole, me, far):
+    rows = whole.shape[0] // lax.axis_size("dp")
+    return lax.dynamic_slice_in_dim(whole, (me ^ far) * rows, rows, 0)
+
+
+def odd_rows(whole, me):
+    return jnp.concatenate([cut_out(whole, me, r) for r in range(1, lax.axis_size("dp"), 2)], 0)
+
+
+def scatter_2_add(whole, got, me):
+    size = lax.axis_size("dp")
+    rows = whole.shape[0] // size
+    return {r: add(cut_out(whole, me, r), got[rows * (r // 2) : rows * (r // 2 + 1)]) for r in range(0, size, 2)}
+
+
+def scatter_2_send(pieces):
+    pieces = dict(pieces)
+    if lax.axis_size("dp") == 8:
+        half = pieces[0].shape[0] // 2
+        pieces[-1] = swap(pieces[6][:half], "dp", 2)
+        pieces[-2] = swap(pieces[6][half:], "dp", 4)
+    return pieces
+
+
+def scatter_3_add(pieces):
+    if lax.axis_size("dp") == 8:
+        half = pieces[0].shape[0] // 2
+        to_y = jnp.concatenate([add(pieces[4][:half], pieces[-1]), pieces[4][half:]], 0)
+        to_x = jnp.concatenate([pieces[2][:half], add(pieces[2][half:], pieces[-2])], 0)
+        return {0: pieces[0], 2: to_x, 4: to_y}
+    return pieces
+
+
+def scatter_3_send(pieces):
+    size = lax.axis_size("dp")
+    if size == 8:
+        return [pieces[0], swap(pieces[2], "dp", 2), swap(pieces[4], "dp", 4)]
+    for bit in reversed(high_bits(size)):
+        got = {r: swap(pieces[r], "dp", bit) for r in pieces if r & bit}
+        pieces = {r: add(p, got[r | bit]) for r, p in pieces.items() if not r & bit}
+    return [pieces[0]]
+
+
+def rows_major(value):
+    return with_layout_constraint(value, Layout(major_to_minor=(0, 1)))
 
 
 def scatter(whole):
@@ -647,19 +759,22 @@
         if 0 <= chunk < chunks:
             outs = feed(chunk, block, own, at, x, cot, gains, out_all, ffn_all, us[chunk], kept_ffn)
             kept_ffn, parts[chunk] = outs[:6], outs[6:-1]
-            gmids.append(outs[-1][0:1])
+            gmids.append(outs[-1][0:1] + outs[-1][1:2])
         h2, hid, dgu, res, uc, part = kept_ffn if kept_ffn else [None] * 6
         if t == made + first - 1:
             y_acc = turn(y_send)
-        fill = None
-        for i, pair in enumerate(((res, uc), (h2, dgu), (cot, hid))):
-            if t == made + i:
-                fill = product(*pair)
+        fill = []
+        if t == made:
+            fill = [product(res, uc), rows_major(product(cot, hid))]
+        if t == made + 1:
+            fill = [product(h2, dgu)]
+        out_q, out_p = out_p, None if t == 0 else out_p
         new_u, new_du, fresh, kept_att, kept_ffn, parts, fill, out_p, out_all, q8 = tie(
             (new_u, new_du, fresh, kept_att, kept_ffn, parts, fill, out_p, out_all, q8)
         )
-        if fill is not None:
-            sums.append(scatter(fill))
+        if t == 0:
+            out_p = out_q
+        sums += [scatter(value) for value in fill]
         for c, value in new_u.items():
             us[c].append(value)
         if fresh is not None:
@@ -673,20 +788,30 @@
     pairs, back_parts = width // 128, []
     cuts = [0, 1, pairs] if pairs > 1 else [0, pairs]
     y_step = 2
+    ring = out_acc = None
     for begin, end in zip(cuts, cuts[1:]):
-        for pair in range(begin, end):
-            back_parts.append(attend_back(pair, block, heads, q8, aq, kn, ak, vl, og, att, li, du))
-        y_acc, back_parts = tie((y_acc, back_parts))
+        back_parts.append(attend_back(begin, end, block, heads, q8, aq, kn, ak, vl, og, att, li, du))
+        y_acc, back_parts, out_acc = tie((y_acc, back_parts, out_acc))
         if y_step < tp:
+            if ring is None:
+                ring = [sums[0][:, i * width : (i + 1) * width] for i in range(tp)]
+                out_send, out_step = ring[1], 2
+            else:
+                out_send, out_step = add(out_acc, ring[out_step]), out_step + 1
             send, y_step = add(y_acc, token_part(part, y_step)), y_step + 1
-            send, du = tie((send, du))
-            y_acc = turn(send)
+            send, du, out_send = tie((send, du, out_send))
+            y_acc, out_acc = turn(send), turn(out_send)
     dq, dk, dv, dc = zip(*back_parts)
     dp_all, gt, g0, gq, gb = post(
         heads, dq, dk, dv, dc, q, ks, kd, vd, lg, du, att, og, x, res, gains, w, bias_row, gqk
     )
-    y_acc, dp_all, gt, g0 = tie((y_acc, dp_all, gt, g0))
-
+    y_acc, dp_all, gt, g0, out_acc = tie((y_acc, dp_all, gt, g0, out_acc))
+
+    send = token_part(gt, 1)
+    send, dp_all, y_acc, out_acc = tie((send, dp_all, y_acc, out_acc))
+    back = turn(send)
+    attn_s = product(hn, dp_all)
+    odd = odd_rows(attn_s, me_d)
     gq = gq[0:2].reshape(2, heads, 64).sum(1)
     gb = lax.dynamic_update_slice_in_dim(
         jnp.zeros(forget_bias.shape, F32), gb[0, 2 * heads : 2 * heads + heads_real], me_t * heads_real, 0
@@ -694,27 +819,43 @@
     small = jnp.concatenate([gq.reshape(-1), gb])
     small = jnp.pad(small, (0, model - small.shape[0]))[None]
     flat = jnp.concatenate([g0[0:1], gmid, small, jnp.zeros((5, model), F32)], 0)
-    ring = [sums[0][:, i * width : (i + 1) * width] for i in range(tp)]
-    low, high = slice(0, model // 2), slice(model // 2, model)
-    send, out_send = [token_part(gt[:, cols], 1) for cols in (low, high)], ring[1]
-    send, out_send, flat, dp_all = tie((send, out_send, flat, dp_all))
+    back, attn_s, odd, flat = tie((back, attn_s, odd, flat))
     while y_step < tp:
         y_acc, y_step = turn(add(y_acc, token_part(part, y_step))), y_step + 1
-    back = [turn(value) for value in send]
-    fill = product(hn, dp_all)
-    back, fill = tie((back, fill))
-    sums.append(scatter(fill))
+    across = [1 << i for i in range(tp.bit_length() - 1)]
+    along = [1 << i for i in range(dp.bit_length() - 1)]
+    stage = 0
     for s in range(2, tp):
-        back = [turn(add(value, token_part(gt[:, cols], s))) for value, cols in zip(back, (low, high))]
-    out_acc = turn(out_send)
-    for s in range(2, tp):
-        out_acc = turn(add(out_acc, ring[s]))
-    for axis, size in (("tp", tp), ("dp", dp)):
-        for bit in range(size.bit_length() - 1):
-            flat = flat + swap(flat, axis, 1 << bit)
-    result = total_of((y_acc, token_part(part, 0))).astype(BF)
-    grad_tokens = total_of((token_part(gt, 0), jnp.concatenate(back, 1)))
-    grad_gu, grad_down, grad_attn = [value.astype(F32) for value in sums[1:]]
+        send, out_send = add(back, token_part(gt, s)), None
+        if out_step < tp:
+            out_send, out_step = add(out_acc, ring[out_step]), out_step + 1
+        if stage == 1:
+            attn_s = scatter_3_add(attn_s)
+        send, flat, out_send, attn_s, odd = tie((send, flat, out_send, attn_s, odd))
+        back = turn(send)
+        if out_send is not None:
+            out_acc = turn(out_send)
+        if stage == 0:
+            attn_s, stage = scatter_2_send(scatter_2_add(attn_s, swap(odd, "dp", 1), me_d)), 1
+        elif stage == 1:
+            attn_s, stage = scatter_3_send(attn_s), 2
+        for axis, bits in (("dp", along), ("tp", across)):
+            for _ in range(2):
+                if bits and (axis == "dp" or s > 2):
+                    flat = flat + swap(flat, axis, bits.pop(0))
+                    break
+        back, flat, out_acc, attn_s = tie((back, flat, out_acc, attn_s))
+    while out_step < tp:
+        out_acc, out_step = turn(add(out_acc, ring[out_step])), out_step + 1
+    if stage == 1:
+        attn_s = scatter_3_send(scatter_3_add(attn_s))
+    for axis, bits in (("dp", along), ("tp", across)):
+        for bit in bits:
+            flat = flat + swap(flat, axis, bit)
+    result, back, gt = tie((total_of((y_acc, token_part(part, 0))).astype(BF), back, gt))
+    grad_tokens = total_of((token_part(gt, 0), back))
+    grad_attn = total_of(attn_s)
+    grad_down, grad_gu = [value.astype(F32) for value in sums[1:]]
     grad_out_own = total_of((ring[0], out_acc))
     norm_grad = flat[0:2]
     qk_grad = flat[2, : 2 * 64].reshape(2, 64)

time: 526 us -> 500 us (0.951); the launches traced: 516 us -> 496 us
  local copies, waits for them, and re-layouts: 47.1 us -> 30.1 us
  starting transfers between devices: 59.5 us -> 44.8 us
  waiting for transfers between devices: 122 us -> 134 us
    ppermute x23 -> x28, waiting for transfers between devices: 19.8 us -> 37 us  [swap(): return lax.ppermute(value, axis, [(i, i ^ bit) for i in range(size)])]
    ppermute x33 -> x30, starting transfers between devices: 43.4 us -> 27.8 us  [turn(): return lax.ppermute(value, 'tp', [(i, (i + 1) % size) for i in range(size)])]
    unnamed x75 -> x72, local copies, waits for them, and re-layouts: 10.8 us -> 2.3 us
    ppermute x33 -> x30, waiting for transfers between devices: 101 us -> 96.8 us  [turn(): return lax.ppermute(value, 'tp', [(i, (i + 1) % size) for i in range(size)])]
    pallas_call x4 -> x3, Pallas kernels: 65 us -> 61.4 us  [the longest x2 35.6 us: attend_back(): pl.pallas_call(functools.partial(bwd_kernel, begin, heads, block), grid=(...]
    convert_element_type x16 -> x17, other arithmetic: 16.5 us -> 18.6 us  [add(): return (a.astype(F32) + b.astype(F32)).astype(BF)]
    ppermute x23 -> x28, starting transfers between devices: 15.7 us -> 16.9 us  [swap(): return lax.ppermute(value, axis, [(i, i ^ bit) for i in range(size)])]
  transfers between devices with their start and end apart: 61 -> 62, of which waited for: 26 -> 27; matrix products, arithmetic and copies ran while one was open for 24% -> 22% of each run, Pallas kernels for 36% -> 37%
where the time goes in v3:
time: 500 us; the launch traced here: 496 us
  Pallas kernels  182 us (36%)
  waiting for transfers between devices  134 us (27%)
  matrix products  48.6 us (10%)
  starting transfers between devices  44.8 us (9%)
  other arithmetic  40.7 us (8%)
  local copies, waits for them, and re-layouts  30.1 us (6%)
  between operations  15.4 us (3%)
    ppermute x30, waiting for transfers between devices, turn(): return lax.ppermute(value, 'tp', [(i, (i + 1) % size) for i in range(size)])  96.8 us
    pallas_call x3, Pallas kernels, feed(): pl.pallas_call(functools.partial(ffn_kernel, count, chunk, block, step_ro...  77.3 us
    dot_general x4, matrix products, dot(): return lax.dot_general(a, b, dims, preferred_element_type=F32)  48.6 us
    ppermute x28, waiting for transfers between devices, swap(): return lax.ppermute(value, axis, [(i, i ^ bit) for i in range(size)])  37 us
    pallas_call x2, Pallas kernels, attend_back(): pl.pallas_call(functools.partial(bwd_kernel, begin, heads, block), grid=(...  35.6 us
    ppermute x30, starting transfers between devices, turn(): return lax.ppermute(value, 'tp', [(i, (i + 1) % size) for i in range(size)])  27.8 us
    pallas_call x1, Pallas kernels, post(): pl.pallas_call(functools.partial(post_kernel, heads, groups), grid=(count...  25.8 us
    pallas_call x1, Pallas kernels, pre(): pl.pallas_call(functools.partial(pre_kernel, heads, spots), grid=(seq //...  23.2 us
  transfers between devices with their start and end apart: 62, of which 27 were waited for; matrix products, arithmetic and copies ran while one was open for 22% of the time, Pallas kernels for 37%

profile of v3, /device:TPU:0, one launch (start us, length us, event | category | flops | bytes accessed | tf_op | source)
XLA Modules:
  0.0 496.0 jit_solution(11181922391080711807)
XLA Ops:
  16.3 6.0 %collective-permute-done.3 = bf16[192,384]{1,0:T(8,128)(2,1)} collective-permute-done((bf16[192,384]{1,0:T(8,128)(2,1)S(1)}, bf16[192,384]{1,0:T(8,128)(2,1)}, u32[]{:S(2)}, u32[]{:S(2)}) %collective-permute-start.3) | collective-permute-done | bytes 147488 | tf_op jit(solution)/shard_map/ppermute | solution.py:557
  23.4 6.0 %collective-permute-done.4 = bf16[192,384]{1,0:T(8,128)(2,1)S(1)} collective-permute-done((bf16[192,384]{1,0:T(8,128)(2,1)}, bf16[192,384]{1,0:T(8,128)(2,1)S(1)}, u32[]{:S(2)}, u32[]{:S(2)}) %collective-permute-start.4) | collective-permute-done | bytes 147488 | tf_op jit(solution)/shard_map/ppermute | solution.py:557
  33.9 5.5 %collective-permute-done.9 = bf16[192,384]{1,0:T(8,128)(2,1)S(1)} collective-permute-done((bf16[192,384]{1,0:T(8,128)(2,1)S(1)}, bf16[192,384]{1,0:T(8,128)(2,1)S(1)}, u32[]{:S(2)}, u32[]{:S(2)}) %collective-permute-start.9) | collective-permute-done | bytes 147488 | tf_op jit(solution)/shard_map/ppermute | solution.py:557
  48.6 23.2 %pre.1 = (bf16[1536,1536]{1,0:T(8,128)(2,1)}, bf16[1536,1664]{1,0:T(8,128)(2,1)}, f32[8,1536]{1,0:T(8,128)}, bf16[1536,384]{1,0:T(8,128)(2,1)}, bf16[1536,384]{1...) custom-call(s32[1]{0:T(128)} %bitcast.me_ref, ...), custom_call_target="tpu_custom_call" | custom-call | flops 1 | bytes 1 | tf_op jit(solution)/shard_map/pre/pallas_call | solution.py:158
  84.0 6.3 %attend.4 = (bf16[512,384]{1,0:T(8,128)(2,1)}, f32[1536,384]{1,0:T(8,128)}, f32[1536,384]{1,0:T(8,128)}) custom-call(bf16[1536,384]{1,0:T(8,128)(2,1)} %get-tuple-element.601.q_ref, bf16[1536,128]{1,0:T(8,128)(2,1)} %get-tuple-element.388.aq_ref, bf16[1536,384]{1,0:T(8,128)(2,1)} %get-tuple-element.389.k_ref, ...), custom_call_target="tpu_custom_call", output_to_operand_aliasing={{1}: (6, {}), {2}: (7, {})} | custom-call | flops 1 | bytes 1 | tf_op jit(solution)/shard_map/attend/pallas_call | solution.py:218
  98.6 8.9 %attend.5 = (bf16[512,384]{1,0:T(8,128)(2,1)}, f32[1536,384]{1,0:T(8,128)}, f32[1536,384]{1,0:T(8,128)}) custom-call(bf16[1536,384]{1,0:T(8,128)(2,1)} %get-tuple-element.601.q_ref, bf16[1536,128]{1,0:T(8,128)(2,1)} %get-tuple-element.388.aq_ref, bf16[1536,384]{1,0:T(8,128)(2,1)} %get-tuple-element.389.k_ref, ...), custom_call_target="tpu_custom_call", output_to_operand_aliasing={{1}: (6, {}), {2}: (7, {})} | custom-call | flops 1 | bytes 1 | tf_op jit(solution)/shard_map/attend/pallas_call | solution.py:218
  128.9 6.0 %collective-permute-done.25.refs_2_ = bf16[512,384]{1,0:T(8,128)(2,1)} collective-permute-done((bf16[512,384]{1,0:T(8,128)(2,1)S(1)}, bf16[512,384]{1,0:T(8,128)(2,1)}, u32[]{:S(2)}, u32[]{:S(2)}) %collective-permute-start.25) | collective-permute-done | bytes 393248 | tf_op jit(solution)/shard_map/ppermute | solution.py:557
  134.9 5.5 %collective-permute-done.26.refs_1_ = bf16[512,384]{1,0:T(8,128)(2,1)} collective-permute-done((bf16[512,384]{1,0:T(8,128)(2,1)}, bf16[512,384]{1,0:T(8,128)(2,1)}, u32[]{:S(2)}, u32[]{:S(2)}) %collective-permute-start.26) | collective-permute-done | bytes 393248 | tf_op jit(solution)/shard_map/ppermute | solution.py:557
  141.9 31.9 %feed.3 = (bf16[1536,1536]{1,0:T(8,128)(2,1)}, bf16[1536,1024]{1,0:T(8,128)(2,1)}, bf16[1536,2048]{1,0:T(8,128)(2,1)}, bf16[1536,1536]{1,0:T(8,128)(2,1)}, bf16[...) custom-call(s32[1]{0:T(128)} %bitcast.12.at_ref, ...), custom_call_target="tpu_custom_call" | custom-call | flops 1 | bytes 1 | tf_op jit(solution)/shard_map/feed/pallas_call | solution.py:337
  177.6 22.8 %feed.4 = (bf16[1536,1536]{1,0:T(8,128)(2,1)}, bf16[1536,1024]{1,0:T(8,128)(2,1)}, bf16[1536,2048]{1,0:T(8,128)(2,1)}, bf16[1536,1536]{1,0:T(8,128)(2,1)}, bf16[...) custom-call(s32[1]{0:T(128)} %bitcast.12.at_ref, ...), custom_call_target="tpu_custom_call", output_to_operand_aliasing={{0}: (10, {}), {1}: (11, {}), {2}: (12, {}), {3}: (13, {}),... | custom-call | flops 1 | bytes 1 | tf_op jit(solution)/shard_map/feed/pallas_call | solution.py:337
  201.9 22.6 %feed.5 = (bf16[1536,1536]{1,0:T(8,128)(2,1)}, bf16[1536,1024]{1,0:T(8,128)(2,1)}, bf16[1536,2048]{1,0:T(8,128)(2,1)}, bf16[1536,1536]{1,0:T(8,128)(2,1)}, bf16[...) custom-call(s32[1]{0:T(128)} %bitcast.12.at_ref, ...), custom_call_target="tpu_custom_call", output_to_operand_aliasing={{0}: (10, {}), {1}: (11, {}), {2}: (12, {}), {3}: (13, {}),... | custom-call | flops 1 | bytes 1 | tf_op jit(solution)/shard_map/feed/pallas_call | solution.py:337
  229.3 12.3 %convolution_convert_fusion.2 = bf16[1536,1536]{1,0:T(8,128)(2,1)} fusion(bf16[1536,1536]{1,0:T(8,128)(2,1)} %get-tuple-element.642.res_ref, bf16[1536,1536]{1,0:T(8,128)(2,1)} %get-tuple-element.553), kind=kOutput, calls=%fused_computation.2 | convolution fusion | flops 7250116608 | bytes 14155776 | tf_op jit(solution)/shard_map/dot_general | solution.py:24
  241.6 8.9 %fusion = bf16[1536,1024]{1,0:T(8,128)(2,1)} fusion(bf16[1536,1024]{1,0:T(8,128)(2,1)S(1)} %copy-done, bf16[1,1536,1536]{2,1,0:T(8,128)(2,1)} %param.36), kind=kOutput, calls=%fused_computation.4 | convolution fusion | flops 4833411072 | bytes 11010048 | tf_op jit(solution)/shard_map/dot_general | solution.py:24
  256.5 15.2 %convolution_convert_fusion.1 = bf16[1536,2048]{1,0:T(8,128)(2,1)} fusion(bf16[1536,1536]{1,0:T(8,128)(2,1)} %get-tuple-element.576, bf16[1536,2048]{1,0:T(8,128)(2,1)} %get-tuple-element.577), kind=kOutput, calls=%fused_computation.1 | convolution fusion | flops 9666822144 | bytes 17301504 | tf_op jit(solution)/shard_map/dot_general | solution.py:24
  278.3 9.9 %collective-permute-done.39 = bf16[512,384]{1,0:T(8,128)(2,1)S(1)} collective-permute-done((bf16[512,384]{1,0:T(8,128)(2,1)S(1)}, bf16[512,384]{1,0:T(8,128)(2,1)S(1)}, u32[]{:S(2)}, u32[]{:S(2)}) %collective-permute-start.39) | collective-permute-done | bytes 393248 | tf_op jit(solution)/shard_map/ppermute | solution.py:557
  290.7 12.7 %attend_back.2 = (f32[1536,128]{1,0:T(8,128)}, f32[1536,128]{1,0:T(8,128)}, f32[1536,128]{1,0:T(8,128)}, f32[1536,128]{1,0:T(8,128)}) custom-call(bf16[1536,384]{1,0:T(8,128)(2,1)} %get-tuple-element.601.q_ref, bf16[1536,128]{1,0:T(8,128)(2,1)} %get-tuple-element.388.aq_ref, bf16[1536,384]{1,0:T(8,128)(2,1)} %get-tuple-element.389.k_ref, ...), custom_call_target="tpu_custom_call" | custom-call | flops 1 | bytes 1 | tf_op jit(solution)/shard_map/attend_back/pallas_call | solution.py:430
  313.0 22.9 %attend_back.3 = (f32[1536,256]{1,0:T(8,128)}, f32[1536,256]{1,0:T(8,128)}, f32[1536,256]{1,0:T(8,128)}, f32[1536,128]{1,0:T(8,128)}) custom-call(bf16[1536,384]{1,0:T(8,128)(2,1)} %get-tuple-element.601.q_ref, bf16[1536,128]{1,0:T(8,128)(2,1)} %get-tuple-element.388.aq_ref, bf16[1536,384]{1,0:T(8,128)(2,1)} %get-tuple-element.389.k_ref, ...), custom_call_target="tpu_custom_call" | custom-call | flops 1 | bytes 1 | tf_op jit(solution)/shard_map/attend_back/pallas_call | solution.py:430
  335.9 6.4 %collective-permute-done.41 = bf16[192,384]{1,0:T(8,128)(2,1)S(1)} collective-permute-done((bf16[192,384]{1,0:T(8,128)(2,1)S(1)}, bf16[192,384]{1,0:T(8,128)(2,1)S(1)}, u32[]{:S(2)}, u32[]{:S(2)}) %collective-permute-start.41) | collective-permute-done | bytes 147488 | tf_op jit(solution)/shard_map/ppermute | solution.py:557
  346.3 25.8 %post.1 = (bf16[1536,1664]{1,0:T(8,128)(2,1)}, bf16[1536,1536]{1,0:T(8,128)(2,1)}, f32[8,1536]{1,0:T(8,128)}, f32[8,384]{1,0:T(8,128)}, f32[8,128]{1,0:T(8,128)}) custom-call(bf16[1536,384]{1,0:T(8,128)(2,1)} %get-tuple-element.635.q_ref, bf16[1536,384]{1,0:T(8,128)(2,1)} %get-tuple-element.636.ks_ref, bf16[1536,384]{1,0:T(8,128)(2,1)} %get-tuple-element.637.kd_ref, ...), custom_call_target="tpu_custom_call" | custom-call | flops 1 | bytes 1 | tf_op jit(solution)/shard_map/post/pallas_call | solution.py:532
  377.2 12.3 %convolution_convert_fusion = bf16[1536,1664]{1,0:T(8,128)(2,1)S(1)} fusion(bf16[1536,1536]{1,0:T(8,128)(2,1)} %get-tuple-element.662, bf16[1536,1664]{1,0:T(8,128)(2,1)} %get-tuple-element.663), kind=kOutput, calls=%fused_computation | convolution fusion | flops 7854292992 | bytes 14942208 | tf_op jit(solution)/shard_map/dot_general | solution.py:24
  392.4 11.6 %collective-permute-done.44 = bf16[384,1536]{1,0:T(8,128)(2,1)S(1)} collective-permute-done((bf16[384,1536]{1,0:T(8,128)(2,1)S(1)}, bf16[384,1536]{1,0:T(8,128)(2,1)S(1)}, u32[]{:S(2)}, u32[]{:S(2)}) %collective-permute-start.44) | collective-permute-done | bytes 1179680 | tf_op jit(solution)/shard_map/ppermute | solution.py:557
  416.3 23.8 %collective-permute-done.47 = bf16[192,384]{1,0:T(8,128)(2,1)} collective-permute-done((bf16[192,384]{1,0:T(8,128)(2,1)}, bf16[192,384]{1,0:T(8,128)(2,1)}, u32[]{:S(2)}, u32[]{:S(2)}) %collective-permute-start.47) | collective-permute-done | bytes 147488 | tf_op jit(solution)/shard_map/ppermute | solution.py:557
  455.1 11.1 %collective-permute-done.52 = f32[8,1536]{1,0:T(8,128)S(1)} collective-permute-done((f32[8,1536]{1,0:T(8,128)S(1)}, f32[8,1536]{1,0:T(8,128)S(1)}, u32[]{:S(2)}, u32[]{:S(2)}) %collective-permute-start.52) | collective-permute-done | bytes 49184 | tf_op jit(solution)/shard_map/ppermute | solution.py:552
  467.6 10.1 %collective-permute-done.53 = f32[8,1536]{1,0:T(8,128)S(1)} collective-permute-done((f32[8,1536]{1,0:T(8,128)S(1)}, f32[8,1536]{1,0:T(8,128)S(1)}, u32[]{:S(2)}, u32[]{:S(2)}) %collective-permute-start.53) | collective-permute-done | bytes 49184 | tf_op jit(solution)/shard_map/ppermute | solution.py:552
  (283 shorter events, 152.8 us)
Async XLA Ops:
  7.2 134.7 %all-gather.2.cloned.1.call-start = ((), (), s32[]{:S(2)}) async-start(), calls=%async_computation.3 | async-start | bytes 10616832 | tf_op jit(solution)/shard_map/all_gather | solution.py:724
  42.8 266.8 %reduce-scatter.4.cloned.1.call-start = ((), (), s32[]{:S(2)}) async-start(), calls=%async_computation.4 | async-start | bytes 5308416 | tf_op jit(solution)/shard_map/reduce_scatter | solution.py:657
  42.9 28.9 %collective-permute-start.12 = (bf16[192,1536]{1,0:T(8,128)(2,1)S(1)}, bf16[192,1536]{1,0:T(8,128)(2,1)}, u32[]{:S(2)}, u32[]{:S(2)}) collective-permute-start(bf16[192,1536]{1,0:T(8,128)(2,1)S(1)} %pad_maximum_fusion.6), channel_id=1, source_target_pairs={{0,4},{4,0},{8,12},{12,8},{16,20},{20,16},{24,28},{28,24},{1,5},{5... | collective-permute-start | bytes 1769480 | tf_op jit(solution)/shard_map/ppermute | solution.py:552
  42.9 28.9 %collective-permute-start.13 = (bf16[192,1536]{1,0:T(8,128)(2,1)S(1)}, bf16[192,1536]{1,0:T(8,128)(2,1)S(1)}, u32[]{:S(2)}, u32[]{:S(2)}) collective-permute-start(bf16[192,1536]{1,0:T(8,128)(2,1)S(1)} %pad_maximum_fusion.6), channel_id=1, source_target_pairs={{0,8},{4,12},{8,0},{12,4},{16,24},{20,28},{24,16},{28,20},{1,9},{5... | collective-permute-start | bytes 1769480 | tf_op jit(solution)/shard_map/ppermute | solution.py:552
  43.5 28.3 %collective-permute-start.14 = (bf16[192,1536]{1,0:T(8,128)(2,1)S(1)}, bf16[192,1536]{1,0:T(8,128)(2,1)S(1)}, u32[]{:S(2)}, u32[]{:S(2)}) collective-permute-start(bf16[192,1536]{1,0:T(8,128)(2,1)S(1)} %pad_maximum_fusion.6), channel_id=1, source_target_pairs={{0,16},{4,20},{8,24},{12,28},{16,0},{20,4},{24,8},{28,12},{1,17},{... | collective-permute-start | bytes 1769480 | tf_op jit(solution)/shard_map/ppermute | solution.py:552
  113.6 26.9 %collective-permute-start.26 = (bf16[512,384]{1,0:T(8,128)(2,1)}, bf16[512,384]{1,0:T(8,128)(2,1)}, u32[]{:S(2)}, u32[]{:S(2)}) collective-permute-start(bf16[512,384]{1,0:T(8,128)(2,1)} %get-tuple-element.420.refs_0_), channel_id=1, source_target_pairs={{0,1},{1,2},{2,3},{3,0},{4,5},{5,6},{6,7},{7,4},{8,9},{9,10},{10,1... | collective-permute-start | bytes 1179656 | tf_op jit(solution)/shard_map/ppermute | solution.py:557
  140.4 33.3 %collective-permute-start.27 = (bf16[512,384]{1,0:T(8,128)(2,1)}, bf16[512,384]{1,0:T(8,128)(2,1)S(1)}, u32[]{:S(2)}, u32[]{:S(2)}) collective-permute-start(bf16[512,384]{1,0:T(8,128)(2,1)} %collective-permute-done.25.refs_2_), channel_id=1, source_target_pairs={{0,1},{1,2},{2,3},{3,0},{4,5},{5,6},{6,7},{7,4},{8,9},{9,10},{10,1... | collective-permute-start | bytes 1179656 | tf_op jit(solution)/shard_map/ppermute | solution.py:557
  140.4 33.4 %collective-permute-start.28 = (bf16[512,384]{1,0:T(8,128)(2,1)}, bf16[512,384]{1,0:T(8,128)(2,1)S(1)}, u32[]{:S(2)}, u32[]{:S(2)}) collective-permute-start(bf16[512,384]{1,0:T(8,128)(2,1)} %collective-permute-done.26.refs_1_), channel_id=1, source_target_pairs={{0,1},{1,2},{2,3},{3,0},{4,5},{5,6},{6,7},{7,4},{8,9},{9,10},{10,1... | collective-permute-start | bytes 1179656 | tf_op jit(solution)/shard_map/ppermute | solution.py:557
  173.8 26.7 %collective-permute-start.30 = (bf16[512,384]{1,0:T(8,128)(2,1)}, bf16[512,384]{1,0:T(8,128)(2,1)S(1)}, u32[]{:S(2)}, u32[]{:S(2)}) collective-permute-start(bf16[512,384]{1,0:T(8,128)(2,1)} %get-tuple-element.467), channel_id=1, source_target_pairs={{0,1},{1,2},{2,3},{3,0},{4,5},{5,6},{6,7},{7,4},{8,9},{9,10},{10,1... | collective-permute-start | bytes 1179656 | tf_op jit(solution)/shard_map/ppermute | solution.py:557
  252.9 194.2 %reduce-scatter.8.cloned.1.call-start = ((), (), s32[]{:S(2)}) async-start(), calls=%async_computation.6 | async-start | bytes 3538944 | tf_op jit(solution)/shard_map/reduce_scatter | solution.py:657
  271.8 181.2 %reduce-scatter.6.cloned.1.call-start = ((), (), s32[]{:S(2)}) async-start(), calls=%async_computation.5 | async-start | bytes 7077888 | tf_op jit(solution)/shard_map/reduce_scatter | solution.py:657
  275.6 32.4 %collective-permute-start.38 = (bf16[384,1536]{1,0:T(8,128)(2,1)S(1)}, bf16[384,1536]{1,0:T(8,128)(2,1)S(1)}, u32[]{:S(2)}, u32[]{:S(2)}) collective-permute-start(bf16[384,1536]{1,0:T(8,128)(2,1)S(1)} %constant_dynamic-slice_fusion.5), channel_id=1, source_target_pairs={{0,1},{1,2},{2,3},{3,0},{4,5},{5,6},{6,7},{7,4},{8,9},{9,10},{10,1... | collective-permute-start | bytes 3538952 | tf_op jit(solution)/shard_map/ppermute | solution.py:557
  310.5 31.8 %collective-permute-start.40 = (bf16[384,1536]{1,0:T(8,128)(2,1)S(1)}, bf16[384,1536]{1,0:T(8,128)(2,1)S(1)}, u32[]{:S(2)}, u32[]{:S(2)}) collective-permute-start(bf16[384,1536]{1,0:T(8,128)(2,1)S(1)} %add_convert_fusion.4), channel_id=1, source_target_pairs={{0,1},{1,2},{2,3},{3,0},{4,5},{5,6},{6,7},{7,4},{8,9},{9,10},{10,1... | collective-permute-start | bytes 3538952 | tf_op jit(solution)/shard_map/ppermute | solution.py:557
  311.1 31.2 %collective-permute-start.41 = (bf16[192,384]{1,0:T(8,128)(2,1)S(1)}, bf16[192,384]{1,0:T(8,128)(2,1)S(1)}, u32[]{:S(2)}, u32[]{:S(2)}) collective-permute-start(bf16[192,384]{1,0:T(8,128)(2,1)S(1)} %slice.144), channel_id=1, source_target_pairs={{0,1},{1,2},{2,3},{3,0},{4,5},{5,6},{6,7},{7,4},{8,9},{9,10},{10,1... | collective-permute-start | bytes 442376 | tf_op jit(solution)/shard_map/ppermute | solution.py:557
  344.9 30.8 %collective-permute-start.42 = (bf16[384,1536]{1,0:T(8,128)(2,1)S(1)}, bf16[384,1536]{1,0:T(8,128)(2,1)S(1)}, u32[]{:S(2)}, u32[]{:S(2)}) collective-permute-start(bf16[384,1536]{1,0:T(8,128)(2,1)S(1)} %add_convert_fusion.3), channel_id=1, source_target_pairs={{0,1},{1,2},{2,3},{3,0},{4,5},{5,6},{6,7},{7,4},{8,9},{9,10},{10,1... | collective-permute-start | bytes 3538952 | tf_op jit(solution)/shard_map/ppermute | solution.py:557
  345.0 30.7 %collective-permute-start.43 = (bf16[192,384]{1,0:T(8,128)(2,1)S(1)}, bf16[192,384]{1,0:T(8,128)(2,1)S(1)}, u32[]{:S(2)}, u32[]{:S(2)}) collective-permute-start(bf16[192,384]{1,0:T(8,128)(2,1)S(1)} %add_convert_fusion.21), channel_id=1, source_target_pairs={{0,1},{1,2},{2,3},{3,0},{4,5},{5,6},{6,7},{7,4},{8,9},{9,10},{10,1... | collective-permute-start | bytes 442376 | tf_op jit(solution)/shard_map/ppermute | solution.py:557
  377.1 26.8 %collective-permute-start.44 = (bf16[384,1536]{1,0:T(8,128)(2,1)S(1)}, bf16[384,1536]{1,0:T(8,128)(2,1)S(1)}, u32[]{:S(2)}, u32[]{:S(2)}) collective-permute-start(bf16[384,1536]{1,0:T(8,128)(2,1)S(1)} %constant_dynamic-slice_fusion.4), channel_id=1, source_target_pairs={{0,1},{1,2},{2,3},{3,0},{4,5},{5,6},{6,7},{7,4},{8,9},{9,10},{10,1... | collective-permute-start | bytes 3538952 | tf_op jit(solution)/shard_map/ppermute | solution.py:557
  406.5 33.7 %collective-permute-start.45 = (bf16[384,1536]{1,0:T(8,128)(2,1)}, bf16[384,1536]{1,0:T(8,128)(2,1)}, u32[]{:S(2)}, u32[]{:S(2)}) collective-permute-start(bf16[384,1536]{1,0:T(8,128)(2,1)} %add_convert_fusion.1), channel_id=1, source_target_pairs={{0,1},{1,2},{2,3},{3,0},{4,5},{5,6},{6,7},{7,4},{8,9},{9,10},{10,1... | collective-permute-start | bytes 3538952 | tf_op jit(solution)/shard_map/ppermute | solution.py:557
  412.7 27.4 %collective-permute-start.49 = (bf16[96,1664]{1,0:T(8,128)(2,1)}, bf16[96,1664]{1,0:T(8,128)(2,1)}, u32[]{:S(2)}, u32[]{:S(2)}) collective-permute-start(bf16[96,1664]{1,0:T(8,128)(2,1)} %get-tuple-element.715), channel_id=1, source_target_pairs={{0,16},{4,20},{8,24},{12,28},{16,0},{20,4},{24,8},{28,12},{1,17},{... | collective-permute-start | bytes 958472 | tf_op jit(solution)/shard_map/ppermute | solution.py:552
  412.7 27.4 %collective-permute-start.50 = (bf16[96,1664]{1,0:T(8,128)(2,1)S(1)}, bf16[96,1664]{1,0:T(8,128)(2,1)}, u32[]{:S(2)}, u32[]{:S(2)}) collective-permute-start(bf16[96,1664]{1,0:T(8,128)(2,1)S(1)} %get-tuple-element.714), channel_id=1, source_target_pairs={{0,8},{4,12},{8,0},{12,4},{16,24},{20,28},{24,16},{28,20},{1,9},{5... | collective-permute-start | bytes 958472 | tf_op jit(solution)/shard_map/ppermute | solution.py:552
  414.1 26.0 %collective-permute-start.47 = (bf16[192,384]{1,0:T(8,128)(2,1)}, bf16[192,384]{1,0:T(8,128)(2,1)}, u32[]{:S(2)}, u32[]{:S(2)}) collective-permute-start(bf16[192,384]{1,0:T(8,128)(2,1)} %add_convert_fusion.20), channel_id=1, source_target_pairs={{0,1},{1,2},{2,3},{3,0},{4,5},{5,6},{6,7},{7,4},{8,9},{9,10},{10,1... | collective-permute-start | bytes 442376 | tf_op jit(solution)/shard_map/ppermute | solution.py:557
  447.0 30.7 %collective-permute-start.51 = (bf16[384,1536]{1,0:T(8,128)(2,1)}, bf16[384,1536]{1,0:T(8,128)(2,1)S(1)}, u32[]{:S(2)}, u32[]{:S(2)}) collective-permute-start(bf16[384,1536]{1,0:T(8,128)(2,1)} %add_convert_fusion), channel_id=1, source_target_pairs={{0,1},{1,2},{2,3},{3,0},{4,5},{5,6},{6,7},{7,4},{8,9},{9,10},{10,1... | collective-permute-start | bytes 3538952 | tf_op jit(solution)/shard_map/ppermute | solution.py:557
  449.0 28.7 %collective-permute-start.54 = (bf16[192,1664]{1,0:T(8,128)(2,1)}, bf16[192,1664]{1,0:T(8,128)(2,1)}, u32[]{:S(2)}, u32[]{:S(2)}) collective-permute-start(bf16[192,1664]{1,0:T(8,128)(2,1)} %pad_maximum_fusion.4), channel_id=1, source_target_pairs={{0,8},{4,12},{8,0},{12,4},{16,24},{20,28},{24,16},{28,20},{1,9},{5... | collective-permute-start | bytes 1916936 | tf_op jit(solution)/shard_map/ppermute | solution.py:552
  450.4 27.3 %collective-permute-start.55 = (bf16[192,1664]{1,0:T(8,128)(2,1)}, bf16[192,1664]{1,0:T(8,128)(2,1)}, u32[]{:S(2)}, u32[]{:S(2)}) collective-permute-start(bf16[192,1664]{1,0:T(8,128)(2,1)} %pad_maximum_fusion.5), channel_id=1, source_target_pairs={{0,16},{4,20},{8,24},{12,28},{16,0},{20,4},{24,8},{28,12},{1,17},{... | collective-permute-start | bytes 1916936 | tf_op jit(solution)/shard_map/ppermute | solution.py:552
  (74 other events, 964.8 us)
Sparse Core Ops, SparseCore 0:
  42.9 69.8 all-gather.1
  253.0 55.6 reduce-scatter.3
  312.4 46.2 reduce-scatter.7
  361.9 68.3 reduce-scatter.5

commit v4 on v3

--- a/solution.py
+++ b/solution.py
@@ -65,7 +65,8 @@
 ):
     pieces, refs = refs[: len(spots)], refs[len(spots) :]
     (hn_ref, w_ref, gain_ref, q8_ref, kn_ref, vl_ref, aq_ref, ak_ref, og_ref, q_ref, ks_ref, kd_ref, vd_ref, lg_ref,
-     gain_s, carry_k, carry_v, carry_c, sems) = refs
+     gain_s, carry_k, carry_v, carry_c, w_s, sems) = refs
+    keep = pltpu.make_async_copy(w_s, w_ref, sems.at[len(spots)])
     step = pl.program_id(0)
     width = q8_ref.shape[1]
     wide = 4 * width
@@ -75,14 +76,15 @@
         copies = []
         for i, (far, start, count, cut) in enumerate(spots):
             row = pl.multiple_of((me_ref[0] ^ far) * cut + start, 16)
-            copies.append(pltpu.make_async_copy(pieces[i], w_ref.at[pl.ds(row, count), :], sems.at[i]))
+            copies.append(pltpu.make_async_copy(pieces[i], w_s.at[pl.ds(row, count), :], sems.at[i]))
         for copy in copies:
             copy.start()
         for copy in copies:
             copy.wait()
+        keep.start()
         pick = (lanes((8, 128)) == 3 * heads + rows_of((8, 128))).astype(F32)
         pick = jnp.where(rows_of((8, 128)) < 2, pick, 0.0).astype(BF)
-        gain_s[...] = dot(pick, w_ref[:, wide:], NT)
+        gain_s[...] = dot(pick, w_s[:, wide:], NT)
         carry_k[...] = jnp.zeros_like(carry_k)
         carry_v[...] = jnp.zeros_like(carry_v)
         carry_c[...] = jnp.zeros_like(carry_c)
@@ -92,7 +94,7 @@
     factor = lax.rsqrt(jnp.mean(x * x, -1, keepdims=True) + EPS)
     hn = (x * factor * gain_s[0:1, :]).astype(BF)
     hn_ref[...] = hn
-    proj = dot(hn, w_ref[...])
+    proj = dot(hn, w_s[...])
     q = proj[:, :width]
     k = proj[:, width : 2 * width]
     v = proj[:, 2 * width : 3 * width]
@@ -125,6 +127,10 @@
     aq_ref[...] = (dot(parts, mq_ref[...]) + rows_ref[1:2, :]).astype(BF)
     ak_ref[...] = (dot(parts, mk_ref[...]) + rows_ref[2:3, :]).astype(BF)
 
+    @pl.when(step == pl.num_programs(0) - 1)
+    def _():
+        keep.wait()
+
 
 def pre(x, place, pieces, bias_row, gqk, heads):
     seq, model = x.shape
@@ -160,12 +166,13 @@
         grid=(seq // block,),
         in_specs=[SMEM, row(model), full(ba.shape), full(g64.shape), full(tri.shape), full(mq.shape), full(mk.shape),
                   full((8, 128)), full(gqk.shape)] + [ANY] * len(spots),
-        out_specs=[row(model), full((model, wide)), full((8, model))] + [row(width)] * 3 + [row(128)] * 2 + [row(width)] * 5 + [row(128)],
+        out_specs=[row(model), ANY, full((8, model))] + [row(width)] * 3 + [row(128)] * 2 + [row(width)] * 5 + [row(128)],
         out_shape=[shape(model, BF), jax.ShapeDtypeStruct((model, wide), BF), jax.ShapeDtypeStruct((8, model), F32)]
         + [shape(width, BF)] * 3
         + [shape(128, BF)] * 2 + [shape(width, F32)] + [shape(width, BF)] * 4 + [shape(128, F32)],
         scratch_shapes=[pltpu.VMEM((8, model), F32), pltpu.VMEM((8, width), F32), pltpu.VMEM((8, width), F32),
-                        pltpu.VMEM((8, 128), F32), pltpu.SemaphoreType.DMA((len(spots),))],
+                        pltpu.VMEM((8, 128), F32), pltpu.VMEM((model, wide), BF),
+                        pltpu.SemaphoreType.DMA((len(spots) + 1,))],
         compiler_params=params(),
         cost_estimate=COST,
         name="pre",
@@ -445,7 +452,7 @@
     res_ref, gain_ref, w_ref, ba_ref, g64_ref, tri_ref, ms_ref, rows_ref, gqk_ref, *refs,
 ):
     grads, refs = refs[: 4 * groups], refs[4 * groups :]
-    dp_ref, gt_ref, g0_ref, gq_ref, gb_ref, carry_k, carry_v, carry_c = refs
+    dp_ref, gt_ref, g0_ref, gq_ref, gb_ref, carry_k, carry_v, carry_c, w_s, sem = refs
     dq_raw, dk_raw, dvs = [
         jnp.concatenate([r[...] for r in grads[i * groups : (i + 1) * groups]], 1) for i in range(3)
     ]
@@ -453,8 +460,11 @@
     step = pl.program_id(0)
     rows, width = q_ref.shape
 
+    move = pltpu.make_async_copy(w_ref, w_s, sem)
+
     @pl.when(step == 0)
     def _():
+        move.start()
         carry_k[...] = jnp.zeros_like(carry_k)
         carry_v[...] = jnp.zeros_like(carry_v)
         carry_c[...] = jnp.zeros_like(carry_c)
@@ -499,7 +509,12 @@
     do = du_ref[...].astype(F32) * att_ref[...] * og * (1.0 - og)
     dp = jnp.concatenate([dq.astype(BF), dk.astype(BF), dv.astype(BF), do.astype(BF), dgl.astype(BF)], 1)
     dp_ref[...] = dp
-    dhn = dot(dp, w_ref[...], NT)
+
+    @pl.when(step == 0)
+    def _():
+        move.wait()
+
+    dhn = dot(dp, w_s[...], NT)
     x = x_ref[...].astype(F32)
     factor = lax.rsqrt(jnp.mean(x * x, -1, keepdims=True) + EPS)
     n = x * factor
@@ -533,13 +548,14 @@
         functools.partial(post_kernel, heads, groups),
         grid=(count,),
         in_specs=[row(width)] * 4 + [row(128)] + [row(width)] * 3 + [row(model)] * 2
-        + [full(gains.shape), full(w.shape), full(ba.shape), full(g64.shape), full(tri.shape),
+        + [full(gains.shape), ANY, full(ba.shape), full(g64.shape), full(tri.shape),
            full(ms.shape), full((8, 128)), full(gqk.shape)] + [row(g.shape[1]) for g in dq + dk + dv + dc],
         out_specs=[row(wide), row(model), full((8, model)), full((8, width)), full((8, 128))],
         out_shape=[jax.ShapeDtypeStruct((seq, wide), BF), jax.ShapeDtypeStruct((seq, model), BF),
                    jax.ShapeDtypeStruct((8, model), F32), jax.ShapeDtypeStruct((8, width), F32),
                    jax.ShapeDtypeStruct((8, 128), F32)],
-        scratch_shapes=[pltpu.VMEM((8, width), F32), pltpu.VMEM((8, width), F32), pltpu.VMEM((8, 128), F32)],
+        scratch_shapes=[pltpu.VMEM((8, width), F32), pltpu.VMEM((8, width), F32), pltpu.VMEM((8, 128), F32),
+                        pltpu.VMEM(w.shape, BF), pltpu.SemaphoreType.DMA],
         compiler_params=params(),
         cost_estimate=COST,
         name="post",
@@ -604,49 +620,6 @@
     for (far, start), piece in sorted(pieces.items()):
         whole = lax.dynamic_update_slice_in_dim(whole, piece, (me ^ far) * cut + start, 0)
     return whole
-
-
-def cut_out(whole, me, far):
-    rows = whole.shape[0] // lax.axis_size("dp")
-    return lax.dynamic_slice_in_dim(whole, (me ^ far) * rows, rows, 0)
-
-
-def odd_rows(whole, me):
-    return jnp.concatenate([cut_out(whole, me, r) for r in range(1, lax.axis_size("dp"), 2)], 0)
-
-
-def scatter_2_add(whole, got, me):
-    size = lax.axis_size("dp")
-    rows = whole.shape[0] // size
-    return {r: add(cut_out(whole, me, r), got[rows * (r // 2) : rows * (r // 2 + 1)]) for r in range(0, size, 2)}
-
-
-def scatter_2_send(pieces):
-    pieces = dict(pieces)
-    if lax.axis_size("dp") == 8:
-        half = pieces[0].shape[0] // 2
-        pieces[-1] = swap(pieces[6][:half], "dp", 2)
-        pieces[-2] = swap(pieces[6][half:], "dp", 4)
-    return pieces
-
-
-def scatter_3_add(pieces):
-    if lax.axis_size("dp") == 8:
-        half = pieces[0].shape[0] // 2
-        to_y = jnp.concatenate([add(pieces[4][:half], pieces[-1]), pieces[4][half:]], 0)
-        to_x = jnp.concatenate([pieces[2][:half], add(pieces[2][half:], pieces[-2])], 0)
-        return {0: pieces[0], 2: to_x, 4: to_y}
-    return pieces
-
-
-def scatter_3_send(pieces):
-    size = lax.axis_size("dp")
-    if size == 8:
-        return [pieces[0], swap(pieces[2], "dp", 2), swap(pieces[4], "dp", 4)]
-    for bit in reversed(high_bits(size)):
-        got = {r: swap(pieces[r], "dp", bit) for r in pieces if r & bit}
-        pieces = {r: add(p, got[r | bit]) for r, p in pieces.items() if not r & bit}
-    return [pieces[0]]
 
 
 def rows_major(value):
@@ -791,16 +764,16 @@
     ring = out_acc = None
     for begin, end in zip(cuts, cuts[1:]):
         back_parts.append(attend_back(begin, end, block, heads, q8, aq, kn, ak, vl, og, att, li, du))
-        y_acc, back_parts, out_acc = tie((y_acc, back_parts, out_acc))
+        y_acc, back_parts = tie((y_acc, back_parts))
         if y_step < tp:
+            send, y_step = add(y_acc, token_part(part, y_step)), y_step + 1
             if ring is None:
-                ring = [sums[0][:, i * width : (i + 1) * width] for i in range(tp)]
-                out_send, out_step = ring[1], 2
+                ring, out_step = [sums[0][:, i * width : (i + 1) * width] for i in range(tp)], 2
+                send, du, ring = tie((send, du, ring))
+                out_acc = turn(ring[1])
             else:
-                out_send, out_step = add(out_acc, ring[out_step]), out_step + 1
-            send, y_step = add(y_acc, token_part(part, y_step)), y_step + 1
-            send, du, out_send = tie((send, du, out_send))
-            y_acc, out_acc = turn(send), turn(out_send)
+                send, du = tie((send, du))
+            y_acc = turn(send)
     dq, dk, dv, dc = zip(*back_parts)
     dp_all, gt, g0, gq, gb = post(
         heads, dq, dk, dv, dc, q, ks, kd, vd, lg, du, att, og, x, res, gains, w, bias_row, gqk
@@ -810,52 +783,41 @@
     send = token_part(gt, 1)
     send, dp_all, y_acc, out_acc = tie((send, dp_all, y_acc, out_acc))
     back = turn(send)
-    attn_s = product(hn, dp_all)
-    odd = odd_rows(attn_s, me_d)
+    fill = product(hn, dp_all)
+    back, fill, g0, gq, gb = tie((back, fill, g0, gq, gb))
+    sums.append(scatter(fill))
+    while y_step < tp:
+        y_acc, y_step = turn(add(y_acc, token_part(part, y_step))), y_step + 1
     gq = gq[0:2].reshape(2, heads, 64).sum(1)
     gb = lax.dynamic_update_slice_in_dim(
         jnp.zeros(forget_bias.shape, F32), gb[0, 2 * heads : 2 * heads + heads_real], me_t * heads_real, 0
     )
     small = jnp.concatenate([gq.reshape(-1), gb])
     small = jnp.pad(small, (0, model - small.shape[0]))[None]
-    flat = jnp.concatenate([g0[0:1], gmid, small, jnp.zeros((5, model), F32)], 0)
-    back, attn_s, odd, flat = tie((back, attn_s, odd, flat))
-    while y_step < tp:
-        y_acc, y_step = turn(add(y_acc, token_part(part, y_step))), y_step + 1
-    across = [1 << i for i in range(tp.bit_length() - 1)]
-    along = [1 << i for i in range(dp.bit_length() - 1)]
-    stage = 0
+    hops = [("dp", 1 << i) for i in range(dp.bit_length() - 1)]
+    flat = None
     for s in range(2, tp):
-        send, out_send = add(back, token_part(gt, s)), None
-        if out_step < tp:
+        send = add(back, token_part(gt, s))
+        out_send = None
+        if flat is None:
+            flat = jnp.concatenate([g0[0:1], gmid, small, jnp.zeros((5, model), F32)], 0)
+        elif out_step < tp:
             out_send, out_step = add(out_acc, ring[out_step]), out_step + 1
-        if stage == 1:
-            attn_s = scatter_3_add(attn_s)
-        send, flat, out_send, attn_s, odd = tie((send, flat, out_send, attn_s, odd))
+        send, flat, out_send, y_acc = tie((send, flat, out_send, y_acc))
         back = turn(send)
         if out_send is not None:
             out_acc = turn(out_send)
-        if stage == 0:
-            attn_s, stage = scatter_2_send(scatter_2_add(attn_s, swap(odd, "dp", 1), me_d)), 1
-        elif stage == 1:
-            attn_s, stage = scatter_3_send(attn_s), 2
-        for axis, bits in (("dp", along), ("tp", across)):
-            for _ in range(2):
-                if bits and (axis == "dp" or s > 2):
-                    flat = flat + swap(flat, axis, bits.pop(0))
-                    break
-        back, flat, out_acc, attn_s = tie((back, flat, out_acc, attn_s))
+        for _ in range(2):
+            if hops:
+                flat = flat + swap(flat, *hops.pop(0))
+        back, flat, out_acc = tie((back, flat, out_acc))
     while out_step < tp:
         out_acc, out_step = turn(add(out_acc, ring[out_step])), out_step + 1
-    if stage == 1:
-        attn_s = scatter_3_send(scatter_3_add(attn_s))
-    for axis, bits in (("dp", along), ("tp", across)):
-        for bit in bits:
-            flat = flat + swap(flat, axis, bit)
+    for axis, bit in hops + [("tp", 1 << i) for i in range(tp.bit_length() - 1)]:
+        flat = flat + swap(flat, axis, bit)
     result, back, gt = tie((total_of((y_acc, token_part(part, 0))).astype(BF), back, gt))
     grad_tokens = total_of((token_part(gt, 0), back))
-    grad_attn = total_of(attn_s)
-    grad_down, grad_gu = [value.astype(F32) for value in sums[1:]]
+    grad_down, grad_gu, grad_attn = [value.astype(F32) for value in sums[1:]]
     grad_out_own = total_of((ring[0], out_acc))
     norm_grad = flat[0:2]
     qk_grad = flat[2, : 2 * 64].reshape(2, 64)

time: 500 us -> 491 us (0.982); the launches traced: 496 us -> 481 us
  Pallas kernels: 182 us -> 173 us
  other arithmetic: 40.7 us -> 32.1 us
    ppermute x28 -> x23, waiting for transfers between devices: 37 us -> 18 us  [swap(): return lax.ppermute(value, axis, [(i, i ^ bit) for i in range(size)])]
    ppermute x30, waiting for transfers between devices: 96.8 us -> 109 us  [turn(): return lax.ppermute(value, 'tp', [(i, (i + 1) % size) for i in range(size)])]
    pallas_call x3, Pallas kernels: 77.3 us -> 67.5 us  [feed(): pl.pallas_call(functools.partial(ffn_kernel, count, chunk, block, step_ro...]
    convert_element_type x17 -> x14, other arithmetic: 18.6 us -> 13.1 us  [add(): return (a.astype(F32) + b.astype(F32)).astype(BF)]
    ppermute x28 -> x23, starting transfers between devices: 16.9 us -> 13.9 us  [swap(): return lax.ppermute(value, axis, [(i, i ^ bit) for i in range(size)])]
  transfers between devices with their start and end apart: 62 -> 58, of which waited for: 27 -> 28; matrix products, arithmetic and copies ran while one was open for 22% -> 22% of each run, Pallas kernels for 37% -> 36%
where the time goes in v4:
time: 491 us; the launch traced here: 481 us
  Pallas kernels  173 us (35%)
  waiting for transfers between devices  133 us (27%)
  matrix products  51.1 us (10%)
  starting transfers between devices  42.6 us (9%)
  local copies, waits for them, and re-layouts  34.1 us (7%)
  other arithmetic  32.1 us (7%)
  between operations  15.4 us (3%)
    ppermute x30, waiting for transfers between devices, turn(): return lax.ppermute(value, 'tp', [(i, (i + 1) % size) for i in range(size)])  109 us
    pallas_call x3, Pallas kernels, feed(): pl.pallas_call(functools.partial(ffn_kernel, count, chunk, block, step_ro...  67.5 us
    dot_general x4, matrix products, dot(): return lax.dot_general(a, b, dims, preferred_element_type=F32)  51.1 us
    pallas_call x2, Pallas kernels, attend_back(): pl.pallas_call(functools.partial(bwd_kernel, begin, heads, block), grid=(...  35.8 us
    ppermute x30, starting transfers between devices, turn(): return lax.ppermute(value, 'tp', [(i, (i + 1) % size) for i in range(size)])  28.5 us
    pallas_call x1, Pallas kernels, post(): pl.pallas_call(functools.partial(post_kernel, heads, groups), grid=(count...  27.6 us
    pallas_call x1, Pallas kernels, pre(): pl.pallas_call(functools.partial(pre_kernel, heads, spots), grid=(seq //...  22.1 us
    pallas_call x3, Pallas kernels, attend(): pl.pallas_call(functools.partial(fwd_kernel, chunk, block), grid=grid, in...  20.4 us
  transfers between devices with their start and end apart: 58, of which 28 were waited for; matrix products, arithmetic and copies ran while one was open for 22% of the time, Pallas kernels for 36%

profile of v4, /device:TPU:0, one launch (start us, length us, event | category | flops | bytes accessed | tf_op | source)
XLA Modules:
  0.0 481.3 jit_solution(8665781452353558371)
XLA Ops:
  16.3 6.0 %collective-permute-done.3 = bf16[192,384]{1,0:T(8,128)(2,1)} collective-permute-done((bf16[192,384]{1,0:T(8,128)(2,1)S(1)}, bf16[192,384]{1,0:T(8,128)(2,1)}, u32[]{:S(2)}, u32[]{:S(2)}) %collective-permute-start.3) | collective-permute-done | bytes 147488 | tf_op jit(solution)/shard_map/ppermute | solution.py:573
  23.4 6.0 %collective-permute-done.4 = bf16[192,384]{1,0:T(8,128)(2,1)S(1)} collective-permute-done((bf16[192,384]{1,0:T(8,128)(2,1)}, bf16[192,384]{1,0:T(8,128)(2,1)S(1)}, u32[]{:S(2)}, u32[]{:S(2)}) %collective-permute-start.4) | collective-permute-done | bytes 147488 | tf_op jit(solution)/shard_map/ppermute | solution.py:573
  33.9 5.5 %collective-permute-done.9 = bf16[192,384]{1,0:T(8,128)(2,1)S(1)} collective-permute-done((bf16[192,384]{1,0:T(8,128)(2,1)S(1)}, bf16[192,384]{1,0:T(8,128)(2,1)S(1)}, u32[]{:S(2)}, u32[]{:S(2)}) %collective-permute-start.9) | collective-permute-done | bytes 147488 | tf_op jit(solution)/shard_map/ppermute | solution.py:573
  48.6 22.1 %pre.1 = (bf16[1536,1536]{1,0:T(8,128)(2,1)}, bf16[1536,1664]{1,0:T(8,128)(2,1)}, f32[8,1536]{1,0:T(8,128)}, bf16[1536,384]{1,0:T(8,128)(2,1)}, bf16[1536,384]{1...) custom-call(s32[1]{0:T(128)} %bitcast.me_ref, ...), custom_call_target="tpu_custom_call" | custom-call | flops 1 | bytes 1 | tf_op jit(solution)/shard_map/pre/pallas_call | solution.py:164
  72.4 5.3 %attend.3 = (bf16[512,384]{1,0:T(8,128)(2,1)}, f32[1536,384]{1,0:T(8,128)}, f32[1536,384]{1,0:T(8,128)}) custom-call(bf16[1536,384]{1,0:T(8,128)(2,1)} %get-tuple-element.592.q_ref, bf16[1536,128]{1,0:T(8,128)(2,1)} %get-tuple-element.379.aq_ref, bf16[1536,384]{1,0:T(8,128)(2,1)} %get-tuple-element.380.k_ref, bf16[1536,128]{1,0:T(8,128)(2,1)} %get-tuple-element.381.ak_ref, ...), custom_call_target="tpu_custom_call" | custom-call | flops 1 | bytes 1 | tf_op jit(solution)/shard_map/attend/pallas_call | solution.py:225
  81.8 6.3 %attend.4 = (bf16[512,384]{1,0:T(8,128)(2,1)}, f32[1536,384]{1,0:T(8,128)}, f32[1536,384]{1,0:T(8,128)}) custom-call(bf16[1536,384]{1,0:T(8,128)(2,1)} %get-tuple-element.592.q_ref, bf16[1536,128]{1,0:T(8,128)(2,1)} %get-tuple-element.379.aq_ref, bf16[1536,384]{1,0:T(8,128)(2,1)} %get-tuple-element.380.k_ref, ...), custom_call_target="tpu_custom_call", output_to_operand_aliasing={{1}: (6, {}), {2}: (7, {})} | custom-call | flops 1 | bytes 1 | tf_op jit(solution)/shard_map/attend/pallas_call | solution.py:225
  97.5 8.8 %attend.5 = (bf16[512,384]{1,0:T(8,128)(2,1)}, f32[1536,384]{1,0:T(8,128)}, f32[1536,384]{1,0:T(8,128)}) custom-call(bf16[1536,384]{1,0:T(8,128)(2,1)} %get-tuple-element.592.q_ref, bf16[1536,128]{1,0:T(8,128)(2,1)} %get-tuple-element.379.aq_ref, bf16[1536,384]{1,0:T(8,128)(2,1)} %get-tuple-element.380.k_ref, ...), custom_call_target="tpu_custom_call", output_to_operand_aliasing={{1}: (6, {}), {2}: (7, {})} | custom-call | flops 1 | bytes 1 | tf_op jit(solution)/shard_map/attend/pallas_call | solution.py:225
  106.4 4.9 %collective-permute-done.17.refs_1_ = bf16[512,384]{1,0:T(8,128)(2,1)S(1)} collective-permute-done((bf16[512,384]{1,0:T(8,128)(2,1)}, bf16[512,384]{1,0:T(8,128)(2,1)S(1)}, u32[]{:S(2)}, u32[]{:S(2)}) %collective-permute-start.17) | collective-permute-done | bytes 393248 | tf_op jit(solution)/shard_map/ppermute | solution.py:573
  126.6 7.3 %collective-permute-done.25.refs_2_ = bf16[512,384]{1,0:T(8,128)(2,1)} collective-permute-done((bf16[512,384]{1,0:T(8,128)(2,1)S(1)}, bf16[512,384]{1,0:T(8,128)(2,1)}, u32[]{:S(2)}, u32[]{:S(2)}) %collective-permute-start.25) | collective-permute-done | bytes 393248 | tf_op jit(solution)/shard_map/ppermute | solution.py:573
  133.9 5.5 %collective-permute-done.26.refs_1_ = bf16[512,384]{1,0:T(8,128)(2,1)} collective-permute-done((bf16[512,384]{1,0:T(8,128)(2,1)}, bf16[512,384]{1,0:T(8,128)(2,1)}, u32[]{:S(2)}, u32[]{:S(2)}) %collective-permute-start.26) | collective-permute-done | bytes 393248 | tf_op jit(solution)/shard_map/ppermute | solution.py:573
  139.8 22.1 %feed.3 = (bf16[1536,1536]{1,0:T(8,128)(2,1)}, bf16[1536,1024]{1,0:T(8,128)(2,1)}, bf16[1536,2048]{1,0:T(8,128)(2,1)}, bf16[1536,1536]{1,0:T(8,128)(2,1)}, bf16[...) custom-call(s32[1]{0:T(128)} %bitcast.12.at_ref, ...), custom_call_target="tpu_custom_call" | custom-call | flops 1 | bytes 1 | tf_op jit(solution)/shard_map/feed/pallas_call | solution.py:344
  166.9 22.8 %feed.4 = (bf16[1536,1536]{1,0:T(8,128)(2,1)}, bf16[1536,1024]{1,0:T(8,128)(2,1)}, bf16[1536,2048]{1,0:T(8,128)(2,1)}, bf16[1536,1536]{1,0:T(8,128)(2,1)}, bf16[...) custom-call(s32[1]{0:T(128)} %bitcast.12.at_ref, ...), custom_call_target="tpu_custom_call", output_to_operand_aliasing={{0}: (10, {}), {1}: (11, {}), {2}: (12, {}), {3}: (13, {}),... | custom-call | flops 1 | bytes 1 | tf_op jit(solution)/shard_map/feed/pallas_call | solution.py:344
  190.6 22.6 %feed.5 = (bf16[1536,1536]{1,0:T(8,128)(2,1)}, bf16[1536,1024]{1,0:T(8,128)(2,1)}, bf16[1536,2048]{1,0:T(8,128)(2,1)}, bf16[1536,1536]{1,0:T(8,128)(2,1)}, bf16[...) custom-call(s32[1]{0:T(128)} %bitcast.12.at_ref, ...), custom_call_target="tpu_custom_call", output_to_operand_aliasing={{0}: (10, {}), {1}: (11, {}), {2}: (12, {}), {3}: (13, {}),... | custom-call | flops 1 | bytes 1 | tf_op jit(solution)/shard_map/feed/pallas_call | solution.py:344
  218.6 12.4 %convolution_convert_fusion.2 = bf16[1536,1536]{1,0:T(8,128)(2,1)} fusion(bf16[1536,1536]{1,0:T(8,128)(2,1)} %get-tuple-element.631.res_ref, bf16[1536,1536]{1,0:T(8,128)(2,1)} %get-tuple-element.544), kind=kOutput, calls=%fused_computation.2 | convolution fusion | flops 7250116608 | bytes 14155776 | tf_op jit(solution)/shard_map/dot_general | solution.py:24
  231.0 8.9 %fusion = bf16[1536,1024]{1,0:T(8,128)(2,1)} fusion(bf16[1536,1024]{1,0:T(8,128)(2,1)S(1)} %copy-done, bf16[1,1536,1536]{2,1,0:T(8,128)(2,1)} %param.36), kind=kOutput, calls=%fused_computation.4 | convolution fusion | flops 4833411072 | bytes 11010048 | tf_op jit(solution)/shard_map/dot_general | solution.py:24
  245.5 15.6 %convolution_convert_fusion.1 = bf16[1536,2048]{1,0:T(8,128)(2,1)} fusion(bf16[1536,1536]{1,0:T(8,128)(2,1)} %get-tuple-element.567, bf16[1536,2048]{1,0:T(8,128)(2,1)} %get-tuple-element.568), kind=kOutput, calls=%fused_computation.1 | convolution fusion | flops 9666822144 | bytes 17301504 | tf_op jit(solution)/shard_map/dot_general | solution.py:24
  267.8 9.7 %collective-permute-done.39 = bf16[512,384]{1,0:T(8,128)(2,1)S(1)} collective-permute-done((bf16[512,384]{1,0:T(8,128)(2,1)S(1)}, bf16[512,384]{1,0:T(8,128)(2,1)S(1)}, u32[]{:S(2)}, u32[]{:S(2)}) %collective-permute-start.39) | collective-permute-done | bytes 393248 | tf_op jit(solution)/shard_map/ppermute | solution.py:573
  280.0 12.9 %attend_back.2 = (f32[1536,128]{1,0:T(8,128)}, f32[1536,128]{1,0:T(8,128)}, f32[1536,128]{1,0:T(8,128)}, f32[1536,128]{1,0:T(8,128)}) custom-call(bf16[1536,384]{1,0:T(8,128)(2,1)} %get-tuple-element.592.q_ref, bf16[1536,128]{1,0:T(8,128)(2,1)} %get-tuple-element.379.aq_ref, bf16[1536,384]{1,0:T(8,128)(2,1)} %get-tuple-element.380.k_ref, ...), custom_call_target="tpu_custom_call" | custom-call | flops 1 | bytes 1 | tf_op jit(solution)/shard_map/attend_back/pallas_call | solution.py:437
  300.1 22.9 %attend_back.3 = (f32[1536,256]{1,0:T(8,128)}, f32[1536,256]{1,0:T(8,128)}, f32[1536,256]{1,0:T(8,128)}, f32[1536,128]{1,0:T(8,128)}) custom-call(bf16[1536,384]{1,0:T(8,128)(2,1)} %get-tuple-element.592.q_ref, bf16[1536,128]{1,0:T(8,128)(2,1)} %get-tuple-element.379.aq_ref, bf16[1536,384]{1,0:T(8,128)(2,1)} %get-tuple-element.380.k_ref, ...), custom_call_target="tpu_custom_call" | custom-call | flops 1 | bytes 1 | tf_op jit(solution)/shard_map/attend_back/pallas_call | solution.py:437
  330.8 27.6 %post.1 = (bf16[1536,1664]{1,0:T(8,128)(2,1)}, bf16[1536,1536]{1,0:T(8,128)(2,1)}, f32[8,1536]{1,0:T(8,128)}, f32[8,384]{1,0:T(8,128)}, f32[8,128]{1,0:T(8,128)}) custom-call(bf16[1536,384]{1,0:T(8,128)(2,1)} %get-tuple-element.624.q_ref, bf16[1536,384]{1,0:T(8,128)(2,1)} %get-tuple-element.625.ks_ref, bf16[1536,384]{1,0:T(8,128)(2,1)} %get-tuple-element.626.kd_ref, ...), custom_call_target="tpu_custom_call" | custom-call | flops 1 | bytes 1 | tf_op jit(solution)/shard_map/post/pallas_call | solution.py:547
  361.9 14.2 %convolution_convert_fusion = bf16[1536,1664]{1,0:T(8,128)(2,1)} fusion(bf16[1536,1536]{1,0:T(8,128)(2,1)} %get-tuple-element.650, bf16[1536,1664]{1,0:T(8,128)(2,1)} %get-tuple-element.651), kind=kOutput, calls=%fused_computation | convolution fusion | flops 7854292992 | bytes 14942208 | tf_op jit(solution)/shard_map/dot_general | solution.py:24
  376.2 12.5 %collective-permute-done.43 = bf16[384,1536]{1,0:T(8,128)(2,1)S(1)} collective-permute-done((bf16[384,1536]{1,0:T(8,128)(2,1)S(1)}, bf16[384,1536]{1,0:T(8,128)(2,1)S(1)}, u32[]{:S(2)}, u32[]{:S(2)}) %collective-permute-start.43) | collective-permute-done | bytes 1179680 | tf_op jit(solution)/shard_map/ppermute | solution.py:573
  402.0 18.1 %collective-permute-done.44 = bf16[384,1536]{1,0:T(8,128)(2,1)S(1)} collective-permute-done((bf16[384,1536]{1,0:T(8,128)(2,1)S(1)}, bf16[384,1536]{1,0:T(8,128)(2,1)S(1)}, u32[]{:S(2)}, u32[]{:S(2)}) %collective-permute-start.44) | collective-permute-done | bytes 1179680 | tf_op jit(solution)/shard_map/ppermute | solution.py:573
  432.6 21.1 %collective-permute-done.49 = bf16[192,384]{1,0:T(8,128)(2,1)S(1)} collective-permute-done((bf16[192,384]{1,0:T(8,128)(2,1)S(1)}, bf16[192,384]{1,0:T(8,128)(2,1)S(1)}, u32[]{:S(2)}, u32[]{:S(2)}) %collective-permute-start.49) | collective-permute-done | bytes 147488 | tf_op jit(solution)/shard_map/ppermute | solution.py:573
  (277 shorter events, 144.8 us)
Async XLA Ops:
  7.2 132.6 %all-gather.2.cloned.1.call-start = ((), (), s32[]{:S(2)}) async-start(), calls=%async_computation.4 | async-start | bytes 10616832 | tf_op jit(solution)/shard_map/all_gather | solution.py:697
  42.8 254.3 %reduce-scatter.5.cloned.1.call-start = ((), (), s32[]{:S(2)}) async-start(), calls=%async_computation.5 | async-start | bytes 5308416 | tf_op jit(solution)/shard_map/reduce_scatter | solution.py:630
  42.9 27.8 %collective-permute-start.12 = (bf16[192,1536]{1,0:T(8,128)(2,1)S(1)}, bf16[192,1536]{1,0:T(8,128)(2,1)}, u32[]{:S(2)}, u32[]{:S(2)}) collective-permute-start(bf16[192,1536]{1,0:T(8,128)(2,1)S(1)} %pad_maximum_fusion.3), channel_id=1, source_target_pairs={{0,4},{4,0},{8,12},{12,8},{16,20},{20,16},{24,28},{28,24},{1,5},{5... | collective-permute-start | bytes 1769480 | tf_op jit(solution)/shard_map/ppermute | solution.py:568
  42.9 27.8 %collective-permute-start.13 = (bf16[192,1536]{1,0:T(8,128)(2,1)S(1)}, bf16[192,1536]{1,0:T(8,128)(2,1)S(1)}, u32[]{:S(2)}, u32[]{:S(2)}) collective-permute-start(bf16[192,1536]{1,0:T(8,128)(2,1)S(1)} %pad_maximum_fusion.3), channel_id=1, source_target_pairs={{0,8},{4,12},{8,0},{12,4},{16,24},{20,28},{24,16},{28,20},{1,9},{5... | collective-permute-start | bytes 1769480 | tf_op jit(solution)/shard_map/ppermute | solution.py:568
  43.5 27.2 %collective-permute-start.14 = (bf16[192,1536]{1,0:T(8,128)(2,1)S(1)}, bf16[192,1536]{1,0:T(8,128)(2,1)S(1)}, u32[]{:S(2)}, u32[]{:S(2)}) collective-permute-start(bf16[192,1536]{1,0:T(8,128)(2,1)S(1)} %pad_maximum_fusion.3), channel_id=1, source_target_pairs={{0,16},{4,20},{8,24},{12,28},{16,0},{20,4},{24,8},{28,12},{1,17},{... | collective-permute-start | bytes 1769480 | tf_op jit(solution)/shard_map/ppermute | solution.py:568
  81.3 25.0 %collective-permute-start.18 = (bf16[192,1536]{1,0:T(8,128)(2,1)S(1)}, bf16[192,1536]{1,0:T(8,128)(2,1)S(1)}, u32[]{:S(2)}, u32[]{:S(2)}) collective-permute-start(bf16[192,1536]{1,0:T(8,128)(2,1)S(1)} %collective-permute-done.13), channel_id=1, source_target_pairs={{0,4},{4,0},{8,12},{12,8},{16,20},{20,16},{24,28},{28,24},{1,5},{5... | collective-permute-start | bytes 1769480 | tf_op jit(solution)/shard_map/ppermute | solution.py:568
  81.8 24.5 %collective-permute-start.19 = (bf16[192,1536]{1,0:T(8,128)(2,1)S(1)}, bf16[192,1536]{1,0:T(8,128)(2,1)S(1)}, u32[]{:S(2)}, u32[]{:S(2)}) collective-permute-start(bf16[192,1536]{1,0:T(8,128)(2,1)S(1)} %collective-permute-done.14), channel_id=1, source_target_pairs={{0,4},{4,0},{8,12},{12,8},{16,20},{20,16},{24,28},{28,24},{1,5},{5... | collective-permute-start | bytes 1769480 | tf_op jit(solution)/shard_map/ppermute | solution.py:568
  111.3 28.0 %collective-permute-start.26 = (bf16[512,384]{1,0:T(8,128)(2,1)}, bf16[512,384]{1,0:T(8,128)(2,1)}, u32[]{:S(2)}, u32[]{:S(2)}) collective-permute-start(bf16[512,384]{1,0:T(8,128)(2,1)} %get-tuple-element.411.refs_0_), channel_id=1, source_target_pairs={{0,1},{1,2},{2,3},{3,0},{4,5},{5,6},{6,7},{7,4},{8,9},{9,10},{10,1... | collective-permute-start | bytes 1179656 | tf_op jit(solution)/shard_map/ppermute | solution.py:573
  162.0 27.8 %collective-permute-start.30 = (bf16[512,384]{1,0:T(8,128)(2,1)}, bf16[512,384]{1,0:T(8,128)(2,1)S(1)}, u32[]{:S(2)}, u32[]{:S(2)}) collective-permute-start(bf16[512,384]{1,0:T(8,128)(2,1)} %get-tuple-element.458), channel_id=1, source_target_pairs={{0,1},{1,2},{2,3},{3,0},{4,5},{5,6},{6,7},{7,4},{8,9},{9,10},{10,1... | collective-permute-start | bytes 1179656 | tf_op jit(solution)/shard_map/ppermute | solution.py:573
  162.6 27.1 %collective-permute-start.29 = (bf16[512,384]{1,0:T(8,128)(2,1)S(1)}, bf16[512,384]{1,0:T(8,128)(2,1)S(1)}, u32[]{:S(2)}, u32[]{:S(2)}) collective-permute-start(bf16[512,384]{1,0:T(8,128)(2,1)S(1)} %collective-permute-done.28.refs_2_), channel_id=1, source_target_pairs={{0,1},{1,2},{2,3},{3,0},{4,5},{5,6},{6,7},{7,4},{8,9},{9,10},{10,1... | collective-permute-start | bytes 1179656 | tf_op jit(solution)/shard_map/ppermute | solution.py:573
  189.9 23.3 %collective-permute-start.31 = (bf16[512,384]{1,0:T(8,128)(2,1)S(1)}, bf16[512,384]{1,0:T(8,128)(2,1)S(1)}, u32[]{:S(2)}, u32[]{:S(2)}) collective-permute-start(bf16[512,384]{1,0:T(8,128)(2,1)S(1)} %add_convert_fusion.13), channel_id=1, source_target_pairs={{0,1},{1,2},{2,3},{3,0},{4,5},{5,6},{6,7},{7,4},{8,9},{9,10},{10,1... | collective-permute-start | bytes 1179656 | tf_op jit(solution)/shard_map/ppermute | solution.py:573
  214.2 25.6 %collective-permute-start.33 = (bf16[512,384]{1,0:T(8,128)(2,1)}, bf16[512,384]{1,0:T(8,128)(2,1)}, u32[]{:S(2)}, u32[]{:S(2)}) collective-permute-start(bf16[512,384]{1,0:T(8,128)(2,1)} %get-tuple-element.535), channel_id=1, source_target_pairs={{0,1},{1,2},{2,3},{3,0},{4,5},{5,6},{6,7},{7,4},{8,9},{9,10},{10,1... | collective-permute-start | bytes 1179656 | tf_op jit(solution)/shard_map/ppermute | solution.py:573
  214.3 25.5 %collective-permute-start.34 = (bf16[512,384]{1,0:T(8,128)(2,1)S(1)}, bf16[512,384]{1,0:T(8,128)(2,1)}, u32[]{:S(2)}, u32[]{:S(2)}) collective-permute-start(bf16[512,384]{1,0:T(8,128)(2,1)S(1)} %get-tuple-element.536), channel_id=1, source_target_pairs={{0,1},{1,2},{2,3},{3,0},{4,5},{5,6},{6,7},{7,4},{8,9},{9,10},{10,1... | collective-permute-start | bytes 1179656 | tf_op jit(solution)/shard_map/ppermute | solution.py:573
  240.3 183.3 %reduce-scatter.11.cloned.1.call-start = ((), (), s32[]{:S(2)}) async-start(), calls=%async_computation.8 | async-start | bytes 3538944 | tf_op jit(solution)/shard_map/reduce_scatter | solution.py:630
  241.0 184.6 %reduce-scatter.9.cloned.1.call-start = ((), (), s32[]{:S(2)}) async-start(), calls=%async_computation.7 | async-start | bytes 7077888 | tf_op jit(solution)/shard_map/reduce_scatter | solution.py:630
  261.2 209.6 %reduce-scatter.7.cloned.1.call-start = ((), (), s32[]{:S(2)}) async-start(), calls=%async_computation.6 | async-start | bytes 5750784 | tf_op jit(solution)/shard_map/reduce_scatter | solution.py:630
  266.4 29.1 %collective-permute-start.38 = (bf16[384,1536]{1,0:T(8,128)(2,1)S(1)}, bf16[384,1536]{1,0:T(8,128)(2,1)S(1)}, u32[]{:S(2)}, u32[]{:S(2)}) collective-permute-start(bf16[384,1536]{1,0:T(8,128)(2,1)S(1)} %constant_dynamic-slice_fusion.1), channel_id=1, source_target_pairs={{0,1},{1,2},{2,3},{3,0},{4,5},{5,6},{6,7},{7,4},{8,9},{9,10},{10,1... | collective-permute-start | bytes 3538952 | tf_op jit(solution)/shard_map/ppermute | solution.py:573
  299.0 28.9 %collective-permute-start.40 = (bf16[384,1536]{1,0:T(8,128)(2,1)S(1)}, bf16[384,1536]{1,0:T(8,128)(2,1)S(1)}, u32[]{:S(2)}, u32[]{:S(2)}) collective-permute-start(bf16[384,1536]{1,0:T(8,128)(2,1)S(1)} %add_convert_fusion.4), channel_id=1, source_target_pairs={{0,1},{1,2},{2,3},{3,0},{4,5},{5,6},{6,7},{7,4},{8,9},{9,10},{10,1... | collective-permute-start | bytes 3538952 | tf_op jit(solution)/shard_map/ppermute | solution.py:573
  329.4 30.8 %collective-permute-start.41 = (bf16[384,1536]{1,0:T(8,128)(2,1)S(1)}, bf16[384,1536]{1,0:T(8,128)(2,1)S(1)}, u32[]{:S(2)}, u32[]{:S(2)}) collective-permute-start(bf16[384,1536]{1,0:T(8,128)(2,1)S(1)} %add_convert_fusion.3), channel_id=1, source_target_pairs={{0,1},{1,2},{2,3},{3,0},{4,5},{5,6},{6,7},{7,4},{8,9},{9,10},{10,1... | collective-permute-start | bytes 3538952 | tf_op jit(solution)/shard_map/ppermute | solution.py:573
  329.5 30.8 %collective-permute-start.42 = (bf16[192,384]{1,0:T(8,128)(2,1)S(1)}, bf16[192,384]{1,0:T(8,128)(2,1)S(1)}, u32[]{:S(2)}, u32[]{:S(2)}) collective-permute-start(bf16[192,384]{1,0:T(8,128)(2,1)S(1)} %get-tuple-element.644), channel_id=1, source_target_pairs={{0,1},{1,2},{2,3},{3,0},{4,5},{5,6},{6,7},{7,4},{8,9},{9,10},{10,1... | collective-permute-start | bytes 442376 | tf_op jit(solution)/shard_map/ppermute | solution.py:573
  361.9 26.8 %collective-permute-start.43 = (bf16[384,1536]{1,0:T(8,128)(2,1)S(1)}, bf16[384,1536]{1,0:T(8,128)(2,1)S(1)}, u32[]{:S(2)}, u32[]{:S(2)}) collective-permute-start(bf16[384,1536]{1,0:T(8,128)(2,1)S(1)} %constant_dynamic-slice_fusion), channel_id=1, source_target_pairs={{0,1},{1,2},{2,3},{3,0},{4,5},{5,6},{6,7},{7,4},{8,9},{9,10},{10,1... | collective-permute-start | bytes 3538952 | tf_op jit(solution)/shard_map/ppermute | solution.py:573
  394.2 25.9 %collective-permute-start.44 = (bf16[384,1536]{1,0:T(8,128)(2,1)S(1)}, bf16[384,1536]{1,0:T(8,128)(2,1)S(1)}, u32[]{:S(2)}, u32[]{:S(2)}) collective-permute-start(bf16[384,1536]{1,0:T(8,128)(2,1)S(1)} %add_convert_fusion.2), channel_id=1, source_target_pairs={{0,1},{1,2},{2,3},{3,0},{4,5},{5,6},{6,7},{7,4},{8,9},{9,10},{10,1... | collective-permute-start | bytes 3538952 | tf_op jit(solution)/shard_map/ppermute | solution.py:573
  423.6 30.2 %collective-permute-start.47 = (bf16[384,1536]{1,0:T(8,128)(2,1)S(1)}, bf16[384,1536]{1,0:T(8,128)(2,1)S(1)}, u32[]{:S(2)}, u32[]{:S(2)}) collective-permute-start(bf16[384,1536]{1,0:T(8,128)(2,1)S(1)} %add_convert_fusion.1), channel_id=1, source_target_pairs={{0,1},{1,2},{2,3},{3,0},{4,5},{5,6},{6,7},{7,4},{8,9},{9,10},{10,1... | collective-permute-start | bytes 3538952 | tf_op jit(solution)/shard_map/ppermute | solution.py:573
  428.5 25.2 %collective-permute-start.49 = (bf16[192,384]{1,0:T(8,128)(2,1)S(1)}, bf16[192,384]{1,0:T(8,128)(2,1)S(1)}, u32[]{:S(2)}, u32[]{:S(2)}) collective-permute-start(bf16[192,384]{1,0:T(8,128)(2,1)S(1)} %copy-done.36), channel_id=1, source_target_pairs={{0,1},{1,2},{2,3},{3,0},{4,5},{5,6},{6,7},{7,4},{8,9},{9,10},{10,1... | collective-permute-start | bytes 442376 | tf_op jit(solution)/shard_map/ppermute | solution.py:573
  (76 other events, 888.7 us)
Sparse Core Ops, SparseCore 0:
  42.9 69.8 all-gather.1
  240.4 55.6 reduce-scatter.4
  299.9 46.2 reduce-scatter.10
  349.3 61.7 reduce-scatter.8
  414.9 55.7 reduce-scatter.6

commit v5 on v4

--- a/solution.py
+++ b/solution.py
@@ -622,6 +622,24 @@
     return whole
 
 
+def sides():
+    size = lax.axis_size("dp")
+    return [list(range(0, size, 2)), list(range(1, size, 2))]
+
+
+def by_side(whole, me):
+    rows = whole.shape[0] // lax.axis_size("dp")
+    split = whole.reshape(-1, 2, rows, whole.shape[1])
+    return [
+        lax.dynamic_index_in_dim(split, side, 1, keepdims=False).reshape(-1, whole.shape[1])
+        for side in (me % 2, 1 - me % 2)
+    ]
+
+
+def side_scatter(whole):
+    return lax.psum_scatter(whole, "dp", scatter_dimension=0, tiled=True, axis_index_groups=sides())
+
+
 def rows_major(value):
     return with_layout_constraint(value, Layout(major_to_minor=(0, 1)))
 
@@ -724,10 +742,8 @@
         fresh = None
         if t + 1 < chunks:
             fresh, *kept_att = attend(t + 1, block, q8, aq, kn, ak, vl, og, kept_att)
-        if t == 1:
-            out_p = gather_3(out_p)
         if t == 2:
-            out_all = assemble(out_p, me_d)
+            out_all = assemble(gather_3(out_p), me_d)
         chunk = t - first
         if 0 <= chunk < chunks:
             outs = feed(chunk, block, own, at, x, cot, gains, out_all, ffn_all, us[chunk], kept_ffn)
@@ -780,44 +796,51 @@
     )
     y_acc, dp_all, gt, g0, out_acc = tie((y_acc, dp_all, gt, g0, out_acc))
 
-    send = token_part(gt, 1)
-    send, dp_all, y_acc, out_acc = tie((send, dp_all, y_acc, out_acc))
+    send, out_send = token_part(gt, 1), None
+    if out_step < tp:
+        out_send, out_step = add(out_acc, ring[out_step]), out_step + 1
+    send, dp_all, y_acc, out_acc, out_send, sums[1] = tie((send, dp_all, y_acc, out_acc, out_send, sums[1]))
     back = turn(send)
-    fill = product(hn, dp_all)
-    back, fill, g0, gq, gb = tie((back, fill, g0, gq, gb))
-    sums.append(scatter(fill))
+    if out_send is not None:
+        out_acc = turn(out_send)
+    attn_mine, attn_other = by_side(product(hn, dp_all), me_d)
     while y_step < tp:
         y_acc, y_step = turn(add(y_acc, token_part(part, y_step))), y_step + 1
+    result = total_of((y_acc, token_part(part, 0))).astype(BF)
+    grad_down = jnp.transpose(sums[1].astype(F32))
     gq = gq[0:2].reshape(2, heads, 64).sum(1)
     gb = lax.dynamic_update_slice_in_dim(
         jnp.zeros(forget_bias.shape, F32), gb[0, 2 * heads : 2 * heads + heads_real], me_t * heads_real, 0
     )
     small = jnp.concatenate([gq.reshape(-1), gb])
     small = jnp.pad(small, (0, model - small.shape[0]))[None]
-    hops = [("dp", 1 << i) for i in range(dp.bit_length() - 1)]
-    flat = None
+    flat = jnp.concatenate([g0[0:1], gmid, small, jnp.zeros((5, model), F32)], 0)
+    back, attn_mine, attn_other, flat, result, grad_down, out_acc = tie(
+        (back, attn_mine, attn_other, flat, result, grad_down, out_acc)
+    )
+    hops = [("dp", 1 << i) for i in range(dp.bit_length() - 1)] + [("tp", 1 << i) for i in range(tp.bit_length() - 1)]
     for s in range(2, tp):
         send = add(back, token_part(gt, s))
         out_send = None
-        if flat is None:
-            flat = jnp.concatenate([g0[0:1], gmid, small, jnp.zeros((5, model), F32)], 0)
-        elif out_step < tp:
+        if out_step < tp:
             out_send, out_step = add(out_acc, ring[out_step]), out_step + 1
-        send, flat, out_send, y_acc = tie((send, flat, out_send, y_acc))
+        send, flat, out_send, attn_other = tie((send, flat, out_send, attn_other))
         back = turn(send)
         if out_send is not None:
             out_acc = turn(out_send)
+        attn_sum = add(attn_mine, swap(attn_other, "dp", 1)) if s == 2 else None
         for _ in range(2):
             if hops:
                 flat = flat + swap(flat, *hops.pop(0))
-        back, flat, out_acc = tie((back, flat, out_acc))
+        back, flat, out_acc, attn_sum = tie((back, flat, out_acc, attn_sum))
+        if attn_sum is not None:
+            sums.append(side_scatter(attn_sum))
     while out_step < tp:
         out_acc, out_step = turn(add(out_acc, ring[out_step])), out_step + 1
-    for axis, bit in hops + [("tp", 1 << i) for i in range(tp.bit_length() - 1)]:
+    for axis, bit in hops:
         flat = flat + swap(flat, axis, bit)
-    result, back, gt = tie((total_of((y_acc, token_part(part, 0))).astype(BF), back, gt))
     grad_tokens = total_of((token_part(gt, 0), back))
-    grad_down, grad_gu, grad_attn = [value.astype(F32) for value in sums[1:]]
+    grad_gu, grad_attn = [value.astype(F32) for value in sums[2:]]
     grad_out_own = total_of((ring[0], out_acc))
     norm_grad = flat[0:2]
     qk_grad = flat[2, : 2 * 64].reshape(2, 64)
@@ -832,7 +855,7 @@
         jnp.transpose(grad_gates, (1, 0, 2)),
         jnp.transpose(grad_out_own[:, :width_real]),
         jnp.stack([grad_gu[:, :hidden], grad_gu[:, hidden:]]),
-        jnp.transpose(grad_down),
+        grad_down,
         norm_grad,
         qk_grad,
         bias_grad,

time: 491 us -> 485 us (0.988)
  starting transfers between devices: 42.6 us -> 48.9 us
    ppermute x23 -> x24, waiting for transfers between devices: 18 us -> 43.1 us  [swap(): return lax.ppermute(value, axis, [(i, i ^ bit) for i in range(size)])]
    ppermute x30, waiting for transfers between devices: 109 us -> 85.6 us  [turn(): return lax.ppermute(value, 'tp', [(i, (i + 1) % size) for i in range(size)])]
    ppermute x23 -> x24, starting transfers between devices: 13.9 us -> 16.9 us  [swap(): return lax.ppermute(value, axis, [(i, i ^ bit) for i in range(size)])]
    convert_element_type x14 -> x15, other arithmetic: 13.1 us -> 13.1 us  [add(): return (a.astype(F32) + b.astype(F32)).astype(BF)]
  transfers between devices with their start and end apart: 58 -> 59, of which waited for: 28 -> 26; matrix products, arithmetic and copies ran while one was open for 22% -> 21% of each run, Pallas kernels for 36% -> 36%
where the time goes in v5:
time: 485 us; the launch traced here: 476 us
  Pallas kernels  173 us (36%)
  waiting for transfers between devices  129 us (27%)
  matrix products  49.2 us (10%)
  starting transfers between devices  48.9 us (10%)
  local copies, waits for them, and re-layouts  31.8 us (7%)
  other arithmetic  28.9 us (6%)
  between operations  15.4 us (3%)
    ppermute x30, waiting for transfers between devices, turn(): return lax.ppermute(value, 'tp', [(i, (i + 1) % size) for i in range(size)])  85.6 us
    pallas_call x3, Pallas kernels, feed(): pl.pallas_call(functools.partial(ffn_kernel, count, chunk, block, step_ro...  67.4 us
    dot_general x4, matrix products, dot(): return lax.dot_general(a, b, dims, preferred_element_type=F32)  49.2 us
    ppermute x24, waiting for transfers between devices, swap(): return lax.ppermute(value, axis, [(i, i ^ bit) for i in range(size)])  43.1 us
    pallas_call x2, Pallas kernels, attend_back(): pl.pallas_call(functools.partial(bwd_kernel, begin, heads, block), grid=(...  35.7 us
    ppermute x30, starting transfers between devices, turn(): return lax.ppermute(value, 'tp', [(i, (i + 1) % size) for i in range(size)])  31.4 us
    pallas_call x1, Pallas kernels, post(): pl.pallas_call(functools.partial(post_kernel, heads, groups), grid=(count...  27.6 us
    pallas_call x1, Pallas kernels, pre(): pl.pallas_call(functools.partial(pre_kernel, heads, spots), grid=(seq //...  22.1 us
  transfers between devices with their start and end apart: 59, of which 26 were waited for; matrix products, arithmetic and copies ran while one was open for 21% of the time, Pallas kernels for 36%

profile of v5, /device:TPU:0, one launch (start us, length us, event | category | flops | bytes accessed | tf_op | source)
XLA Modules:
  0.0 476.3 jit_solution(6809389359490793633)
XLA Ops:
  16.3 6.0 %collective-permute-done.3 = bf16[192,384]{1,0:T(8,128)(2,1)} collective-permute-done((bf16[192,384]{1,0:T(8,128)(2,1)S(1)}, bf16[192,384]{1,0:T(8,128)(2,1)}, u32[]{:S(2)}, u32[]{:S(2)}) %collective-permute-start.3) | collective-permute-done | bytes 147488 | tf_op jit(solution)/shard_map/ppermute | solution.py:573
  23.4 6.0 %collective-permute-done.4 = bf16[192,384]{1,0:T(8,128)(2,1)S(1)} collective-permute-done((bf16[192,384]{1,0:T(8,128)(2,1)}, bf16[192,384]{1,0:T(8,128)(2,1)S(1)}, u32[]{:S(2)}, u32[]{:S(2)}) %collective-permute-start.4) | collective-permute-done | bytes 147488 | tf_op jit(solution)/shard_map/ppermute | solution.py:573
  33.9 5.5 %collective-permute-done.9 = bf16[192,384]{1,0:T(8,128)(2,1)S(1)} collective-permute-done((bf16[192,384]{1,0:T(8,128)(2,1)S(1)}, bf16[192,384]{1,0:T(8,128)(2,1)S(1)}, u32[]{:S(2)}, u32[]{:S(2)}) %collective-permute-start.9) | collective-permute-done | bytes 147488 | tf_op jit(solution)/shard_map/ppermute | solution.py:573
  48.6 22.1 %pre.1 = (bf16[1536,1536]{1,0:T(8,128)(2,1)}, bf16[1536,1664]{1,0:T(8,128)(2,1)}, f32[8,1536]{1,0:T(8,128)}, bf16[1536,384]{1,0:T(8,128)(2,1)}, bf16[1536,384]{1...) custom-call(s32[1]{0:T(128)} %bitcast.me_ref, ...), custom_call_target="tpu_custom_call" | custom-call | flops 1 | bytes 1 | tf_op jit(solution)/shard_map/pre/pallas_call | solution.py:164
  70.7 5.3 %attend.3 = (bf16[512,384]{1,0:T(8,128)(2,1)}, f32[1536,384]{1,0:T(8,128)}, f32[1536,384]{1,0:T(8,128)}) custom-call(bf16[1536,384]{1,0:T(8,128)(2,1)} %get-tuple-element.588.q_ref, bf16[1536,128]{1,0:T(8,128)(2,1)} %get-tuple-element.377.aq_ref, bf16[1536,384]{1,0:T(8,128)(2,1)} %get-tuple-element.378.k_ref, bf16[1536,128]{1,0:T(8,128)(2,1)} %get-tuple-element.379.ak_ref, ...), custom_call_target="tpu_custom_call" | custom-call | flops 1 | bytes 1 | tf_op jit(solution)/shard_map/attend/pallas_call | solution.py:225
  79.8 6.3 %attend.4 = (bf16[512,384]{1,0:T(8,128)(2,1)}, f32[1536,384]{1,0:T(8,128)}, f32[1536,384]{1,0:T(8,128)}) custom-call(bf16[1536,384]{1,0:T(8,128)(2,1)} %get-tuple-element.588.q_ref, bf16[1536,128]{1,0:T(8,128)(2,1)} %get-tuple-element.377.aq_ref, bf16[1536,384]{1,0:T(8,128)(2,1)} %get-tuple-element.378.k_ref, ...), custom_call_target="tpu_custom_call", output_to_operand_aliasing={{1}: (6, {}), {2}: (7, {})} | custom-call | flops 1 | bytes 1 | tf_op jit(solution)/shard_map/attend/pallas_call | solution.py:225
  95.7 8.9 %attend.5 = (bf16[512,384]{1,0:T(8,128)(2,1)}, f32[1536,384]{1,0:T(8,128)}, f32[1536,384]{1,0:T(8,128)}) custom-call(bf16[1536,384]{1,0:T(8,128)(2,1)} %get-tuple-element.588.q_ref, bf16[1536,128]{1,0:T(8,128)(2,1)} %get-tuple-element.377.aq_ref, bf16[1536,384]{1,0:T(8,128)(2,1)} %get-tuple-element.378.k_ref, ...), custom_call_target="tpu_custom_call", output_to_operand_aliasing={{1}: (6, {}), {2}: (7, {})} | custom-call | flops 1 | bytes 1 | tf_op jit(solution)/shard_map/attend/pallas_call | solution.py:225
  104.6 5.4 %collective-permute-done.21 = bf16[96,1536]{1,0:T(8,128)(2,1)} collective-permute-done((bf16[96,1536]{1,0:T(8,128)(2,1)}, bf16[96,1536]{1,0:T(8,128)(2,1)}, u32[]{:S(2)}, u32[]{:S(2)}) %collective-permute-start.21) | collective-permute-done | bytes 294944 | tf_op jit(solution)/shard_map/ppermute | solution.py:568
  126.4 7.0 %collective-permute-done.23.refs_2_ = bf16[512,384]{1,0:T(8,128)(2,1)} collective-permute-done((bf16[512,384]{1,0:T(8,128)(2,1)S(1)}, bf16[512,384]{1,0:T(8,128)(2,1)}, u32[]{:S(2)}, u32[]{:S(2)}) %collective-permute-start.23) | collective-permute-done | bytes 393248 | tf_op jit(solution)/shard_map/ppermute | solution.py:573
  133.4 7.5 %collective-permute-done.24.refs_1_ = bf16[512,384]{1,0:T(8,128)(2,1)} collective-permute-done((bf16[512,384]{1,0:T(8,128)(2,1)}, bf16[512,384]{1,0:T(8,128)(2,1)}, u32[]{:S(2)}, u32[]{:S(2)}) %collective-permute-start.24) | collective-permute-done | bytes 393248 | tf_op jit(solution)/shard_map/ppermute | solution.py:573
  142.5 22.0 %feed.3 = (bf16[1536,1536]{1,0:T(8,128)(2,1)}, bf16[1536,1024]{1,0:T(8,128)(2,1)}, bf16[1536,2048]{1,0:T(8,128)(2,1)}, bf16[1536,1536]{1,0:T(8,128)(2,1)}, bf16[...) custom-call(s32[1]{0:T(128)} %bitcast.12.at_ref, ...), custom_call_target="tpu_custom_call" | custom-call | flops 1 | bytes 1 | tf_op jit(solution)/shard_map/feed/pallas_call | solution.py:344
  168.4 22.8 %feed.4 = (bf16[1536,1536]{1,0:T(8,128)(2,1)}, bf16[1536,1024]{1,0:T(8,128)(2,1)}, bf16[1536,2048]{1,0:T(8,128)(2,1)}, bf16[1536,1536]{1,0:T(8,128)(2,1)}, bf16[...) custom-call(s32[1]{0:T(128)} %bitcast.12.at_ref, ...), custom_call_target="tpu_custom_call", output_to_operand_aliasing={{0}: (10, {}), {1}: (11, {}), {2}: (12, {}), {3}: (13, {}),... | custom-call | flops 1 | bytes 1 | tf_op jit(solution)/shard_map/feed/pallas_call | solution.py:344
  192.6 22.6 %feed.5 = (bf16[1536,1536]{1,0:T(8,128)(2,1)}, bf16[1536,1024]{1,0:T(8,128)(2,1)}, bf16[1536,2048]{1,0:T(8,128)(2,1)}, bf16[1536,1536]{1,0:T(8,128)(2,1)}, bf16[...) custom-call(s32[1]{0:T(128)} %bitcast.12.at_ref, ...), custom_call_target="tpu_custom_call", output_to_operand_aliasing={{0}: (10, {}), {1}: (11, {}), {2}: (12, {}), {3}: (13, {}),... | custom-call | flops 1 | bytes 1 | tf_op jit(solution)/shard_map/feed/pallas_call | solution.py:344
  220.1 12.3 %convolution_convert_fusion.2 = bf16[1536,1536]{1,0:T(8,128)(2,1)} fusion(bf16[1536,1536]{1,0:T(8,128)(2,1)} %get-tuple-element.627.res_ref, bf16[1536,1536]{1,0:T(8,128)(2,1)} %get-tuple-element.540), kind=kOutput, calls=%fused_computation.2 | convolution fusion | flops 7250116608 | bytes 14155776 | tf_op jit(solution)/shard_map/dot_general | solution.py:24
  232.3 8.9 %fusion = bf16[1536,1024]{1,0:T(8,128)(2,1)} fusion(bf16[1536,1024]{1,0:T(8,128)(2,1)S(1)} %copy-done, bf16[1,1536,1536]{2,1,0:T(8,128)(2,1)} %param.36), kind=kOutput, calls=%fused_computation.5 | convolution fusion | flops 4833411072 | bytes 11010048 | tf_op jit(solution)/shard_map/dot_general | solution.py:24
  248.2 15.8 %convolution_convert_fusion.1 = bf16[1536,2048]{1,0:T(8,128)(2,1)} fusion(bf16[1536,1536]{1,0:T(8,128)(2,1)} %get-tuple-element.563, bf16[1536,2048]{1,0:T(8,128)(2,1)} %get-tuple-element.564), kind=kOutput, calls=%fused_computation.1 | convolution fusion | flops 9666822144 | bytes 17301504 | tf_op jit(solution)/shard_map/dot_general | solution.py:24
  269.8 9.8 %collective-permute-done.39 = bf16[512,384]{1,0:T(8,128)(2,1)S(1)} collective-permute-done((bf16[512,384]{1,0:T(8,128)(2,1)S(1)}, bf16[512,384]{1,0:T(8,128)(2,1)S(1)}, u32[]{:S(2)}, u32[]{:S(2)}) %collective-permute-start.39) | collective-permute-done | bytes 393248 | tf_op jit(solution)/shard_map/ppermute | solution.py:573
  282.0 12.7 %attend_back.2 = (f32[1536,128]{1,0:T(8,128)}, f32[1536,128]{1,0:T(8,128)}, f32[1536,128]{1,0:T(8,128)}, f32[1536,128]{1,0:T(8,128)}) custom-call(bf16[1536,384]{1,0:T(8,128)(2,1)} %get-tuple-element.588.q_ref, bf16[1536,128]{1,0:T(8,128)(2,1)} %get-tuple-element.377.aq_ref, bf16[1536,384]{1,0:T(8,128)(2,1)} %get-tuple-element.378.k_ref, ...), custom_call_target="tpu_custom_call" | custom-call | flops 1 | bytes 1 | tf_op jit(solution)/shard_map/attend_back/pallas_call | solution.py:437
  302.9 23.0 %attend_back.3 = (f32[1536,256]{1,0:T(8,128)}, f32[1536,256]{1,0:T(8,128)}, f32[1536,256]{1,0:T(8,128)}, f32[1536,128]{1,0:T(8,128)}) custom-call(bf16[1536,384]{1,0:T(8,128)(2,1)} %get-tuple-element.588.q_ref, bf16[1536,128]{1,0:T(8,128)(2,1)} %get-tuple-element.377.aq_ref, bf16[1536,384]{1,0:T(8,128)(2,1)} %get-tuple-element.378.k_ref, ...), custom_call_target="tpu_custom_call" | custom-call | flops 1 | bytes 1 | tf_op jit(solution)/shard_map/attend_back/pallas_call | solution.py:437
  330.5 27.6 %post.1 = (bf16[1536,1664]{1,0:T(8,128)(2,1)}, bf16[1536,1536]{1,0:T(8,128)(2,1)}, f32[8,1536]{1,0:T(8,128)}, f32[8,384]{1,0:T(8,128)}, f32[8,128]{1,0:T(8,128)}) custom-call(bf16[1536,384]{1,0:T(8,128)(2,1)} %get-tuple-element.620.q_ref, bf16[1536,384]{1,0:T(8,128)(2,1)} %get-tuple-element.621.ks_ref, bf16[1536,384]{1,0:T(8,128)(2,1)} %get-tuple-element.622.kd_ref, ...), custom_call_target="tpu_custom_call" | custom-call | flops 1 | bytes 1 | tf_op jit(solution)/shard_map/post/pallas_call | solution.py:547
  366.1 12.2 %convolution_convert_fusion = bf16[1536,1664]{1,0:T(8,128)(2,1)S(1)} fusion(bf16[1536,1536]{1,0:T(8,128)(2,1)} %get-tuple-element.648, bf16[1536,1664]{1,0:T(8,128)(2,1)} %get-tuple-element.649), kind=kOutput, calls=%fused_computation | convolution fusion | flops 7854292992 | bytes 14942208 | tf_op jit(solution)/shard_map/dot_general | solution.py:24
  382.4 9.0 %collective-permute-done.44 = bf16[192,384]{1,0:T(8,128)(2,1)S(1)} collective-permute-done((bf16[192,384]{1,0:T(8,128)(2,1)S(1)}, bf16[192,384]{1,0:T(8,128)(2,1)S(1)}, u32[]{:S(2)}, u32[]{:S(2)}) %collective-permute-start.44) | collective-permute-done | bytes 147488 | tf_op jit(solution)/shard_map/ppermute | solution.py:573
  404.5 21.9 %collective-permute-done.48 = bf16[192,384]{1,0:T(8,128)(2,1)S(1)} collective-permute-done((bf16[192,384]{1,0:T(8,128)(2,1)S(1)}, bf16[192,384]{1,0:T(8,128)(2,1)S(1)}, u32[]{:S(2)}, u32[]{:S(2)}) %collective-permute-start.48) | collective-permute-done | bytes 147488 | tf_op jit(solution)/shard_map/ppermute | solution.py:573
  435.7 22.7 %collective-permute-done.52 = f32[8,1536]{1,0:T(8,128)S(1)} collective-permute-done((f32[8,1536]{1,0:T(8,128)S(1)}, f32[8,1536]{1,0:T(8,128)S(1)}, u32[]{:S(2)}, u32[]{:S(2)}) %collective-permute-start.52) | collective-permute-done | bytes 49184 | tf_op jit(solution)/shard_map/ppermute | solution.py:568
  (268 shorter events, 137.7 us)
Async XLA Ops:
  7.2 135.3 %all-gather.2.cloned.1.call-start = ((), (), s32[]{:S(2)}) async-start(), calls=%async_computation.4 | async-start | bytes 10616832 | tf_op jit(solution)/shard_map/all_gather | solution.py:715
  42.8 258.4 %reduce-scatter.5.cloned.1.call-start = ((), (), s32[]{:S(2)}) async-start(), calls=%async_computation.5 | async-start | bytes 5308416 | tf_op jit(solution)/shard_map/reduce_scatter | solution.py:648
  42.9 27.8 %collective-permute-start.12 = (bf16[192,1536]{1,0:T(8,128)(2,1)S(1)}, bf16[192,1536]{1,0:T(8,128)(2,1)}, u32[]{:S(2)}, u32[]{:S(2)}) collective-permute-start(bf16[192,1536]{1,0:T(8,128)(2,1)S(1)} %pad_maximum_fusion.3), channel_id=1, source_target_pairs={{0,4},{4,0},{8,12},{12,8},{16,20},{20,16},{24,28},{28,24},{1,5},{5... | collective-permute-start | bytes 1769480 | tf_op jit(solution)/shard_map/ppermute | solution.py:568
  42.9 27.8 %collective-permute-start.13 = (bf16[192,1536]{1,0:T(8,128)(2,1)S(1)}, bf16[192,1536]{1,0:T(8,128)(2,1)S(1)}, u32[]{:S(2)}, u32[]{:S(2)}) collective-permute-start(bf16[192,1536]{1,0:T(8,128)(2,1)S(1)} %pad_maximum_fusion.3), channel_id=1, source_target_pairs={{0,8},{4,12},{8,0},{12,4},{16,24},{20,28},{24,16},{28,20},{1,9},{5... | collective-permute-start | bytes 1769480 | tf_op jit(solution)/shard_map/ppermute | solution.py:568
  43.5 27.2 %collective-permute-start.14 = (bf16[192,1536]{1,0:T(8,128)(2,1)S(1)}, bf16[192,1536]{1,0:T(8,128)(2,1)S(1)}, u32[]{:S(2)}, u32[]{:S(2)}) collective-permute-start(bf16[192,1536]{1,0:T(8,128)(2,1)S(1)} %pad_maximum_fusion.3), channel_id=1, source_target_pairs={{0,16},{4,20},{8,24},{12,28},{16,0},{20,4},{24,8},{28,12},{1,17},{... | collective-permute-start | bytes 1769480 | tf_op jit(solution)/shard_map/ppermute | solution.py:568
  79.3 30.6 %collective-permute-start.18 = (bf16[192,1536]{1,0:T(8,128)(2,1)S(1)}, bf16[192,1536]{1,0:T(8,128)(2,1)S(1)}, u32[]{:S(2)}, u32[]{:S(2)}) collective-permute-start(bf16[192,1536]{1,0:T(8,128)(2,1)S(1)} %collective-permute-done.13), channel_id=1, source_target_pairs={{0,4},{4,0},{8,12},{12,8},{16,20},{20,16},{24,28},{28,24},{1,5},{5... | collective-permute-start | bytes 1769480 | tf_op jit(solution)/shard_map/ppermute | solution.py:568
  79.3 30.6 %collective-permute-start.19 = (bf16[192,1536]{1,0:T(8,128)(2,1)S(1)}, bf16[192,1536]{1,0:T(8,128)(2,1)S(1)}, u32[]{:S(2)}, u32[]{:S(2)}) collective-permute-start(bf16[192,1536]{1,0:T(8,128)(2,1)S(1)} %collective-permute-done.14), channel_id=1, source_target_pairs={{0,4},{4,0},{8,12},{12,8},{16,20},{20,16},{24,28},{28,24},{1,5},{5... | collective-permute-start | bytes 1769480 | tf_op jit(solution)/shard_map/ppermute | solution.py:568
  113.7 27.2 %collective-permute-start.24 = (bf16[512,384]{1,0:T(8,128)(2,1)}, bf16[512,384]{1,0:T(8,128)(2,1)}, u32[]{:S(2)}, u32[]{:S(2)}) collective-permute-start(bf16[512,384]{1,0:T(8,128)(2,1)} %get-tuple-element.409.refs_0_), channel_id=1, source_target_pairs={{0,1},{1,2},{2,3},{3,0},{4,5},{5,6},{6,7},{7,4},{8,9},{9,10},{10,1... | collective-permute-start | bytes 1179656 | tf_op jit(solution)/shard_map/ppermute | solution.py:573
  164.5 26.7 %collective-permute-start.30 = (bf16[512,384]{1,0:T(8,128)(2,1)}, bf16[512,384]{1,0:T(8,128)(2,1)S(1)}, u32[]{:S(2)}, u32[]{:S(2)}) collective-permute-start(bf16[512,384]{1,0:T(8,128)(2,1)} %get-tuple-element.454), channel_id=1, source_target_pairs={{0,1},{1,2},{2,3},{3,0},{4,5},{5,6},{6,7},{7,4},{8,9},{9,10},{10,1... | collective-permute-start | bytes 1179656 | tf_op jit(solution)/shard_map/ppermute | solution.py:573
  164.8 26.4 %collective-permute-start.29 = (bf16[512,384]{1,0:T(8,128)(2,1)S(1)}, bf16[512,384]{1,0:T(8,128)(2,1)S(1)}, u32[]{:S(2)}, u32[]{:S(2)}) collective-permute-start(bf16[512,384]{1,0:T(8,128)(2,1)S(1)} %collective-permute-done.28.refs_2_), channel_id=1, source_target_pairs={{0,1},{1,2},{2,3},{3,0},{4,5},{5,6},{6,7},{7,4},{8,9},{9,10},{10,1... | collective-permute-start | bytes 1179656 | tf_op jit(solution)/shard_map/ppermute | solution.py:573
  216.1 25.1 %collective-permute-start.33 = (bf16[512,384]{1,0:T(8,128)(2,1)}, bf16[512,384]{1,0:T(8,128)(2,1)}, u32[]{:S(2)}, u32[]{:S(2)}) collective-permute-start(bf16[512,384]{1,0:T(8,128)(2,1)} %get-tuple-element.531), channel_id=1, source_target_pairs={{0,1},{1,2},{2,3},{3,0},{4,5},{5,6},{6,7},{7,4},{8,9},{9,10},{10,1... | collective-permute-start | bytes 1179656 | tf_op jit(solution)/shard_map/ppermute | solution.py:573
  216.4 24.8 %collective-permute-start.34 = (bf16[512,384]{1,0:T(8,128)(2,1)S(1)}, bf16[512,384]{1,0:T(8,128)(2,1)}, u32[]{:S(2)}, u32[]{:S(2)}) collective-permute-start(bf16[512,384]{1,0:T(8,128)(2,1)S(1)} %get-tuple-element.532), channel_id=1, source_target_pairs={{0,1},{1,2},{2,3},{3,0},{4,5},{5,6},{6,7},{7,4},{8,9},{9,10},{10,1... | collective-permute-start | bytes 1179656 | tf_op jit(solution)/shard_map/ppermute | solution.py:573
  243.8 117.7 %reduce-scatter.7.cloned.1.call-start = ((), (), s32[]{:S(2)}) async-start(), calls=%async_computation.6 | async-start | bytes 3538944 | tf_op jit(solution)/shard_map/reduce_scatter | solution.py:648
  248.1 180.0 %reduce-scatter.11.cloned.1.call-start = ((), (), s32[]{:S(2)}) async-start(), calls=%async_computation.8 | async-start | bytes 7077888 | tf_op jit(solution)/shard_map/reduce_scatter | solution.py:648
  267.1 32.5 %collective-permute-start.38 = (bf16[384,1536]{1,0:T(8,128)(2,1)S(1)}, bf16[384,1536]{1,0:T(8,128)(2,1)S(1)}, u32[]{:S(2)}, u32[]{:S(2)}) collective-permute-start(bf16[384,1536]{1,0:T(8,128)(2,1)S(1)} %constant_dynamic-slice_fusion.3), channel_id=1, source_target_pairs={{0,1},{1,2},{2,3},{3,0},{4,5},{5,6},{6,7},{7,4},{8,9},{9,10},{10,1... | collective-permute-start | bytes 3538952 | tf_op jit(solution)/shard_map/ppermute | solution.py:573
  302.4 25.2 %collective-permute-start.40 = (bf16[384,1536]{1,0:T(8,128)(2,1)S(1)}, bf16[384,1536]{1,0:T(8,128)(2,1)S(1)}, u32[]{:S(2)}, u32[]{:S(2)}) collective-permute-start(bf16[384,1536]{1,0:T(8,128)(2,1)S(1)} %add_convert_fusion.5), channel_id=1, source_target_pairs={{0,1},{1,2},{2,3},{3,0},{4,5},{5,6},{6,7},{7,4},{8,9},{9,10},{10,1... | collective-permute-start | bytes 3538952 | tf_op jit(solution)/shard_map/ppermute | solution.py:573
  302.5 162.9 %reduce-scatter.9.cloned.1.call-start = ((), (), s32[]{:S(2)}) async-start(), calls=%async_computation.7 | async-start | bytes 3194880 | tf_op jit(solution)/shard_map/reduce_scatter | solution.py:640
  329.2 30.8 %collective-permute-start.41 = (bf16[384,1536]{1,0:T(8,128)(2,1)S(1)}, bf16[384,1536]{1,0:T(8,128)(2,1)S(1)}, u32[]{:S(2)}, u32[]{:S(2)}) collective-permute-start(bf16[384,1536]{1,0:T(8,128)(2,1)S(1)} %add_convert_fusion.4), channel_id=1, source_target_pairs={{0,1},{1,2},{2,3},{3,0},{4,5},{5,6},{6,7},{7,4},{8,9},{9,10},{10,1... | collective-permute-start | bytes 3538952 | tf_op jit(solution)/shard_map/ppermute | solution.py:573
  329.3 30.7 %collective-permute-start.42 = (bf16[192,384]{1,0:T(8,128)(2,1)S(1)}, bf16[192,384]{1,0:T(8,128)(2,1)S(1)}, u32[]{:S(2)}, u32[]{:S(2)}) collective-permute-start(bf16[192,384]{1,0:T(8,128)(2,1)S(1)} %get-tuple-element.640), channel_id=1, source_target_pairs={{0,1},{1,2},{2,3},{3,0},{4,5},{5,6},{6,7},{7,4},{8,9},{9,10},{10,1... | collective-permute-start | bytes 442376 | tf_op jit(solution)/shard_map/ppermute | solution.py:573
  362.3 29.1 %collective-permute-start.43 = (bf16[384,1536]{1,0:T(8,128)(2,1)S(1)}, bf16[384,1536]{1,0:T(8,128)(2,1)S(1)}, u32[]{:S(2)}, u32[]{:S(2)}) collective-permute-start(bf16[384,1536]{1,0:T(8,128)(2,1)S(1)} %constant_dynamic-slice_fusion.2), channel_id=1, source_target_pairs={{0,1},{1,2},{2,3},{3,0},{4,5},{5,6},{6,7},{7,4},{8,9},{9,10},{10,1... | collective-permute-start | bytes 3538952 | tf_op jit(solution)/shard_map/ppermute | solution.py:573
  364.5 27.0 %collective-permute-start.44 = (bf16[192,384]{1,0:T(8,128)(2,1)S(1)}, bf16[192,384]{1,0:T(8,128)(2,1)S(1)}, u32[]{:S(2)}, u32[]{:S(2)}) collective-permute-start(bf16[192,384]{1,0:T(8,128)(2,1)S(1)} %add_convert_fusion.16), channel_id=1, source_target_pairs={{0,1},{1,2},{2,3},{3,0},{4,5},{5,6},{6,7},{7,4},{8,9},{9,10},{10,1... | collective-permute-start | bytes 442376 | tf_op jit(solution)/shard_map/ppermute | solution.py:573
  393.1 33.3 %collective-permute-start.45 = (bf16[384,1536]{1,0:T(8,128)(2,1)S(1)}, bf16[384,1536]{1,0:T(8,128)(2,1)S(1)}, u32[]{:S(2)}, u32[]{:S(2)}) collective-permute-start(bf16[384,1536]{1,0:T(8,128)(2,1)S(1)} %add_convert_fusion.2), channel_id=1, source_target_pairs={{0,1},{1,2},{2,3},{3,0},{4,5},{5,6},{6,7},{7,4},{8,9},{9,10},{10,1... | collective-permute-start | bytes 3538952 | tf_op jit(solution)/shard_map/ppermute | solution.py:573
  399.5 26.9 %collective-permute-start.48 = (bf16[192,384]{1,0:T(8,128)(2,1)S(1)}, bf16[192,384]{1,0:T(8,128)(2,1)S(1)}, u32[]{:S(2)}, u32[]{:S(2)}) collective-permute-start(bf16[192,384]{1,0:T(8,128)(2,1)S(1)} %add_convert_fusion.15), channel_id=1, source_target_pairs={{0,1},{1,2},{2,3},{3,0},{4,5},{5,6},{6,7},{7,4},{8,9},{9,10},{10,1... | collective-permute-start | bytes 442376 | tf_op jit(solution)/shard_map/ppermute | solution.py:573
  428.0 30.4 %collective-permute-start.50 = (bf16[384,1536]{1,0:T(8,128)(2,1)S(1)}, bf16[384,1536]{1,0:T(8,128)(2,1)S(1)}, u32[]{:S(2)}, u32[]{:S(2)}) collective-permute-start(bf16[384,1536]{1,0:T(8,128)(2,1)S(1)} %add_convert_fusion.1), channel_id=1, source_target_pairs={{0,1},{1,2},{2,3},{3,0},{4,5},{5,6},{6,7},{7,4},{8,9},{9,10},{10,1... | collective-permute-start | bytes 3538952 | tf_op jit(solution)/shard_map/ppermute | solution.py:573
  (70 other events, 948.1 us)
Sparse Core Ops, SparseCore 0:
  42.9 70.2 all-gather.1
  243.9 52.8 reduce-scatter.4
  300.6 46.2 reduce-scatter.6
  350.1 61.7 reduce-scatter.10
  426.6 36.9 reduce-scatter.8

commit v6 on v5

--- a/solution.py
+++ b/solution.py
@@ -701,6 +701,12 @@
 
     def product(left, right):
         return dot(left, right, TN).astype(BF)
+
+    def attn_outputs(rows):
+        rows = rows.astype(F32)
+        proj = rows[:, : 4 * width].reshape(cut, 4, width)[:, :, :width_real]
+        gates = rows[:, 4 * width : 4 * width + 3 * heads].reshape(cut, 3, heads)[:, :, :heads_real]
+        return jnp.transpose(proj, (1, 0, 2)), jnp.transpose(gates, (1, 0, 2))
 
     attn_p = gather_1(attn_rows)
     out_rows = [out_own, turn(out_own)]
@@ -815,10 +821,13 @@
     small = jnp.concatenate([gq.reshape(-1), gb])
     small = jnp.pad(small, (0, model - small.shape[0]))[None]
     flat = jnp.concatenate([g0[0:1], gmid, small, jnp.zeros((5, model), F32)], 0)
+    dp_hops = [("dp", 1 << i) for i in range(dp.bit_length() - 1)]
+    tp_hops = [("tp", 1 << i) for i in range(tp.bit_length() - 1)]
+    flat = flat + swap(flat, *dp_hops.pop(0))
     back, attn_mine, attn_other, flat, result, grad_down, out_acc = tie(
         (back, attn_mine, attn_other, flat, result, grad_down, out_acc)
     )
-    hops = [("dp", 1 << i) for i in range(dp.bit_length() - 1)] + [("tp", 1 << i) for i in range(tp.bit_length() - 1)]
+    finals = None
     for s in range(2, tp):
         send = add(back, token_part(gt, s))
         out_send = None
@@ -829,31 +838,31 @@
         if out_send is not None:
             out_acc = turn(out_send)
         attn_sum = add(attn_mine, swap(attn_other, "dp", 1)) if s == 2 else None
-        for _ in range(2):
-            if hops:
-                flat = flat + swap(flat, *hops.pop(0))
-        back, flat, out_acc, attn_sum = tie((back, flat, out_acc, attn_sum))
+        if dp_hops:
+            flat = flat + swap(flat, *dp_hops.pop(0))
+        if s == tp - 1 and s > 2:
+            attn_rows, out_rows, _ = tie((sums[-1], out_acc, flat))
+            finals = attn_outputs(attn_rows), jnp.transpose(total_of((ring[0], out_rows))[:, :width_real])
+        if tp_hops:
+            flat = flat + swap(flat, *tp_hops.pop(0))
+        back, flat, out_acc, attn_sum, finals = tie((back, flat, out_acc, attn_sum, finals))
         if attn_sum is not None:
             sums.append(side_scatter(attn_sum))
-    while out_step < tp:
-        out_acc, out_step = turn(add(out_acc, ring[out_step])), out_step + 1
-    for axis, bit in hops:
+    for axis, bit in dp_hops + tp_hops:
         flat = flat + swap(flat, axis, bit)
     grad_tokens = total_of((token_part(gt, 0), back))
-    grad_gu, grad_attn = [value.astype(F32) for value in sums[2:]]
-    grad_out_own = total_of((ring[0], out_acc))
+    grad_gu = sums[2].astype(F32)
+    (grad_attn_in, grad_gates), grad_out_own = finals
     norm_grad = flat[0:2]
     qk_grad = flat[2, : 2 * 64].reshape(2, 64)
     bias_grad = flat[2, 2 * 64 : 2 * 64 + forget_bias.shape[0]]
 
-    grad_attn_in = jnp.transpose(grad_attn[:, : 4 * width].reshape(cut, 4, width)[:, :, :width_real], (1, 0, 2))
-    grad_gates = grad_attn[:, 4 * width : 4 * width + 3 * heads].reshape(cut, 3, heads)[:, :, :heads_real]
     return (
         result[None],
         grad_tokens[None],
         grad_attn_in,
-        jnp.transpose(grad_gates, (1, 0, 2)),
-        jnp.transpose(grad_out_own[:, :width_real]),
+        grad_gates,
+        grad_out_own,
         jnp.stack([grad_gu[:, :hidden], grad_gu[:, hidden:]]),
         grad_down,
         norm_grad,

time: 485 us -> 501 us (1.033)
  local copies, waits for them, and re-layouts: 31.8 us -> 37.9 us
    ppermute x24, waiting for transfers between devices: 43.1 us -> 65.3 us  [swap(): return lax.ppermute(value, axis, [(i, i ^ bit) for i in range(size)])]
    ppermute x30, waiting for transfers between devices: 85.6 us -> 66.9 us  [turn(): return lax.ppermute(value, 'tp', [(i, (i + 1) % size) for i in range(size)])]
  transfers between devices with their start and end apart: 59 -> 59, of which waited for: 26 -> 25; matrix products, arithmetic and copies ran while one was open for 21% -> 21% of each run, Pallas kernels for 36% -> 35%
where the time goes in v6:
time: 501 us; the launch traced here: 492 us
  Pallas kernels  174 us (35%)
  waiting for transfers between devices  134 us (27%)
  starting transfers between devices  49.2 us (10%)
  matrix products  49.1 us (10%)
  local copies, waits for them, and re-layouts  37.9 us (8%)
  other arithmetic  32.4 us (6%)
  between operations  15.4 us (3%)
    pallas_call x3, Pallas kernels, feed(): pl.pallas_call(functools.partial(ffn_kernel, count, chunk, block, step_ro...  67.4 us
    ppermute x30, waiting for transfers between devices, turn(): return lax.ppermute(value, 'tp', [(i, (i + 1) % size) for i in range(size)])  66.9 us
    ppermute x24, waiting for transfers between devices, swap(): return lax.ppermute(value, axis, [(i, i ^ bit) for i in range(size)])  65.3 us
    dot_general x4, matrix products, dot(): return lax.dot_general(a, b, dims, preferred_element_type=F32)  49.1 us
    pallas_call x2, Pallas kernels, attend_back(): pl.pallas_call(functools.partial(bwd_kernel, begin, heads, block), grid=(...  36 us
    ppermute x30, starting transfers between devices, turn(): return lax.ppermute(value, 'tp', [(i, (i + 1) % size) for i in range(size)])  31.5 us
    pallas_call x1, Pallas kernels, post(): pl.pallas_call(functools.partial(post_kernel, heads, groups), grid=(count...  27.6 us
    pallas_call x1, Pallas kernels, pre(): pl.pallas_call(functools.partial(pre_kernel, heads, spots), grid=(seq //...  22.1 us
  transfers between devices with their start and end apart: 59, of which 25 were waited for; matrix products, arithmetic and copies ran while one was open for 21% of the time, Pallas kernels for 35%

profile of v6, /device:TPU:0, one launch (start us, length us, event | category | flops | bytes accessed | tf_op | source)
XLA Modules:
  0.0 491.7 jit_solution(10867853200925886372)
XLA Ops:
  16.3 6.0 %collective-permute-done.3 = bf16[192,384]{1,0:T(8,128)(2,1)} collective-permute-done((bf16[192,384]{1,0:T(8,128)(2,1)S(1)}, bf16[192,384]{1,0:T(8,128)(2,1)}, u32[]{:S(2)}, u32[]{:S(2)}) %collective-permute-start.3) | collective-permute-done | bytes 147488 | tf_op jit(solution)/shard_map/ppermute | solution.py:573
  23.4 6.0 %collective-permute-done.4 = bf16[192,384]{1,0:T(8,128)(2,1)S(1)} collective-permute-done((bf16[192,384]{1,0:T(8,128)(2,1)}, bf16[192,384]{1,0:T(8,128)(2,1)S(1)}, u32[]{:S(2)}, u32[]{:S(2)}) %collective-permute-start.4) | collective-permute-done | bytes 147488 | tf_op jit(solution)/shard_map/ppermute | solution.py:573
  33.9 5.5 %collective-permute-done.9 = bf16[192,384]{1,0:T(8,128)(2,1)S(1)} collective-permute-done((bf16[192,384]{1,0:T(8,128)(2,1)S(1)}, bf16[192,384]{1,0:T(8,128)(2,1)S(1)}, u32[]{:S(2)}, u32[]{:S(2)}) %collective-permute-start.9) | collective-permute-done | bytes 147488 | tf_op jit(solution)/shard_map/ppermute | solution.py:573
  48.6 22.1 %pre.1 = (bf16[1536,1536]{1,0:T(8,128)(2,1)}, bf16[1536,1664]{1,0:T(8,128)(2,1)}, f32[8,1536]{1,0:T(8,128)}, bf16[1536,384]{1,0:T(8,128)(2,1)}, bf16[1536,384]{1...) custom-call(s32[1]{0:T(128)} %bitcast.me_ref, ...), custom_call_target="tpu_custom_call" | custom-call | flops 1 | bytes 1 | tf_op jit(solution)/shard_map/pre/pallas_call | solution.py:164
  70.7 5.4 %attend.3 = (bf16[512,384]{1,0:T(8,128)(2,1)}, f32[1536,384]{1,0:T(8,128)}, f32[1536,384]{1,0:T(8,128)}) custom-call(bf16[1536,384]{1,0:T(8,128)(2,1)} %get-tuple-element.592.q_ref, bf16[1536,128]{1,0:T(8,128)(2,1)} %get-tuple-element.381.aq_ref, bf16[1536,384]{1,0:T(8,128)(2,1)} %get-tuple-element.382.k_ref, bf16[1536,128]{1,0:T(8,128)(2,1)} %get-tuple-element.383.ak_ref, ...), custom_call_target="tpu_custom_call" | custom-call | flops 1 | bytes 1 | tf_op jit(solution)/shard_map/attend/pallas_call | solution.py:225
  79.9 6.3 %attend.4 = (bf16[512,384]{1,0:T(8,128)(2,1)}, f32[1536,384]{1,0:T(8,128)}, f32[1536,384]{1,0:T(8,128)}) custom-call(bf16[1536,384]{1,0:T(8,128)(2,1)} %get-tuple-element.592.q_ref, bf16[1536,128]{1,0:T(8,128)(2,1)} %get-tuple-element.381.aq_ref, bf16[1536,384]{1,0:T(8,128)(2,1)} %get-tuple-element.382.k_ref, ...), custom_call_target="tpu_custom_call", output_to_operand_aliasing={{1}: (6, {}), {2}: (7, {})} | custom-call | flops 1 | bytes 1 | tf_op jit(solution)/shard_map/attend/pallas_call | solution.py:225
  95.7 8.9 %attend.5 = (bf16[512,384]{1,0:T(8,128)(2,1)}, f32[1536,384]{1,0:T(8,128)}, f32[1536,384]{1,0:T(8,128)}) custom-call(bf16[1536,384]{1,0:T(8,128)(2,1)} %get-tuple-element.592.q_ref, bf16[1536,128]{1,0:T(8,128)(2,1)} %get-tuple-element.381.aq_ref, bf16[1536,384]{1,0:T(8,128)(2,1)} %get-tuple-element.382.k_ref, ...), custom_call_target="tpu_custom_call", output_to_operand_aliasing={{1}: (6, {}), {2}: (7, {})} | custom-call | flops 1 | bytes 1 | tf_op jit(solution)/shard_map/attend/pallas_call | solution.py:225
  104.6 5.4 %collective-permute-done.21 = bf16[96,1536]{1,0:T(8,128)(2,1)} collective-permute-done((bf16[96,1536]{1,0:T(8,128)(2,1)}, bf16[96,1536]{1,0:T(8,128)(2,1)}, u32[]{:S(2)}, u32[]{:S(2)}) %collective-permute-start.21) | collective-permute-done | bytes 294944 | tf_op jit(solution)/shard_map/ppermute | solution.py:568
  126.4 7.0 %collective-permute-done.23.refs_2_ = bf16[512,384]{1,0:T(8,128)(2,1)} collective-permute-done((bf16[512,384]{1,0:T(8,128)(2,1)S(1)}, bf16[512,384]{1,0:T(8,128)(2,1)}, u32[]{:S(2)}, u32[]{:S(2)}) %collective-permute-start.23) | collective-permute-done | bytes 393248 | tf_op jit(solution)/shard_map/ppermute | solution.py:573
  133.4 7.5 %collective-permute-done.24.refs_1_ = bf16[512,384]{1,0:T(8,128)(2,1)} collective-permute-done((bf16[512,384]{1,0:T(8,128)(2,1)}, bf16[512,384]{1,0:T(8,128)(2,1)}, u32[]{:S(2)}, u32[]{:S(2)}) %collective-permute-start.24) | collective-permute-done | bytes 393248 | tf_op jit(solution)/shard_map/ppermute | solution.py:573
  142.5 22.0 %feed.3 = (bf16[1536,1536]{1,0:T(8,128)(2,1)}, bf16[1536,1024]{1,0:T(8,128)(2,1)}, bf16[1536,2048]{1,0:T(8,128)(2,1)}, bf16[1536,1536]{1,0:T(8,128)(2,1)}, bf16[...) custom-call(s32[1]{0:T(128)} %bitcast.12.at_ref, ...), custom_call_target="tpu_custom_call" | custom-call | flops 1 | bytes 1 | tf_op jit(solution)/shard_map/feed/pallas_call | solution.py:344
  168.4 22.8 %feed.4 = (bf16[1536,1536]{1,0:T(8,128)(2,1)}, bf16[1536,1024]{1,0:T(8,128)(2,1)}, bf16[1536,2048]{1,0:T(8,128)(2,1)}, bf16[1536,1536]{1,0:T(8,128)(2,1)}, bf16[...) custom-call(s32[1]{0:T(128)} %bitcast.12.at_ref, ...), custom_call_target="tpu_custom_call", output_to_operand_aliasing={{0}: (10, {}), {1}: (11, {}), {2}: (12, {}), {3}: (13, {}),... | custom-call | flops 1 | bytes 1 | tf_op jit(solution)/shard_map/feed/pallas_call | solution.py:344
  192.6 22.6 %feed.5 = (bf16[1536,1536]{1,0:T(8,128)(2,1)}, bf16[1536,1024]{1,0:T(8,128)(2,1)}, bf16[1536,2048]{1,0:T(8,128)(2,1)}, bf16[1536,1536]{1,0:T(8,128)(2,1)}, bf16[...) custom-call(s32[1]{0:T(128)} %bitcast.12.at_ref, ...), custom_call_target="tpu_custom_call", output_to_operand_aliasing={{0}: (10, {}), {1}: (11, {}), {2}: (12, {}), {3}: (13, {}),... | custom-call | flops 1 | bytes 1 | tf_op jit(solution)/shard_map/feed/pallas_call | solution.py:344
  220.1 12.4 %convolution_convert_fusion.2 = bf16[1536,1536]{1,0:T(8,128)(2,1)} fusion(bf16[1536,1536]{1,0:T(8,128)(2,1)} %get-tuple-element.631.res_ref, bf16[1536,1536]{1,0:T(8,128)(2,1)} %get-tuple-element.544), kind=kOutput, calls=%fused_computation.2 | convolution fusion | flops 7250116608 | bytes 14155776 | tf_op jit(solution)/shard_map/dot_general | solution.py:24
  232.5 8.9 %fusion = bf16[1536,1024]{1,0:T(8,128)(2,1)} fusion(bf16[1536,1024]{1,0:T(8,128)(2,1)S(1)} %copy-done, bf16[1,1536,1536]{2,1,0:T(8,128)(2,1)} %param.36), kind=kOutput, calls=%fused_computation.5 | convolution fusion | flops 4833411072 | bytes 11010048 | tf_op jit(solution)/shard_map/dot_general | solution.py:24
  248.1 15.7 %convolution_convert_fusion.1 = bf16[1536,2048]{1,0:T(8,128)(2,1)} fusion(bf16[1536,1536]{1,0:T(8,128)(2,1)} %get-tuple-element.567, bf16[1536,2048]{1,0:T(8,128)(2,1)} %get-tuple-element.568), kind=kOutput, calls=%fused_computation.1 | convolution fusion | flops 9666822144 | bytes 17301504 | tf_op jit(solution)/shard_map/dot_general | solution.py:24
  270.9 9.7 %collective-permute-done.39 = bf16[512,384]{1,0:T(8,128)(2,1)S(1)} collective-permute-done((bf16[512,384]{1,0:T(8,128)(2,1)S(1)}, bf16[512,384]{1,0:T(8,128)(2,1)S(1)}, u32[]{:S(2)}, u32[]{:S(2)}) %collective-permute-start.39) | collective-permute-done | bytes 393248 | tf_op jit(solution)/shard_map/ppermute | solution.py:573
  283.1 12.8 %attend_back.2 = (f32[1536,128]{1,0:T(8,128)}, f32[1536,128]{1,0:T(8,128)}, f32[1536,128]{1,0:T(8,128)}, f32[1536,128]{1,0:T(8,128)}) custom-call(bf16[1536,384]{1,0:T(8,128)(2,1)} %get-tuple-element.592.q_ref, bf16[1536,128]{1,0:T(8,128)(2,1)} %get-tuple-element.381.aq_ref, bf16[1536,384]{1,0:T(8,128)(2,1)} %get-tuple-element.382.k_ref, ...), custom_call_target="tpu_custom_call" | custom-call | flops 1 | bytes 1 | tf_op jit(solution)/shard_map/attend_back/pallas_call | solution.py:437
  303.9 23.2 %attend_back.3 = (f32[1536,256]{1,0:T(8,128)}, f32[1536,256]{1,0:T(8,128)}, f32[1536,256]{1,0:T(8,128)}, f32[1536,128]{1,0:T(8,128)}) custom-call(bf16[1536,384]{1,0:T(8,128)(2,1)} %get-tuple-element.592.q_ref, bf16[1536,128]{1,0:T(8,128)(2,1)} %get-tuple-element.381.aq_ref, bf16[1536,384]{1,0:T(8,128)(2,1)} %get-tuple-element.382.k_ref, ...), custom_call_target="tpu_custom_call" | custom-call | flops 1 | bytes 1 | tf_op jit(solution)/shard_map/attend_back/pallas_call | solution.py:437
  331.7 27.6 %post.1 = (bf16[1536,1664]{1,0:T(8,128)(2,1)}, bf16[1536,1536]{1,0:T(8,128)(2,1)}, f32[8,1536]{1,0:T(8,128)}, f32[8,384]{1,0:T(8,128)}, f32[8,128]{1,0:T(8,128)}) custom-call(bf16[1536,384]{1,0:T(8,128)(2,1)} %get-tuple-element.624.q_ref, bf16[1536,384]{1,0:T(8,128)(2,1)} %get-tuple-element.625.ks_ref, bf16[1536,384]{1,0:T(8,128)(2,1)} %get-tuple-element.626.kd_ref, ...), custom_call_target="tpu_custom_call" | custom-call | flops 1 | bytes 1 | tf_op jit(solution)/shard_map/post/pallas_call | solution.py:547
  367.4 12.2 %convolution_convert_fusion = bf16[1536,1664]{1,0:T(8,128)(2,1)S(1)} fusion(bf16[1536,1536]{1,0:T(8,128)(2,1)} %get-tuple-element.652, bf16[1536,1664]{1,0:T(8,128)(2,1)} %get-tuple-element.653), kind=kOutput, calls=%fused_computation | convolution fusion | flops 7854292992 | bytes 14942208 | tf_op jit(solution)/shard_map/dot_general | solution.py:24
  383.7 13.3 %collective-permute-done.45 = bf16[192,384]{1,0:T(8,128)(2,1)S(1)} collective-permute-done((bf16[192,384]{1,0:T(8,128)(2,1)S(1)}, bf16[192,384]{1,0:T(8,128)(2,1)S(1)}, u32[]{:S(2)}, u32[]{:S(2)}) %collective-permute-start.45) | collective-permute-done | bytes 147488 | tf_op jit(solution)/shard_map/ppermute | solution.py:573
  406.1 24.2 %collective-permute-done.48 = f32[8,1536]{1,0:T(8,128)S(1)} collective-permute-done((f32[8,1536]{1,0:T(8,128)S(1)}, f32[8,1536]{1,0:T(8,128)S(1)}, u32[]{:S(2)}, u32[]{:S(2)}) %collective-permute-start.48) | collective-permute-done | bytes 49184 | tf_op jit(solution)/shard_map/ppermute | solution.py:568
  444.6 23.7 %collective-permute-done.53 = f32[8,1536]{1,0:T(8,128)S(1)} collective-permute-done((f32[8,1536]{1,0:T(8,128)S(1)}, f32[8,1536]{1,0:T(8,128)S(1)}, u32[]{:S(2)}, u32[]{:S(2)}) %collective-permute-start.53) | collective-permute-done | bytes 49184 | tf_op jit(solution)/shard_map/ppermute | solution.py:568
  (272 shorter events, 145.3 us)
Async XLA Ops:
  7.2 135.3 %all-gather.2.cloned.1.call-start = ((), (), s32[]{:S(2)}) async-start(), calls=%async_computation.4 | async-start | bytes 10616832 | tf_op jit(solution)/shard_map/all_gather | solution.py:721
  42.8 258.8 %reduce-scatter.5.cloned.1.call-start = ((), (), s32[]{:S(2)}) async-start(), calls=%async_computation.5 | async-start | bytes 5308416 | tf_op jit(solution)/shard_map/reduce_scatter | solution.py:648
  42.9 27.8 %collective-permute-start.12 = (bf16[192,1536]{1,0:T(8,128)(2,1)S(1)}, bf16[192,1536]{1,0:T(8,128)(2,1)}, u32[]{:S(2)}, u32[]{:S(2)}) collective-permute-start(bf16[192,1536]{1,0:T(8,128)(2,1)S(1)} %pad_maximum_fusion.3), channel_id=1, source_target_pairs={{0,4},{4,0},{8,12},{12,8},{16,20},{20,16},{24,28},{28,24},{1,5},{5... | collective-permute-start | bytes 1769480 | tf_op jit(solution)/shard_map/ppermute | solution.py:568
  42.9 27.8 %collective-permute-start.13 = (bf16[192,1536]{1,0:T(8,128)(2,1)S(1)}, bf16[192,1536]{1,0:T(8,128)(2,1)S(1)}, u32[]{:S(2)}, u32[]{:S(2)}) collective-permute-start(bf16[192,1536]{1,0:T(8,128)(2,1)S(1)} %pad_maximum_fusion.3), channel_id=1, source_target_pairs={{0,8},{4,12},{8,0},{12,4},{16,24},{20,28},{24,16},{28,20},{1,9},{5... | collective-permute-start | bytes 1769480 | tf_op jit(solution)/shard_map/ppermute | solution.py:568
  43.5 27.2 %collective-permute-start.14 = (bf16[192,1536]{1,0:T(8,128)(2,1)S(1)}, bf16[192,1536]{1,0:T(8,128)(2,1)S(1)}, u32[]{:S(2)}, u32[]{:S(2)}) collective-permute-start(bf16[192,1536]{1,0:T(8,128)(2,1)S(1)} %pad_maximum_fusion.3), channel_id=1, source_target_pairs={{0,16},{4,20},{8,24},{12,28},{16,0},{20,4},{24,8},{28,12},{1,17},{... | collective-permute-start | bytes 1769480 | tf_op jit(solution)/shard_map/ppermute | solution.py:568
  79.4 30.6 %collective-permute-start.18 = (bf16[192,1536]{1,0:T(8,128)(2,1)S(1)}, bf16[192,1536]{1,0:T(8,128)(2,1)S(1)}, u32[]{:S(2)}, u32[]{:S(2)}) collective-permute-start(bf16[192,1536]{1,0:T(8,128)(2,1)S(1)} %collective-permute-done.13), channel_id=1, source_target_pairs={{0,4},{4,0},{8,12},{12,8},{16,20},{20,16},{24,28},{28,24},{1,5},{5... | collective-permute-start | bytes 1769480 | tf_op jit(solution)/shard_map/ppermute | solution.py:568
  79.4 30.6 %collective-permute-start.19 = (bf16[192,1536]{1,0:T(8,128)(2,1)S(1)}, bf16[192,1536]{1,0:T(8,128)(2,1)S(1)}, u32[]{:S(2)}, u32[]{:S(2)}) collective-permute-start(bf16[192,1536]{1,0:T(8,128)(2,1)S(1)} %collective-permute-done.14), channel_id=1, source_target_pairs={{0,4},{4,0},{8,12},{12,8},{16,20},{20,16},{24,28},{28,24},{1,5},{5... | collective-permute-start | bytes 1769480 | tf_op jit(solution)/shard_map/ppermute | solution.py:568
  113.8 27.2 %collective-permute-start.24 = (bf16[512,384]{1,0:T(8,128)(2,1)}, bf16[512,384]{1,0:T(8,128)(2,1)}, u32[]{:S(2)}, u32[]{:S(2)}) collective-permute-start(bf16[512,384]{1,0:T(8,128)(2,1)} %get-tuple-element.413.refs_0_), channel_id=1, source_target_pairs={{0,1},{1,2},{2,3},{3,0},{4,5},{5,6},{6,7},{7,4},{8,9},{9,10},{10,1... | collective-permute-start | bytes 1179656 | tf_op jit(solution)/shard_map/ppermute | solution.py:573
  164.5 26.7 %collective-permute-start.30 = (bf16[512,384]{1,0:T(8,128)(2,1)}, bf16[512,384]{1,0:T(8,128)(2,1)S(1)}, u32[]{:S(2)}, u32[]{:S(2)}) collective-permute-start(bf16[512,384]{1,0:T(8,128)(2,1)} %get-tuple-element.458), channel_id=1, source_target_pairs={{0,1},{1,2},{2,3},{3,0},{4,5},{5,6},{6,7},{7,4},{8,9},{9,10},{10,1... | collective-permute-start | bytes 1179656 | tf_op jit(solution)/shard_map/ppermute | solution.py:573
  164.9 26.4 %collective-permute-start.29 = (bf16[512,384]{1,0:T(8,128)(2,1)S(1)}, bf16[512,384]{1,0:T(8,128)(2,1)S(1)}, u32[]{:S(2)}, u32[]{:S(2)}) collective-permute-start(bf16[512,384]{1,0:T(8,128)(2,1)S(1)} %collective-permute-done.28.refs_2_), channel_id=1, source_target_pairs={{0,1},{1,2},{2,3},{3,0},{4,5},{5,6},{6,7},{7,4},{8,9},{9,10},{10,1... | collective-permute-start | bytes 1179656 | tf_op jit(solution)/shard_map/ppermute | solution.py:573
  243.9 118.9 %reduce-scatter.7.cloned.1.call-start = ((), (), s32[]{:S(2)}) async-start(), calls=%async_computation.6 | async-start | bytes 3538944 | tf_op jit(solution)/shard_map/reduce_scatter | solution.py:648
  263.9 172.5 %reduce-scatter.11.cloned.1.call-start = ((), (), s32[]{:S(2)}) async-start(), calls=%async_computation.8 | async-start | bytes 7077888 | tf_op jit(solution)/shard_map/reduce_scatter | solution.py:648
  268.2 31.8 %collective-permute-start.38 = (bf16[384,1536]{1,0:T(8,128)(2,1)S(1)}, bf16[384,1536]{1,0:T(8,128)(2,1)S(1)}, u32[]{:S(2)}, u32[]{:S(2)}) collective-permute-start(bf16[384,1536]{1,0:T(8,128)(2,1)S(1)} %constant_dynamic-slice_fusion.3), channel_id=1, source_target_pairs={{0,1},{1,2},{2,3},{3,0},{4,5},{5,6},{6,7},{7,4},{8,9},{9,10},{10,1... | collective-permute-start | bytes 3538952 | tf_op jit(solution)/shard_map/ppermute | solution.py:573
  330.1 31.0 %collective-permute-start.41 = (bf16[384,1536]{1,0:T(8,128)(2,1)S(1)}, bf16[384,1536]{1,0:T(8,128)(2,1)S(1)}, u32[]{:S(2)}, u32[]{:S(2)}) collective-permute-start(bf16[384,1536]{1,0:T(8,128)(2,1)S(1)} %add_convert_fusion.4), channel_id=1, source_target_pairs={{0,1},{1,2},{2,3},{3,0},{4,5},{5,6},{6,7},{7,4},{8,9},{9,10},{10,1... | collective-permute-start | bytes 3538952 | tf_op jit(solution)/shard_map/ppermute | solution.py:573
  330.2 140.3 %reduce-scatter.9.cloned.1.call-start = ((), (), s32[]{:S(2)}) async-start(), calls=%async_computation.7 | async-start | bytes 3194880 | tf_op jit(solution)/shard_map/reduce_scatter | solution.py:640
  330.3 30.8 %collective-permute-start.42 = (bf16[192,384]{1,0:T(8,128)(2,1)S(1)}, bf16[192,384]{1,0:T(8,128)(2,1)S(1)}, u32[]{:S(2)}, u32[]{:S(2)}) collective-permute-start(bf16[192,384]{1,0:T(8,128)(2,1)S(1)} %get-tuple-element.644), channel_id=1, source_target_pairs={{0,1},{1,2},{2,3},{3,0},{4,5},{5,6},{6,7},{7,4},{8,9},{9,10},{10,1... | collective-permute-start | bytes 442376 | tf_op jit(solution)/shard_map/ppermute | solution.py:573
  363.6 33.3 %collective-permute-start.43 = (bf16[384,1536]{1,0:T(8,128)(2,1)S(1)}, bf16[384,1536]{1,0:T(8,128)(2,1)S(1)}, u32[]{:S(2)}, u32[]{:S(2)}) collective-permute-start(bf16[384,1536]{1,0:T(8,128)(2,1)S(1)} %constant_dynamic-slice_fusion.2), channel_id=1, source_target_pairs={{0,1},{1,2},{2,3},{3,0},{4,5},{5,6},{6,7},{7,4},{8,9},{9,10},{10,1... | collective-permute-start | bytes 3538952 | tf_op jit(solution)/shard_map/ppermute | solution.py:573
  365.9 31.0 %collective-permute-start.45 = (bf16[192,384]{1,0:T(8,128)(2,1)S(1)}, bf16[192,384]{1,0:T(8,128)(2,1)S(1)}, u32[]{:S(2)}, u32[]{:S(2)}) collective-permute-start(bf16[192,384]{1,0:T(8,128)(2,1)S(1)} %add_convert_fusion.16), channel_id=1, source_target_pairs={{0,1},{1,2},{2,3},{3,0},{4,5},{5,6},{6,7},{7,4},{8,9},{9,10},{10,1... | collective-permute-start | bytes 442376 | tf_op jit(solution)/shard_map/ppermute | solution.py:573
  398.6 32.4 %collective-permute-start.50 = (bf16[768,1664]{1,0:T(8,128)(2,1)S(1)}, bf16[768,1664]{1,0:T(8,128)(2,1)S(1)}, u32[]{:S(2)}, u32[]{:S(2)}) collective-permute-start(bf16[768,1664]{1,0:T(8,128)(2,1)S(1)} %bitcast.72), channel_id=1, source_target_pairs={{0,4},{4,0},{8,12},{12,8},{16,20},{20,16},{24,28},{28,24},{1,5},{5... | collective-permute-start | bytes 7667720 | tf_op jit(solution)/shard_map/ppermute | solution.py:568
  398.7 34.5 %collective-permute-start.46 = (bf16[384,1536]{1,0:T(8,128)(2,1)S(1)}, bf16[384,1536]{1,0:T(8,128)(2,1)S(1)}, u32[]{:S(2)}, u32[]{:S(2)}) collective-permute-start(bf16[384,1536]{1,0:T(8,128)(2,1)S(1)} %add_convert_fusion.2), channel_id=1, source_target_pairs={{0,1},{1,2},{2,3},{3,0},{4,5},{5,6},{6,7},{7,4},{8,9},{9,10},{10,1... | collective-permute-start | bytes 3538952 | tf_op jit(solution)/shard_map/ppermute | solution.py:573
  404.1 26.3 %collective-permute-start.48 = (f32[8,1536]{1,0:T(8,128)S(1)}, f32[8,1536]{1,0:T(8,128)S(1)}, u32[]{:S(2)}, u32[]{:S(2)}) collective-permute-start(f32[8,1536]{1,0:T(8,128)S(1)} %add.253), channel_id=1, source_target_pairs={{0,1},{1,0},{2,3},{3,2},{4,5},{5,4},{6,7},{7,6},{8,9},{9,8},{10,11... | collective-permute-start | bytes 147464 | tf_op jit(solution)/shard_map/ppermute | solution.py:568
  405.6 27.5 %collective-permute-start.49 = (bf16[192,384]{1,0:T(8,128)(2,1)S(1)}, bf16[192,384]{1,0:T(8,128)(2,1)S(1)}, u32[]{:S(2)}, u32[]{:S(2)}) collective-permute-start(bf16[192,384]{1,0:T(8,128)(2,1)S(1)} %add_convert_fusion.15), channel_id=1, source_target_pairs={{0,1},{1,2},{2,3},{3,0},{4,5},{5,6},{6,7},{7,4},{8,9},{9,10},{10,1... | collective-permute-start | bytes 442376 | tf_op jit(solution)/shard_map/ppermute | solution.py:573
  436.4 40.6 %collective-permute-start.51 = (bf16[384,1536]{1,0:T(8,128)(2,1)}, bf16[384,1536]{1,0:T(8,128)(2,1)S(1)}, u32[]{:S(2)}, u32[]{:S(2)}) collective-permute-start(bf16[384,1536]{1,0:T(8,128)(2,1)} %add_convert_fusion.1), channel_id=1, source_target_pairs={{0,1},{1,2},{2,3},{3,0},{4,5},{5,6},{6,7},{7,4},{8,9},{9,10},{10,1... | collective-permute-start | bytes 3538952 | tf_op jit(solution)/shard_map/ppermute | solution.py:573
  443.1 25.2 %collective-permute-start.53 = (f32[8,1536]{1,0:T(8,128)S(1)}, f32[8,1536]{1,0:T(8,128)S(1)}, u32[]{:S(2)}, u32[]{:S(2)}) collective-permute-start(f32[8,1536]{1,0:T(8,128)S(1)} %add.257), channel_id=1, source_target_pairs={{0,2},{1,3},{2,0},{3,1},{4,6},{5,7},{6,4},{7,5},{8,10},{9,11},{10,... | collective-permute-start | bytes 147464 | tf_op jit(solution)/shard_map/ppermute | solution.py:568
  (72 other events, 994.0 us)
Sparse Core Ops, SparseCore 0:
  42.9 70.2 all-gather.1
  244.0 52.8 reduce-scatter.4
  300.6 46.2 reduce-scatter.6
  350.2 62.4 reduce-scatter.10
  433.3 37.2 reduce-scatter.8
